TPU v7x, 256 devices: a whole 4x4x8 slice. The times are simulated.
256 devices in a mesh: section: 16 (over z_hi, y), seq: 16 (over x, z_lo, core).
Axes of the slice: x: 4, y: 4, z: 8 (z_hi: 4, z_lo: 2; z = z_hi * 2 + z_lo), core: 2. Of those that a mesh axis runs over, the one named last changes fastest.
Arguments:
- queries: bfloat16 [16, 1024, 2048], P('section', 'seq'), may hold values from -6 to 6
- out_grad: bfloat16 [16, 1024, 2048], P('section', 'seq'), may hold values from -96 to 96
- keys: bfloat16 [16, 2048, 2048], P('section', 'seq'), may hold values from -6 to 6
- values: bfloat16 [16, 2048, 2048], P('section', 'seq'), may hold values from -6 to 6
- key_weight: bfloat16 [16, 4096, 2048], P('section', 'seq'), may hold values from -0.125 to 0.125
- value_weight: bfloat16 [16, 4096, 2048], P('section', 'seq'), may hold values from -0.125 to 0.125
- owner: int32 [1], replicated, may hold values from 0 to 15
Outputs:
- enc_grad: bfloat16 [16, 2048, 4096], P('section', None, 'seq')
All inputs are finite; a program needn't handle non-finite values.
Results may differ from a plain program's by a relative error of at most 0.012.
Values may be sent and summed in bfloat16 or wider, within the bound.
No kernel may reach another device: no remote copies, remote signals or barrier semaphores. Data moves between devices by JAX's collectives and lax.ppermute only.
A program may use at most 128 MiB of HBM per device.

v0:
```python
import jax
import jax.numpy as jnp
from jax import lax
from jax.sharding import PartitionSpec as P

HEADS = 8
HEAD = 256


def local(queries, out_grad, keys, values, key_weight, value_weight, owner):
    head_count = HEADS
    head_width = HEAD
    score_scale = HEAD ** (-0.5)
    group_size = min(head_count, 8)
    group_count = head_count // group_size
    block_cols = group_size * head_width
    query_rows = queries[0]
    grad_rows = out_grad[0]
    key_rows = keys[0]
    value_rows = values[0]
    all_queries, all_grads = (
        lax.all_gather(query_rows, "seq", axis=0, tiled=True),
        lax.all_gather(grad_rows, "seq", axis=0, tiled=True),
    )
    local_keys = key_rows.shape[0]

    def columns(matrix):
        return matrix.reshape(matrix.shape[0], group_size, head_width)

    def scores_of():
        query_cols = columns(all_queries)
        grad_cols = columns(all_grads)
        key_cols = columns(key_rows)
        value_cols = columns(value_rows)
        scores = (
            jnp.einsum("qhd,khd->hqk", query_cols, key_cols, preferred_element_type=jnp.float32)
            * score_scale
        )
        grad_probs = jnp.einsum(
            "qhd,khd->hqk", grad_cols, value_cols, preferred_element_type=jnp.float32
        )
        return (query_cols, grad_cols, scores, grad_probs)

    def first_pass(block_index):
        query_cols, grad_cols, scores, grad_probs = scores_of()
        row_peak = jnp.max(scores, axis=2)
        shifted = jnp.exp(scores - row_peak[:, :, None])
        return (row_peak, jnp.sum(shifted, axis=2), jnp.sum(shifted * grad_probs, axis=2))

    block_ids = jnp.arange(group_count, dtype=jnp.int32)
    row_peak, row_total, row_weighted = lax.map(first_pass, block_ids)
    global_peak = lax.pmax(row_peak.astype(jnp.bfloat16), "seq").astype(row_peak.dtype)
    factor = jnp.exp(row_peak - global_peak)
    row_total, row_weighted = lax.psum((row_total * factor, row_weighted * factor), "seq")
    row_peak = global_peak
    lse = row_peak + jnp.log(row_total)
    row_delta = row_weighted / row_total

    def second_pass(block_index):
        query_cols, grad_cols, scores, grad_probs = scores_of()
        probs = jnp.exp(scores - lse[block_index][:, :, None])
        grad_scores = (probs * (grad_probs - row_delta[block_index][:, :, None])).astype(
            jnp.bfloat16
        )
        probs_low = probs.astype(jnp.bfloat16)
        value_grad = jnp.einsum(
            "hqk,qhd->khd", probs_low, grad_cols, preferred_element_type=jnp.float32
        ).astype(jnp.bfloat16)
        key_grad = (
            jnp.einsum("hqk,qhd->khd", grad_scores, query_cols, preferred_element_type=jnp.float32)
            * score_scale
        ).astype(jnp.bfloat16)
        return (
            key_grad.reshape(local_keys, block_cols),
            value_grad.reshape(local_keys, block_cols),
        )

    key_blocks, value_blocks = lax.map(second_pass, block_ids)
    key_grad = key_blocks.transpose(1, 0, 2).reshape(local_keys, head_count * head_width)
    value_grad = value_blocks.transpose(1, 0, 2).reshape(local_keys, head_count * head_width)
    key_value = jnp.concatenate([key_grad, value_grad], axis=1)
    projections = jnp.concatenate([key_weight[0], value_weight[0]], axis=1)
    partial_value = lax.dot_general(
        lax.all_gather(key_value, "seq", axis=0, tiled=True),
        projections,
        (((1,), (1,)), ((), ())),
        preferred_element_type=jnp.float32,
    )
    is_owner = lax.axis_index("section") == owner[0]
    summed = lax.psum(partial_value, "section")
    rounded = summed.astype(jnp.bfloat16)
    return jnp.where(is_owner, rounded, jnp.zeros((), jnp.bfloat16))[None]


def solution(mesh):
    in_specs = (
        P("section", "seq", None),
        P("section", "seq", None),
        P("section", "seq", None),
        P("section", "seq", None),
        P("section", "seq", None),
        P("section", "seq", None),
        P(),
    )
    out_specs = P("section", None, "seq")
    return jax.shard_map(local, mesh=mesh, in_specs=in_specs, out_specs=out_specs, check_vma=False)
```

profile of v0, /device:TPU:6, one launch (start us, length us, event | category | flops | bytes accessed | tf_op | source)
XLA Modules:
  0.0 483.0 jit_solution(11008667202934519078)
XLA Ops:
  6.5 0.7 all-gather.8.cloned.1.call-update
  7.3 0.7 all-gather.10.cloned.1.call-update
  8.1 1.2 copy.34
  9.2 1.2 copy.35
  10.4 41.0 %all-gather.8.cloned.1.call-done = bf16[1,1024,2048]{2,1,0:T(8,128)(2,1)} async-done(((bf16[1,64,2048]{2,1,0:T(8,128)(2,1)}), bf16[1,1024,2048]{2,1,0:T(8,128)(2,1)}) %all-gather.8.cloned.1.call-update) | async-done | bytes 4194320 | tf_op jit(solution)/shard_map/all_gather | solution.py:22
  51.4 6.4 %copy.20 = bf16[1,1024,2048]{1,2,0:T(8,128)(2,1)} copy(bf16[1,1024,2048]{2,1,0:T(8,128)(2,1)} %all-gather.8.cloned.1.call-done) | data formatting | bytes 8388608 | tf_op jit(solution)/shard_map/all_gather | solution.py:22
  57.8 5.1 %multiply_reduce_fusion.1 = (f32[8,1024]{1,0:T(8,128)S(1)}, f32[8,1024,128]{1,2,0:T(8,128)}) fusion(bf16[1024,8,256]{0,2,1:T(8,128)(2,1)} %bitcast.40, bf16[128,8,256]{2,1,0:T(8,128)(2,1)S(1)} %bitcast.44), kind=kOutput, calls=%fused_computation.6 | convolution fusion | flops 538959872 | bytes 8945664 | tf_op jit(solution)/shard_map/while/body/eval_jaxpr/qhd,khd->hqk/dot_general | solution.py:36
  62.9 47.6 %pmax.7 = bf16[1,8,1024]{2,1,0:T(8,128)(2,1)S(1)} all-reduce(bf16[1,8,1024]{2,1,0:T(8,128)(2,1)S(1)} %bitcast_convert_fusion), channel_id=1, replica_groups=mesh['section'=16,'seq'=16] {'seq'}, use_global_device_ids=true, to_apply=%region_1.2 | all-reduce | flops 8192 | bytes 32768 | tf_op jit(solution)/shard_map/pmax | solution.py:52
  110.5 6.4 %copy.23 = bf16[1,1024,2048]{1,2,0:T(8,128)(2,1)} copy(bf16[1,1024,2048]{2,1,0:T(8,128)(2,1)} %all-gather.10.cloned.1.call-done) | data formatting | bytes 8388608 | tf_op jit(solution)/shard_map/all_gather | solution.py:23
  116.9 6.9 %multiply_reduce_fusion = (f32[8,1024]{1,0:T(8,128)S(1)}, f32[8,1024]{1,0:T(8,128)S(1)}, f32[8,1024,128]{1,2,0:T(8,128)}) fusion(f32[8,1024,128]{1,2,0:T(8,128)} %get-tuple-element.54, f32[8,1024]{1,0:T(8,128)S(1)} %get-tuple-element.53, bf16[1024,8,256]{0,2,1:T(8,128)(2,1)} %bitcast.42, bf16[128,8,256]{2,1,0:T(8,128)(2,1)S(1)} %bitcast.45), kind=kOutput, calls=%fused_computation.1 | convolution fusion | flops 542097408 | bytes 13205504 | tf_op jit(solution)/shard_map/while/body/eval_jaxpr/qhd,khd->hqk/dot_general | solution.py:39
  123.8 0.7 bitcast_multiply_fusion
  124.5 0.0 all-gather.6.cloned.1.call-start
  124.5 110.7 %all-reduce.4.cloned.1.call-done = (f32[1,8,1024]{2,1,0:T(8,128)}, f32[1,8,1024]{2,1,0:T(8,128)}) async-done(((f32[1,8,1024]{2,1,0:T(8,128)}, f32[1,8,1024]{2,1,0:T(8,128)}), (f32[1,8,1024]{2,1,0:T(8,128)}, f32[1,8,1024]{2,1,0:T(8,128)})) %all-reduce.4.cloned.1.call-update) | async-done | bytes 65552 | tf_op jit(solution)/shard_map/psum | solution.py:54
  235.2 0.8 divide_bitcast_fusion
  236.0 5.2 %fusion.20 = bf16[128,8,256]{2,0,1:T(8,128)(2,1)S(1)} fusion(bf16[1024,8,256]{0,2,1:T(8,128)(2,1)} %bitcast.43, f32[8,1024,128]{1,2,0:T(8,128)} %get-tuple-element.54, f32[8,1024]{1,0:T(8,128)S(1)} %get-tuple-element.52), kind=kOutput, calls=%fused_computation.22 | convolution fusion | flops 540278784 | bytes 8945664 | tf_op jit(solution)/shard_map/while/body/eval_jaxpr/hqk,qhd->khd/dot_general | solution.py:66
  241.2 0.7 copy-done.1
  241.9 4.2 fusion.19
  246.1 0.3 copy.27
  246.4 0.3 copy.29
  246.7 1.0 pad_maximum_fusion
  248.4 106.1 %all-gather.6.cloned.1.call-done = bf16[2048,4096]{0,1:T(8,128)(2,1)} async-done(((bf16[128,4096]{0,1:T(8,128)(2,1)}), bf16[2048,4096]{0,1:T(8,128)(2,1)}) %all-gather.6.cloned.1.call-update) | async-done | bytes 16777232 | tf_op jit(solution)/shard_map/all_gather | solution.py:84
  354.5 8.8 %fusion.5 = f32[2048,256]{1,0:T(8,128)S(1)} fusion(bf16[2048,4096]{0,1:T(8,128)(2,1)} %all-gather.6.cloned.1.call-done, bf16[256,2048]{1,0:T(8,128)(2,1)} %bitcast.50, bf16[256,2048]{1,0:T(8,128)(2,1)} %bitcast.51), kind=kOutput, calls=%fused_computation.9 | convolution fusion | flops 4299161600 | bytes 20971520 | tf_op jit(solution)/shard_map/dot_general | solution.py:83
  363.3 112.1 %all-reduce.5 = bf16[2048,256]{1,0:T(8,128)(2,1)S(1)} all-reduce(f32[2048,256]{1,0:T(8,128)S(1)} %fusion.5), channel_id=1, replica_groups=mesh['section'=16,'seq'=16] {'section'}, use_global_device_ids=true, to_apply=%region_6.7 | all-reduce | flops 524288 | bytes 3145728 | tf_op jit(solution)/shard_map/psum | solution.py:90
  475.4 1.0 select_bitcast_fusion
  (10 shorter events, 0.1 us)
Async XLA Ops:
  6.5 44.8 %all-gather.8.cloned.1.call-start = ((), (), s32[]{:S(2)}) async-start(), calls=%async_computation.1 | async-start | bytes 4456448 | tf_op jit(solution)/shard_map/all_gather | solution.py:22
  7.3 103.2 %all-gather.10.cloned.1.call-start = ((), (), s32[]{:S(2)}) async-start(), calls=%async_computation.2 | async-start | bytes 4456448 | tf_op jit(solution)/shard_map/all_gather | solution.py:23
  8.0 227.2 %all-reduce.4.cloned.1.call-start = ((), (), s32[]{:S(2)}) async-start(), calls=%async_computation.3 | async-start | bytes 131072 | tf_op jit(solution)/shard_map/psum | solution.py:54
  124.5 230.0 %all-gather.6.cloned.1.call-start = ((), (), s32[]{:S(2)}) async-start(), calls=%async_computation | async-start | bytes 17825792 | tf_op jit(solution)/shard_map/all_gather | solution.py:84
  236.0 5.2 %copy-start = (f32[8,1024,128]{1,2,0:T(8,128)S(1)}, f32[8,1024,128]{1,2,0:T(8,128)}, u32[]{:S(2)}) copy-start(f32[8,1024,128]{1,2,0:T(8,128)} %get-tuple-element.54) | copy-start | bytes 12582916
  236.0 5.9 %copy-start.1 = (bf16[1,1024,2048]{1,2,0:T(8,128)(2,1)S(1)}, bf16[1,1024,2048]{1,2,0:T(8,128)(2,1)}, u32[]{:S(2)}) copy-start(bf16[1,1024,2048]{1,2,0:T(8,128)(2,1)} %copy.20) | copy-start | bytes 12582916
Sparse Core Ops, SparseCore 0:
  9.2 42.1 all-gather.7
  53.2 39.8 all-gather.9
  124.6 110.5 all-reduce.3
  247.9 106.5 all-gather.5
where the time goes:
time: 492 us; the launch traced here: 483 us
  waiting for transfers between devices  259 us (53%)
  blocking collectives  160 us (33%)
  matrix products  30.1 us (6%)
  local copies, waits for them, and re-layouts  16.4 us (3%)
  between operations  13.9 us (3%)
    psum x1, blocking collectives, local(): summed = lax.psum(partial_value, 'section')  112 us
    psum x1, waiting for transfers between devices, local(): lax.psum((row_total * factor, row_weighted * factor), 'seq')  111 us
    all_gather x1, waiting for transfers between devices, local(): lax.all_gather(key_value, 'seq', axis=0, tiled=True)  106 us
    pmax x1, blocking collectives, local(): lax.pmax(row_peak.astype(jnp.bfloat16), 'seq').astype(row_peak.dtype)  47.6 us
    all_gather x1, waiting for transfers between devices, local(): lax.all_gather(query_rows, 'seq', axis=0, tiled=True)  41 us
  transfers between devices with their start and end apart: 4, of which 3 were waited for; matrix products, arithmetic and copies ran while one was open for 3% of the time, Pallas kernels for 0%

commit v1 on v0

v1 whole, which is shorter than its diff:
```python
import functools

import jax
import jax.numpy as jnp
from jax import lax
from jax.experimental import pallas as pl
from jax.experimental.pallas import tpu as pltpu
from jax.sharding import PartitionSpec as P

HEAD = 256
PAIR = 512
SCALE = HEAD ** -0.5
F32 = jnp.float32
BF16 = jnp.bfloat16
NT = (((1,), (1,)), ((), ()))
NN = (((1,), (0,)), ((), ()))


def seq_moves(dx, dz, dc):
    pairs = []
    for x in range(4):
        for z in range(2):
            for c in range(2):
                pairs.append((x * 4 + z * 2 + c, ((x + dx) % 4) * 4 + ((z + dz) % 2) * 2 + (c + dc) % 2))
    return pairs


def section_moves(dh, dy):
    return [(h * 4 + y, ((h + dh) % 4) * 4 + (y + dy) % 4) for h in range(4) for y in range(4)]


def along_seq(value, dx=0, dz=0, dc=0):
    return lax.ppermute(value, "seq", seq_moves(dx, dz, dc))


def along_section(value, dh=0, dy=0):
    return lax.ppermute(value, "section", section_moves(dh, dy))


def along_both(value, dh, dz):
    pairs = [(s * 16 + i, t * 16 + j) for s, t in section_moves(dh, 0) for i, j in seq_moves(0, dz, 0)]
    return lax.ppermute(value, ("section", "seq"), pairs)


def dot(a, b, dims):
    return lax.dot_general(a, b, dims, preferred_element_type=F32)


def pack_kernel(q_ref, g_ref, k_ref, v_ref, out_ref):
    for to in range(8):
        cols = pl.ds(((to % 2) * 4 + to // 2) * HEAD, HEAD)
        out_ref[to, pl.ds(0, 64), :] = q_ref[:, cols]
        out_ref[to, pl.ds(64, 64), :] = g_ref[:, cols]
        out_ref[to, pl.ds(128, 128), :] = k_ref[:, cols]
        out_ref[to, pl.ds(256, 128), :] = v_ref[:, cols]


def pack(q, g, k, v):
    return pl.pallas_call(
        pack_kernel,
        out_shape=jax.ShapeDtypeStruct((8, 384, HEAD), BF16),
        in_specs=[pl.BlockSpec(memory_space=pltpu.VMEM)] * 4,
        out_specs=pl.BlockSpec(memory_space=pltpu.VMEM),
        compiler_params=pltpu.CompilerParams(vmem_limit_bytes=4 * 2**20),
        cost_estimate=pl.CostEstimate(flops=0, bytes_accessed=2**22, transcendentals=0),
        name="pack",
    )(q, g, k, v)


def query_quarter(mine, other, j, first):
    source = mine if j < 2 else other
    return jnp.concatenate([source[(j % 2) * 4 + i, pl.ds(first, 64), :] for i in range(4)], axis=0)


def key_rows(mine, first, blocks):
    return jnp.concatenate([mine[i, pl.ds(first, 128), :] for i in blocks], axis=0)


def stats_kernel(m_ref, o_ref, out_ref):
    out_ref[...] = jnp.zeros_like(out_ref)
    k, v = key_rows(m_ref, 128, range(8)), key_rows(m_ref, 256, range(8))
    for j in range(4):
        spot = pl.ds(j * 256, 256)
        s = dot(k, query_quarter(m_ref, o_ref, j, 0), NT) * SCALE
        gp = dot(v, query_quarter(m_ref, o_ref, j, 64), NT)
        peak = jnp.max(s, axis=0, keepdims=True)
        p = jnp.exp(s - peak)
        out_ref[pl.ds(0, 1), spot] = peak
        out_ref[pl.ds(1, 1), spot] = jnp.sum(p, axis=0, keepdims=True)
        out_ref[pl.ds(2, 1), spot] = jnp.sum(p * gp, axis=0, keepdims=True)


def stats(mine, other):
    return pl.pallas_call(
        stats_kernel,
        out_shape=jax.ShapeDtypeStruct((8, 1024), F32),
        in_specs=[pl.BlockSpec(memory_space=pltpu.VMEM)] * 2,
        out_specs=pl.BlockSpec(memory_space=pltpu.VMEM),
        compiler_params=pltpu.CompilerParams(vmem_limit_bytes=8 * 2**20),
        cost_estimate=pl.CostEstimate(flops=10**9, bytes_accessed=2**22, transcendentals=2**20),
        name="stats",
    )(mine, other)


def grads_kernel(half, s0, s1, m_ref, o_ref, out, p_s, d_s, q_s, g_s):
    for j in range(4):
        q_s[pl.ds(j * 256, 256), :] = query_quarter(m_ref, o_ref, j, 0)
        g_s[pl.ds(j * 256, 256), :] = query_quarter(m_ref, o_ref, j, 64)
    blocks = range(half * 4, half * 4 + 4)
    k, v = key_rows(m_ref, 128, blocks), key_rows(m_ref, 256, blocks)
    for j in range(4):
        rows = pl.ds(j * 256, 256)
        there = pl.ds((j ^ 2) * 256, 256)
        own, far = s0[pl.ds(0, 1), rows], s1[pl.ds(0, 1), there]
        peak = jnp.maximum(own, far)
        own, far = jnp.exp(own - peak), jnp.exp(far - peak)
        total = s0[pl.ds(1, 1), rows] * own + s1[pl.ds(1, 1), there] * far
        weighted = s0[pl.ds(2, 1), rows] * own + s1[pl.ds(2, 1), there] * far
        lse = peak + jnp.log(total)
        delta = weighted / total
        s = dot(k, q_s[rows, :], NT) * SCALE
        gp = dot(v, g_s[rows, :], NT)
        p = jnp.exp(s - lse)
        p_s[:, rows] = p.astype(BF16)
        d_s[:, rows] = (p * (gp - delta)).astype(BF16)
    out[:, pl.ds(0, HEAD)] = (dot(d_s[...], q_s[...], NN) * SCALE).astype(BF16)
    out[:, pl.ds(HEAD, HEAD)] = dot(p_s[...], g_s[...], NN).astype(BF16)


def grads(half, parts, mine, other):
    return pl.pallas_call(
        functools.partial(grads_kernel, half),
        out_shape=jax.ShapeDtypeStruct((512, 2 * HEAD), BF16),
        in_specs=[pl.BlockSpec(memory_space=pltpu.VMEM)] * 4,
        out_specs=pl.BlockSpec(memory_space=pltpu.VMEM),
        scratch_shapes=[pltpu.VMEM((512, 1024), BF16)] * 2 + [pltpu.VMEM((1024, HEAD), BF16)] * 2,
        compiler_params=pltpu.CompilerParams(vmem_limit_bytes=8 * 2**20),
        cost_estimate=pl.CostEstimate(flops=10**9, bytes_accessed=2**22, transcendentals=2**19),
        name="grads",
    )(*parts, mine, other)


def project_kernel(pos_ref, *refs):
    blocks, weights, outs, total = refs[:4], refs[4:8], refs[8:12], refs[12]
    x, y = pos_ref[0], pos_ref[1]
    for w, weight in enumerate(weights):
        acc = None
        for d, block in enumerate(blocks):
            cols = pl.ds(pl.multiple_of(lax.rem(x - d + 4, 4) * HEAD, HEAD), HEAD)
            for kind in range(2):
                term = dot(block[:, pl.ds(kind * HEAD, HEAD)], weight[pl.ds(kind * 256, 256), cols], NT)
                acc = term if acc is None else acc + term
        total[:, pl.ds(w * 256, 256)] = acc.astype(BF16)
    for d, out in enumerate(outs):
        out[...] = total[pl.ds(pl.multiple_of(lax.rem(y + d, 4) * 128, 128), 128), :]


def project(pos, blocks, weights):
    return pl.pallas_call(
        project_kernel,
        out_shape=(jax.ShapeDtypeStruct((128, 1024), BF16),) * 4,
        in_specs=[pl.BlockSpec(memory_space=pltpu.SMEM)] + [pl.BlockSpec(memory_space=pltpu.VMEM)] * 8,
        out_specs=(pl.BlockSpec(memory_space=pltpu.VMEM),) * 4,
        scratch_shapes=[pltpu.VMEM((512, 1024), BF16)],
        compiler_params=pltpu.CompilerParams(vmem_limit_bytes=8 * 2**20),
        cost_estimate=pl.CostEstimate(flops=512 * 1024 * 2048 * 2, bytes_accessed=7 * 2**20, transcendentals=0),
        name="project",
    )(pos, *blocks, *weights)


def sum_y_kernel(a, b, c, d, stay, leave):
    total = ((a[...].astype(F32) + b[...].astype(F32)) + (c[...].astype(F32) + d[...].astype(F32))).astype(BF16)
    stay[...] = total[:, :512]
    leave[...] = total[:, 512:]


def sum_y(terms):
    return pl.pallas_call(
        sum_y_kernel,
        out_shape=(jax.ShapeDtypeStruct((128, 512), BF16),) * 2,
        in_specs=[pl.BlockSpec(memory_space=pltpu.VMEM)] * 4,
        out_specs=(pl.BlockSpec(memory_space=pltpu.VMEM),) * 2,
        compiler_params=pltpu.CompilerParams(vmem_limit_bytes=4 * 2**20),
        cost_estimate=pl.CostEstimate(flops=2**20, bytes_accessed=5 * 2**19, transcendentals=0),
        name="sum_y",
    )(*terms)


def sum_pair_kernel(pos_ref, a, b, c, d, *refs):
    outs, total = refs[:4], refs[4]
    h = pos_ref[5]
    total[pl.ds(0, 128), :] = (a[...].astype(F32) + b[...].astype(F32)).astype(BF16)
    total[pl.ds(128, 128), :] = (c[...].astype(F32) + d[...].astype(F32)).astype(BF16)
    for d, out in enumerate(outs):
        out[...] = total[pl.ds(pl.multiple_of(lax.rem(h + d, 4) * 64, 64), 64), :]


def sum_pair(pos, terms):
    return pl.pallas_call(
        sum_pair_kernel,
        out_shape=(jax.ShapeDtypeStruct((64, 512), BF16),) * 4,
        in_specs=[pl.BlockSpec(memory_space=pltpu.SMEM)] + [pl.BlockSpec(memory_space=pltpu.VMEM)] * 4,
        out_specs=(pl.BlockSpec(memory_space=pltpu.VMEM),) * 4,
        scratch_shapes=[pltpu.VMEM((256, 512), BF16)],
        compiler_params=pltpu.CompilerParams(vmem_limit_bytes=2 * 2**20),
        cost_estimate=pl.CostEstimate(flops=2**18, bytes_accessed=2**19, transcendentals=0),
        name="sum_pair",
    )(pos, *terms)


def sum_z_kernel(a, b, c, d, *outs):
    total = ((a[...].astype(F32) + b[...].astype(F32)) + (c[...].astype(F32) + d[...].astype(F32))).astype(BF16)
    for i, out in enumerate(outs):
        out[...] = total[:, i * 256:(i + 1) * 256]


def sum_z(terms):
    return pl.pallas_call(
        sum_z_kernel,
        out_shape=(jax.ShapeDtypeStruct((64, 256), BF16),) * 2,
        in_specs=[pl.BlockSpec(memory_space=pltpu.VMEM)] * 4,
        out_specs=(pl.BlockSpec(memory_space=pltpu.VMEM),) * 2,
        compiler_params=pltpu.CompilerParams(vmem_limit_bytes=2 * 2**20),
        cost_estimate=pl.CostEstimate(flops=2**17, bytes_accessed=2**18, transcendentals=0),
        name="sum_z",
    )(*terms)


def place_kernel(pos_ref, g0, g1, g2, g3, out_ref):
    y, c, mine, h = pos_ref[1], pos_ref[3], pos_ref[4], pos_ref[5]
    for d, got in enumerate((g0, g1, g2, g3)):
        for e in range(4):
            piece = lax.rem(h - e + 4, 4)
            for i in range(2):
                from_y = lax.rem(y - d + 4, 4)
                at = (lax.div(piece, 2) * 2 + lax.div(from_y, 2)) * 512 + lax.rem(from_y, 2) * 256
                at += lax.rem(c + i, 2) * 128 + lax.rem(piece, 2) * 64
                value = got[e, :, pl.ds(i * 256, 256)]
                out_ref[pl.ds(pl.multiple_of(at, 64), 64), :] = jnp.where(mine == 1, value, jnp.zeros_like(value))


def place(pos, got):
    return pl.pallas_call(
        place_kernel,
        out_shape=jax.ShapeDtypeStruct((2048, 256), BF16),
        in_specs=[pl.BlockSpec(memory_space=pltpu.SMEM)] + [pl.BlockSpec(memory_space=pltpu.VMEM)] * 4,
        out_specs=pl.BlockSpec(memory_space=pltpu.VMEM),
        compiler_params=pltpu.CompilerParams(vmem_limit_bytes=2 * 2**20),
        cost_estimate=pl.CostEstimate(flops=0, bytes_accessed=2**21, transcendentals=0),
        name="place",
    )(pos, *got)


def local(queries, out_grad, keys, values, key_weight, value_weight, owner):
    q, g, k, v = queries[0], out_grad[0], keys[0], values[0]
    kw, vw = key_weight[0], value_weight[0]
    seq = lax.axis_index("seq")
    section = lax.axis_index("section")
    x = lax.div(seq, 4)
    h = lax.div(section, 4)
    y = lax.rem(section, 4)
    c = lax.rem(seq, 2)
    z = lax.rem(lax.div(seq, 2), 2)
    pos = jnp.stack([x, y, z, c, (section == owner[0]).astype(jnp.int32), h]).astype(jnp.int32)

    tie = lax.optimization_barrier
    rows = pack(q, g, k, v)
    groups = [[xx * 4 + zz * 2 + cc for xx in range(4) for zz in range(2)] for cc in range(2)]
    mine = lax.all_to_all(rows, "seq", 0, 0, axis_index_groups=groups)
    mine, kw, vw = tie((mine, kw, vw))
    other = along_seq(mine[:, :128], dc=1)

    def half(matrix, at):
        return lax.dynamic_slice(matrix, (jnp.int32(0), at * 1024), (256, 1024))

    weight = jnp.concatenate([half(kw, z), half(vw, z)], axis=0)
    weight_z = along_seq(jnp.concatenate([half(kw, 1 - z), half(vw, 1 - z)], axis=0), dz=1)
    weight_c = along_seq(weight, dc=1)

    own = stats(mine, other)
    parts = [own, along_seq(own, dc=1)]

    low, high = grads(0, parts, mine, other), grads(1, parts, mine, other)
    low_r, low_l = along_seq(low, dx=1), along_seq(low, dx=3)
    low_r, low_l, high = tie((low_r, low_l, high))
    low_o, high_l = along_seq(low_r, dx=1), along_seq(high, dx=3)
    low_o, high_l, weight_z = tie((low_o, high_l, weight_z))
    high_r, high_o = along_seq(high, dx=1), along_seq(high_l, dx=3)
    weights = (weight, weight_c, weight_z, along_seq(weight_z, dc=1))

    def sum_two(pieces):
        stay, leave = sum_y([pieces[0]] + [along_section(pieces[d], dy=d) for d in (1, 2, 3)])
        return [stay, along_seq(leave, dz=1)]

    low_pieces = project(pos, (low, low_r, low_o, low_l), weights)
    high_r, high_o, first = tie((high_r, high_o, low_pieces[0]))
    high_pieces = project(pos, (high, high_r, high_o, high_l), weights)
    terms = sum_two([first, *low_pieces[1:]]) + sum_two(high_pieces)

    pieces = sum_pair(pos, terms)
    cols = sum_z([pieces[0]] + [along_section(pieces[d], dh=d) for d in (1, 2, 3)])

    rows = jnp.concatenate([cols[0], along_seq(cols[1], dc=1)], axis=1)
    rows = jnp.stack([rows] + [along_section(rows, dh=d) for d in (1, 2, 3)])
    return place(pos, [rows] + [along_section(rows, dy=d) for d in (1, 2, 3)])[None]


def solution(mesh):
    in_specs = (P("section", "seq", None),) * 6 + (P(),)
    return jax.shard_map(local, mesh=mesh, in_specs=in_specs, out_specs=P("section", None, "seq"), check_vma=False)
```

time: 492 us -> 171 us (0.35); the launches traced: 483 us -> 170 us
  waiting for transfers between devices: 259 us -> 75.1 us
  blocking collectives: 160 us -> 25 us
  starting transfers between devices: 0.12 us -> 43.5 us
  matrix products: 30.1 us -> 0 us
  Pallas kernels: 0 us -> 17.1 us
  between operations: 13.9 us -> 0.86 us
  local copies, waits for them, and re-layouts: 16.4 us -> 8.29 us
    all_gather x3 -> x0, waiting for transfers between devices: 147 us -> none  [the longest x1 106 us: local(): lax.all_gather(key_value, 'seq', axis=0, tiled=True)]
    psum x1 -> x0, blocking collectives: 112 us -> none  [local(): summed = lax.psum(partial_value, 'section')]
    psum x1 -> x0, waiting for transfers between devices: 111 us -> none  [local(): lax.psum((row_total * factor, row_weighted * factor), 'seq')]
    ppermute x0 -> x29, waiting for transfers between devices: none -> 75.1 us  [the longest x14 38.8 us: along_seq(): return lax.ppermute(value, 'seq', seq_moves(dx, dz, dc))]
    pmax x1 -> x0, blocking collectives: 47.6 us -> none  [local(): lax.pmax(row_peak.astype(jnp.bfloat16), 'seq').astype(row_peak.dtype)]
    ppermute x0 -> x29, starting transfers between devices: none -> 43.5 us  [the longest x15 32.3 us: along_section(): return lax.ppermute(value, 'section', section_moves(dh, dy))]
    dot_general x5 -> x0, matrix products: 30.1 us -> none  [the longest x1 8.78 us: local(): lax.dot_general(lax.all_gather(key_value, 'seq', axis=0, tiled=True), pro...]
    all_to_all x0 -> x1, blocking collectives: none -> 25 us  [local(): mine = lax.all_to_all(rows, 'seq', 0, 0, axis_index_groups=groups)]
  transfers between devices with their start and end apart: 4 -> 29, of which waited for: 3 -> 21; matrix products, arithmetic and copies ran while one was open for 3% -> 0% of each run, Pallas kernels for 0% -> 4%
where the time goes in v1:
time: 171 us; the launch traced here: 170 us
  waiting for transfers between devices  75.1 us (44%)
  starting transfers between devices  43.5 us (25%)
  blocking collectives  25 us (15%)
  Pallas kernels  17.1 us (10%)
  local copies, waits for them, and re-layouts  8.29 us (5%)
    ppermute x14, waiting for transfers between devices, along_seq(): return lax.ppermute(value, 'seq', seq_moves(dx, dz, dc))  38.8 us
    ppermute x15, waiting for transfers between devices, along_section(): return lax.ppermute(value, 'section', section_moves(dh, dy))  36.3 us
    ppermute x15, starting transfers between devices, along_section(): return lax.ppermute(value, 'section', section_moves(dh, dy))  32.3 us
    all_to_all x1, blocking collectives, local(): mine = lax.all_to_all(rows, 'seq', 0, 0, axis_index_groups=groups)  25 us
    ppermute x14, starting transfers between devices, along_seq(): return lax.ppermute(value, 'seq', seq_moves(dx, dz, dc))  11.2 us
    pallas_call x2, Pallas kernels, project(): pl.pallas_call(project_kernel, out_shape=(jax.ShapeDtypeStruct((128, 1024...  8.69 us
    unnamed x29, local copies, waits for them, and re-layouts  7.96 us
  transfers between devices with their start and end apart: 29, of which 21 were waited for; matrix products, arithmetic and copies ran while one was open for 0% of the time, Pallas kernels for 4%

profile of v1, /device:TPU:6, one launch (start us, length us, event | category | flops | bytes accessed | tf_op | source)
XLA Modules:
  0.0 170.0 jit_solution(16783483644141035689)
XLA Ops:
  4.1 25.0 %all_to_all.5.m_ref = bf16[8,384,256]{2,1,0:T(8,128)(2,1)S(1)} all-to-all(bf16[8,384,256]{2,1,0:T(8,128)(2,1)S(1)} %pack.1), channel_id=1, replica_groups={{0,2,4,6,8,10,12,14},{1,3,5,7,9,11,13,15},{16,18,20,22,24,26,28,30},{17..., dimensions={0} | all-to-all | bytes 3145728 | tf_op jit(solution)/shard_map/all_to_all | solution.py:269
  36.0 2.6 %collective-permute-start.2 = (bf16[512,512]{1,0:T(8,128)(2,1)S(1)}, bf16[512,512]{1,0:T(8,128)(2,1)S(1)}, u32[]{:S(2)}, u32[]{:S(2)}) collective-permute-start(bf16[512,512]{1,0:T(8,128)(2,1)S(1)} %grads.2.refs_0_), channel_id=1, source_target_pairs={{0,4},{1,5},{2,6},{3,7},{4,8},{5,9},{6,10},{7,11},{8,12},{9,13},{1... | collective-permute-start | bytes 1572872 | tf_op jit(solution)/shard_map/ppermute | solution.py:33
  41.5 8.5 %collective-permute-done.2.refs_1_ = bf16[512,512]{1,0:T(8,128)(2,1)S(1)} collective-permute-done((bf16[512,512]{1,0:T(8,128)(2,1)S(1)}, bf16[512,512]{1,0:T(8,128)(2,1)S(1)}, u32[]{:S(2)}, u32[]{:S(2)}) %collective-permute-start.2) | collective-permute-done | bytes 524320 | tf_op jit(solution)/shard_map/ppermute | solution.py:33
  50.1 3.4 %collective-permute-done.3.refs_3_ = bf16[512,512]{1,0:T(8,128)(2,1)S(1)} collective-permute-done((bf16[512,512]{1,0:T(8,128)(2,1)S(1)}, bf16[512,512]{1,0:T(8,128)(2,1)S(1)}, u32[]{:S(2)}, u32[]{:S(2)}) %collective-permute-start.3) | collective-permute-done | bytes 524320 | tf_op jit(solution)/shard_map/ppermute | solution.py:33
  53.5 3.2 %collective-permute-start.5 = (bf16[512,512]{1,0:T(8,128)(2,1)S(1)}, bf16[512,512]{1,0:T(8,128)(2,1)S(1)}, u32[]{:S(2)}, u32[]{:S(2)}) collective-permute-start(bf16[512,512]{1,0:T(8,128)(2,1)S(1)} %collective-permute-done.2.refs_1_), channel_id=1, source_target_pairs={{0,4},{1,5},{2,6},{3,7},{4,8},{5,9},{6,10},{7,11},{8,12},{9,13},{1... | collective-permute-start | bytes 1572872 | tf_op jit(solution)/shard_map/ppermute | solution.py:33
  56.9 6.8 %collective-permute-done.7.refs_6_ = bf16[512,1024]{1,0:T(8,128)(2,1)S(1)} collective-permute-done((bf16[512,1024]{1,0:T(8,128)(2,1)S(1)}, bf16[512,1024]{1,0:T(8,128)(2,1)S(1)}, u32[]{:S(2)}, u32[]{:S(2)}) %collective-permute-start.7) | collective-permute-done | bytes 1048608 | tf_op jit(solution)/shard_map/ppermute | solution.py:33
  63.7 4.2 %collective-permute-done.6.refs_3_ = bf16[512,512]{1,0:T(8,128)(2,1)} collective-permute-done((bf16[512,512]{1,0:T(8,128)(2,1)}, bf16[512,512]{1,0:T(8,128)(2,1)}, u32[]{:S(2)}, u32[]{:S(2)}) %collective-permute-start.6) | collective-permute-done | bytes 524320 | tf_op jit(solution)/shard_map/ppermute | solution.py:33
  68.7 2.6 %collective-permute-start.4 = (bf16[512,512]{1,0:T(8,128)(2,1)}, bf16[512,512]{1,0:T(8,128)(2,1)}, u32[]{:S(2)}, u32[]{:S(2)}) collective-permute-start(bf16[512,512]{1,0:T(8,128)(2,1)} %grads.3.refs_0_), channel_id=1, source_target_pairs={{0,4},{1,5},{2,6},{3,7},{4,8},{5,9},{6,10},{7,11},{8,12},{9,13},{1... | collective-permute-start | bytes 1572872 | tf_op jit(solution)/shard_map/ppermute | solution.py:33
  75.2 4.0 %project.2 = (bf16[128,1024]{1,0:T(8,128)(2,1)S(1)}, bf16[128,1024]{1,0:T(8,128)(2,1)S(1)}, bf16[128,1024]{1,0:T(8,128)(2,1)S(1)}, bf16[128,1024]{1,0:T(8,128)(2,1)S(1)}) custom-call(s32[6]{0:T(128)S(1)} %stack.46.pos_ref, bf16[512,512]{1,0:T(8,128)(2,1)S(1)} %grads.2.refs_0_, bf16[512,512]{1,0:T(8,128)(2,1)S(1)} %copy-done.5, ...), custom_call_target="tpu_custom_call" | custom-call | flops 2147483648 | bytes 7340032 | tf_op jit(solution)/shard_map/project/pallas_call | solution.py:159
  79.2 4.3 %collective-permute-done.4.refs_1_ = bf16[512,512]{1,0:T(8,128)(2,1)} collective-permute-done((bf16[512,512]{1,0:T(8,128)(2,1)}, bf16[512,512]{1,0:T(8,128)(2,1)}, u32[]{:S(2)}, u32[]{:S(2)}) %collective-permute-start.4) | collective-permute-done | bytes 524320 | tf_op jit(solution)/shard_map/ppermute | solution.py:33
  83.5 3.4 %collective-permute-done.8.refs_2_ = bf16[512,512]{1,0:T(8,128)(2,1)} collective-permute-done((bf16[512,512]{1,0:T(8,128)(2,1)}, bf16[512,512]{1,0:T(8,128)(2,1)}, u32[]{:S(2)}, u32[]{:S(2)}) %collective-permute-start.8) | collective-permute-done | bytes 524320 | tf_op jit(solution)/shard_map/ppermute | solution.py:33
  86.9 4.7 %project.3 = (bf16[128,1024]{1,0:T(8,128)(2,1)S(1)}, bf16[128,1024]{1,0:T(8,128)(2,1)S(1)}, bf16[128,1024]{1,0:T(8,128)(2,1)S(1)}, bf16[128,1024]{1,0:T(8,128)(2,1)S(1)}) custom-call(s32[6]{0:T(128)S(1)} %stack.46.pos_ref, bf16[512,512]{1,0:T(8,128)(2,1)} %grads.3.refs_0_, bf16[512,512]{1,0:T(8,128)(2,1)} %collective-permute-done.4.refs_1_, ...), custom_call_target="tpu_custom_call" | custom-call | flops 2147483648 | bytes 7340032 | tf_op jit(solution)/shard_map/project/pallas_call | solution.py:159
  93.2 2.9 %collective-permute-start.16 = (bf16[128,1024]{1,0:T(8,128)(2,1)S(1)}, bf16[128,1024]{1,0:T(8,128)(2,1)S(1)}, u32[]{:S(2)}, u32[]{:S(2)}) collective-permute-start(bf16[128,1024]{1,0:T(8,128)(2,1)S(1)} %get-tuple-element.55), channel_id=1, source_target_pairs={{0,32},{16,48},{32,0},{48,16},{64,96},{80,112},{96,64},{112,80},{1... | collective-permute-start | bytes 786440 | tf_op jit(solution)/shard_map/ppermute | solution.py:37
  98.9 3.3 %collective-permute-done.15.b = bf16[128,1024]{1,0:T(8,128)(2,1)S(1)} collective-permute-done((bf16[128,1024]{1,0:T(8,128)(2,1)S(1)}, bf16[128,1024]{1,0:T(8,128)(2,1)S(1)}, u32[]{:S(2)}, u32[]{:S(2)}) %collective-permute-start.15) | collective-permute-done | bytes 262176 | tf_op jit(solution)/shard_map/ppermute | solution.py:37
  103.9 5.1 %collective-permute-done.16.c = bf16[128,1024]{1,0:T(8,128)(2,1)S(1)} collective-permute-done((bf16[128,1024]{1,0:T(8,128)(2,1)S(1)}, bf16[128,1024]{1,0:T(8,128)(2,1)S(1)}, u32[]{:S(2)}, u32[]{:S(2)}) %collective-permute-start.16) | collective-permute-done | bytes 262176 | tf_op jit(solution)/shard_map/ppermute | solution.py:37
  112.2 6.4 %collective-permute-done.12.c = bf16[128,1024]{1,0:T(8,128)(2,1)S(1)} collective-permute-done((bf16[128,1024]{1,0:T(8,128)(2,1)S(1)}, bf16[128,1024]{1,0:T(8,128)(2,1)S(1)}, u32[]{:S(2)}, u32[]{:S(2)}) %collective-permute-start.12) | collective-permute-done | bytes 262176 | tf_op jit(solution)/shard_map/ppermute | solution.py:37
  119.5 4.3 %collective-permute-done.14.b = bf16[128,512]{1,0:T(8,128)(2,1)S(1)} collective-permute-done((bf16[128,512]{1,0:T(8,128)(2,1)S(1)}, bf16[128,512]{1,0:T(8,128)(2,1)S(1)}, u32[]{:S(2)}, u32[]{:S(2)}) %collective-permute-start.14) | collective-permute-done | bytes 131104 | tf_op jit(solution)/shard_map/ppermute | solution.py:33
  124.5 3.3 %collective-permute-start.19 = (bf16[64,512]{1,0:T(8,128)(2,1)S(1)}, bf16[64,512]{1,0:T(8,128)(2,1)S(1)}, u32[]{:S(2)}, u32[]{:S(2)}) collective-permute-start(bf16[64,512]{1,0:T(8,128)(2,1)S(1)} %get-tuple-element.60), channel_id=1, source_target_pairs={{0,64},{16,80},{32,96},{48,112},{64,128},{80,144},{96,160},{112,17... | collective-permute-start | bytes 196616 | tf_op jit(solution)/shard_map/ppermute | solution.py:37
  127.8 4.5 %collective-permute-start.20 = (bf16[64,512]{1,0:T(8,128)(2,1)S(1)}, bf16[64,512]{1,0:T(8,128)(2,1)S(1)}, u32[]{:S(2)}, u32[]{:S(2)}) collective-permute-start(bf16[64,512]{1,0:T(8,128)(2,1)S(1)} %get-tuple-element.61), channel_id=1, source_target_pairs={{0,128},{16,144},{32,160},{48,176},{64,192},{80,208},{96,224},{112... | collective-permute-start | bytes 196616 | tf_op jit(solution)/shard_map/ppermute | solution.py:37
  132.3 2.7 %collective-permute-start.21 = (bf16[64,512]{1,0:T(8,128)(2,1)S(1)}, bf16[64,512]{1,0:T(8,128)(2,1)S(1)}, u32[]{:S(2)}, u32[]{:S(2)}) collective-permute-start(bf16[64,512]{1,0:T(8,128)(2,1)S(1)} %get-tuple-element.62), channel_id=1, source_target_pairs={{0,192},{16,208},{32,224},{48,240},{64,0},{80,16},{96,32},{112,48}... | collective-permute-start | bytes 196616 | tf_op jit(solution)/shard_map/ppermute | solution.py:37
  141.5 4.2 %collective-permute-start.24 = (bf16[64,512]{1,0:T(8,128)(2,1)S(1)}, bf16[64,512]{1,0:T(8,128)(2,1)S(1)}, u32[]{:S(2)}, u32[]{:S(2)}) collective-permute-start(bf16[64,512]{1,0:T(8,128)(2,1)S(1)} %constant_dynamic-update-slice_fusion), channel_id=1, source_target_pairs={{0,128},{16,144},{32,160},{48,176},{64,192},{80,208},{96,224},{112... | collective-permute-start | bytes 196616 | tf_op jit(solution)/shard_map/ppermute | solution.py:37
  147.4 4.5 %collective-permute-done.24 = bf16[64,512]{1,0:T(8,128)(2,1)S(1)} collective-permute-done((bf16[64,512]{1,0:T(8,128)(2,1)S(1)}, bf16[64,512]{1,0:T(8,128)(2,1)S(1)}, u32[]{:S(2)}, u32[]{:S(2)}) %collective-permute-start.24) | collective-permute-done | bytes 65568 | tf_op jit(solution)/shard_map/ppermute | solution.py:37
  157.6 4.2 %collective-permute-done.26.g1 = bf16[4,64,512]{2,1,0:T(8,128)(2,1)S(1)} collective-permute-done((bf16[4,64,512]{2,1,0:T(8,128)(2,1)S(1)}, bf16[4,64,512]{2,1,0:T(8,128)(2,1)S(1)}, u32[]{:S(2)}, u32[]{:S(2)}) %collective-permute-start.26) | collective-permute-done | bytes 262176 | tf_op jit(solution)/shard_map/ppermute | solution.py:37
  161.8 6.5 %collective-permute-done.27.g2 = bf16[4,64,512]{2,1,0:T(8,128)(2,1)S(1)} collective-permute-done((bf16[4,64,512]{2,1,0:T(8,128)(2,1)S(1)}, bf16[4,64,512]{2,1,0:T(8,128)(2,1)S(1)}, u32[]{:S(2)}, u32[]{:S(2)}) %collective-permute-start.27) | collective-permute-done | bytes 262176 | tf_op jit(solution)/shard_map/ppermute | solution.py:37
  (82 shorter events, 44.4 us)
Async XLA Ops:
  36.0 14.1 %collective-permute-start.2 = (bf16[512,512]{1,0:T(8,128)(2,1)S(1)}, bf16[512,512]{1,0:T(8,128)(2,1)S(1)}, u32[]{:S(2)}, u32[]{:S(2)}) collective-permute-start(bf16[512,512]{1,0:T(8,128)(2,1)S(1)} %grads.2.refs_0_), channel_id=1, source_target_pairs={{0,4},{1,5},{2,6},{3,7},{4,8},{5,9},{6,10},{7,11},{8,12},{9,13},{1... | collective-permute-start | bytes 1572872 | tf_op jit(solution)/shard_map/ppermute | solution.py:33
  38.6 14.9 %collective-permute-start.3 = (bf16[512,512]{1,0:T(8,128)(2,1)S(1)}, bf16[512,512]{1,0:T(8,128)(2,1)S(1)}, u32[]{:S(2)}, u32[]{:S(2)}) collective-permute-start(bf16[512,512]{1,0:T(8,128)(2,1)S(1)} %grads.2.refs_0_), channel_id=1, source_target_pairs={{0,12},{1,13},{2,14},{3,15},{4,0},{5,1},{6,2},{7,3},{8,4},{9,5},{1... | collective-permute-start | bytes 1572872 | tf_op jit(solution)/shard_map/ppermute | solution.py:33
  38.6 25.0 %collective-permute-start.7 = (bf16[512,1024]{1,0:T(8,128)(2,1)S(1)}, bf16[512,1024]{1,0:T(8,128)(2,1)S(1)}, u32[]{:S(2)}, u32[]{:S(2)}) collective-permute-start(bf16[512,1024]{1,0:T(8,128)(2,1)S(1)} %pad_maximum_fusion), channel_id=1, source_target_pairs={{0,2},{1,3},{2,0},{3,1},{4,6},{5,7},{6,4},{7,5},{8,10},{9,11},{10,... | collective-permute-start | bytes 3145736 | tf_op jit(solution)/shard_map/ppermute | solution.py:33
  53.5 14.4 %collective-permute-start.6 = (bf16[512,512]{1,0:T(8,128)(2,1)}, bf16[512,512]{1,0:T(8,128)(2,1)}, u32[]{:S(2)}, u32[]{:S(2)}) collective-permute-start(bf16[512,512]{1,0:T(8,128)(2,1)} %grads.3.refs_0_), channel_id=1, source_target_pairs={{0,12},{1,13},{2,14},{3,15},{4,0},{5,1},{6,2},{7,3},{8,4},{9,5},{1... | collective-permute-start | bytes 1572872 | tf_op jit(solution)/shard_map/ppermute | solution.py:33
  53.5 14.4 %collective-permute-start.5 = (bf16[512,512]{1,0:T(8,128)(2,1)S(1)}, bf16[512,512]{1,0:T(8,128)(2,1)S(1)}, u32[]{:S(2)}, u32[]{:S(2)}) collective-permute-start(bf16[512,512]{1,0:T(8,128)(2,1)S(1)} %collective-permute-done.2.refs_1_), channel_id=1, source_target_pairs={{0,4},{1,5},{2,6},{3,7},{4,8},{5,9},{6,10},{7,11},{8,12},{9,13},{1... | collective-permute-start | bytes 1572872 | tf_op jit(solution)/shard_map/ppermute | solution.py:33
  56.8 15.3 %collective-permute-start.9 = (bf16[512,1024]{1,0:T(8,128)(2,1)S(1)}, bf16[512,1024]{1,0:T(8,128)(2,1)}, u32[]{:S(2)}, u32[]{:S(2)}) collective-permute-start(bf16[512,1024]{1,0:T(8,128)(2,1)S(1)} %pad_maximum_fusion.1.refs_4_), channel_id=1, source_target_pairs={{0,1},{1,0},{2,3},{3,2},{4,5},{5,4},{6,7},{7,6},{8,9},{9,8},{10,11... | collective-permute-start | bytes 3145736 | tf_op jit(solution)/shard_map/ppermute | solution.py:33
  68.7 14.8 %collective-permute-start.4 = (bf16[512,512]{1,0:T(8,128)(2,1)}, bf16[512,512]{1,0:T(8,128)(2,1)}, u32[]{:S(2)}, u32[]{:S(2)}) collective-permute-start(bf16[512,512]{1,0:T(8,128)(2,1)} %grads.3.refs_0_), channel_id=1, source_target_pairs={{0,4},{1,5},{2,6},{3,7},{4,8},{5,9},{6,10},{7,11},{8,12},{9,13},{1... | collective-permute-start | bytes 1572872 | tf_op jit(solution)/shard_map/ppermute | solution.py:33
  71.3 15.6 %collective-permute-start.8 = (bf16[512,512]{1,0:T(8,128)(2,1)}, bf16[512,512]{1,0:T(8,128)(2,1)}, u32[]{:S(2)}, u32[]{:S(2)}) collective-permute-start(bf16[512,512]{1,0:T(8,128)(2,1)} %collective-permute-done.6.refs_3_), channel_id=1, source_target_pairs={{0,12},{1,13},{2,14},{3,15},{4,0},{5,1},{6,2},{7,3},{8,4},{9,5},{1... | collective-permute-start | bytes 1572872 | tf_op jit(solution)/shard_map/ppermute | solution.py:33
  91.6 10.7 %collective-permute-start.15 = (bf16[128,1024]{1,0:T(8,128)(2,1)S(1)}, bf16[128,1024]{1,0:T(8,128)(2,1)S(1)}, u32[]{:S(2)}, u32[]{:S(2)}) collective-permute-start(bf16[128,1024]{1,0:T(8,128)(2,1)S(1)} %get-tuple-element.54), channel_id=1, source_target_pairs={{0,16},{16,32},{32,48},{48,0},{64,80},{80,96},{96,112},{112,64},{1... | collective-permute-start | bytes 786440 | tf_op jit(solution)/shard_map/ppermute | solution.py:37
  93.2 15.8 %collective-permute-start.16 = (bf16[128,1024]{1,0:T(8,128)(2,1)S(1)}, bf16[128,1024]{1,0:T(8,128)(2,1)S(1)}, u32[]{:S(2)}, u32[]{:S(2)}) collective-permute-start(bf16[128,1024]{1,0:T(8,128)(2,1)S(1)} %get-tuple-element.55), channel_id=1, source_target_pairs={{0,32},{16,48},{32,0},{48,16},{64,96},{80,112},{96,64},{112,80},{1... | collective-permute-start | bytes 786440 | tf_op jit(solution)/shard_map/ppermute | solution.py:37
  96.1 12.9 %collective-permute-start.17 = (bf16[128,1024]{1,0:T(8,128)(2,1)S(1)}, bf16[128,1024]{1,0:T(8,128)(2,1)S(1)}, u32[]{:S(2)}, u32[]{:S(2)}) collective-permute-start(bf16[128,1024]{1,0:T(8,128)(2,1)S(1)} %get-tuple-element.56), channel_id=1, source_target_pairs={{0,48},{16,0},{32,16},{48,32},{64,112},{80,64},{96,80},{112,96},{1... | collective-permute-start | bytes 786440 | tf_op jit(solution)/shard_map/ppermute | solution.py:37
  97.5 14.7 %collective-permute-start.11 = (bf16[128,1024]{1,0:T(8,128)(2,1)S(1)}, bf16[128,1024]{1,0:T(8,128)(2,1)S(1)}, u32[]{:S(2)}, u32[]{:S(2)}) collective-permute-start(bf16[128,1024]{1,0:T(8,128)(2,1)S(1)} %get-tuple-element.46), channel_id=1, source_target_pairs={{0,16},{16,32},{32,48},{48,0},{64,80},{80,96},{96,112},{112,64},{1... | collective-permute-start | bytes 786440 | tf_op jit(solution)/shard_map/ppermute | solution.py:37
  98.2 20.5 %collective-permute-start.12 = (bf16[128,1024]{1,0:T(8,128)(2,1)S(1)}, bf16[128,1024]{1,0:T(8,128)(2,1)S(1)}, u32[]{:S(2)}, u32[]{:S(2)}) collective-permute-start(bf16[128,1024]{1,0:T(8,128)(2,1)S(1)} %get-tuple-element.47), channel_id=1, source_target_pairs={{0,32},{16,48},{32,0},{48,16},{64,96},{80,112},{96,64},{112,80},{1... | collective-permute-start | bytes 786440 | tf_op jit(solution)/shard_map/ppermute | solution.py:37
  102.3 16.4 %collective-permute-start.13 = (bf16[128,1024]{1,0:T(8,128)(2,1)S(1)}, bf16[128,1024]{1,0:T(8,128)(2,1)S(1)}, u32[]{:S(2)}, u32[]{:S(2)}) collective-permute-start(bf16[128,1024]{1,0:T(8,128)(2,1)S(1)} %get-tuple-element.48), channel_id=1, source_target_pairs={{0,48},{16,0},{32,16},{48,32},{64,112},{80,64},{96,80},{112,96},{1... | collective-permute-start | bytes 786440 | tf_op jit(solution)/shard_map/ppermute | solution.py:37
  109.2 10.3 %collective-permute-start.18 = (bf16[128,512]{1,0:T(8,128)(2,1)S(1)}, bf16[128,512]{1,0:T(8,128)(2,1)S(1)}, u32[]{:S(2)}, u32[]{:S(2)}) collective-permute-start(bf16[128,512]{1,0:T(8,128)(2,1)S(1)} %get-tuple-element.58), channel_id=1, source_target_pairs={{0,2},{1,3},{2,0},{3,1},{4,6},{5,7},{6,4},{7,5},{8,10},{9,11},{10,... | collective-permute-start | bytes 393224 | tf_op jit(solution)/shard_map/ppermute | solution.py:33
  124.5 10.5 %collective-permute-start.19 = (bf16[64,512]{1,0:T(8,128)(2,1)S(1)}, bf16[64,512]{1,0:T(8,128)(2,1)S(1)}, u32[]{:S(2)}, u32[]{:S(2)}) collective-permute-start(bf16[64,512]{1,0:T(8,128)(2,1)S(1)} %get-tuple-element.60), channel_id=1, source_target_pairs={{0,64},{16,80},{32,96},{48,112},{64,128},{80,144},{96,160},{112,17... | collective-permute-start | bytes 196616 | tf_op jit(solution)/shard_map/ppermute | solution.py:37
  127.8 8.7 %collective-permute-start.20 = (bf16[64,512]{1,0:T(8,128)(2,1)S(1)}, bf16[64,512]{1,0:T(8,128)(2,1)S(1)}, u32[]{:S(2)}, u32[]{:S(2)}) collective-permute-start(bf16[64,512]{1,0:T(8,128)(2,1)S(1)} %get-tuple-element.61), channel_id=1, source_target_pairs={{0,128},{16,144},{32,160},{48,176},{64,192},{80,208},{96,224},{112... | collective-permute-start | bytes 196616 | tf_op jit(solution)/shard_map/ppermute | solution.py:37
  132.3 6.0 %collective-permute-start.21 = (bf16[64,512]{1,0:T(8,128)(2,1)S(1)}, bf16[64,512]{1,0:T(8,128)(2,1)S(1)}, u32[]{:S(2)}, u32[]{:S(2)}) collective-permute-start(bf16[64,512]{1,0:T(8,128)(2,1)S(1)} %get-tuple-element.62), channel_id=1, source_target_pairs={{0,192},{16,208},{32,224},{48,240},{64,0},{80,16},{96,32},{112,48}... | collective-permute-start | bytes 196616 | tf_op jit(solution)/shard_map/ppermute | solution.py:37
  139.6 7.8 %collective-permute-start.23 = (bf16[64,512]{1,0:T(8,128)(2,1)S(1)}, bf16[64,512]{1,0:T(8,128)(2,1)S(1)}, u32[]{:S(2)}, u32[]{:S(2)}) collective-permute-start(bf16[64,512]{1,0:T(8,128)(2,1)S(1)} %constant_dynamic-update-slice_fusion), channel_id=1, source_target_pairs={{0,64},{16,80},{32,96},{48,112},{64,128},{80,144},{96,160},{112,17... | collective-permute-start | bytes 196616 | tf_op jit(solution)/shard_map/ppermute | solution.py:37
  141.5 10.4 %collective-permute-start.24 = (bf16[64,512]{1,0:T(8,128)(2,1)S(1)}, bf16[64,512]{1,0:T(8,128)(2,1)S(1)}, u32[]{:S(2)}, u32[]{:S(2)}) collective-permute-start(bf16[64,512]{1,0:T(8,128)(2,1)S(1)} %constant_dynamic-update-slice_fusion), channel_id=1, source_target_pairs={{0,128},{16,144},{32,160},{48,176},{64,192},{80,208},{96,224},{112... | collective-permute-start | bytes 196616 | tf_op jit(solution)/shard_map/ppermute | solution.py:37
  145.8 6.5 %collective-permute-start.25 = (bf16[64,512]{1,0:T(8,128)(2,1)S(1)}, bf16[64,512]{1,0:T(8,128)(2,1)S(1)}, u32[]{:S(2)}, u32[]{:S(2)}) collective-permute-start(bf16[64,512]{1,0:T(8,128)(2,1)S(1)} %constant_dynamic-update-slice_fusion), channel_id=1, source_target_pairs={{0,192},{16,208},{32,224},{48,240},{64,0},{80,16},{96,32},{112,48}... | collective-permute-start | bytes 196616 | tf_op jit(solution)/shard_map/ppermute | solution.py:37
  152.3 9.4 %collective-permute-start.26 = (bf16[4,64,512]{2,1,0:T(8,128)(2,1)S(1)}, bf16[4,64,512]{2,1,0:T(8,128)(2,1)S(1)}, u32[]{:S(2)}, u32[]{:S(2)}) collective-permute-start(bf16[4,64,512]{2,1,0:T(8,128)(2,1)S(1)} %pad_maximum_fusion.2.g0), channel_id=1, source_target_pairs={{0,16},{16,32},{32,48},{48,0},{64,80},{80,96},{96,112},{112,64},{1... | collective-permute-start | bytes 786440 | tf_op jit(solution)/shard_map/ppermute | solution.py:37
  154.2 14.1 %collective-permute-start.27 = (bf16[4,64,512]{2,1,0:T(8,128)(2,1)S(1)}, bf16[4,64,512]{2,1,0:T(8,128)(2,1)S(1)}, u32[]{:S(2)}, u32[]{:S(2)}) collective-permute-start(bf16[4,64,512]{2,1,0:T(8,128)(2,1)S(1)} %pad_maximum_fusion.2.g0), channel_id=1, source_target_pairs={{0,32},{16,48},{32,0},{48,16},{64,96},{80,112},{96,64},{112,80},{1... | collective-permute-start | bytes 786440 | tf_op jit(solution)/shard_map/ppermute | solution.py:37
  156.5 11.8 %collective-permute-start.28 = (bf16[4,64,512]{2,1,0:T(8,128)(2,1)S(1)}, bf16[4,64,512]{2,1,0:T(8,128)(2,1)S(1)}, u32[]{:S(2)}, u32[]{:S(2)}) collective-permute-start(bf16[4,64,512]{2,1,0:T(8,128)(2,1)S(1)} %pad_maximum_fusion.2.g0), channel_id=1, source_target_pairs={{0,48},{16,0},{32,16},{48,32},{64,112},{80,64},{96,80},{112,96},{1... | collective-permute-start | bytes 786440 | tf_op jit(solution)/shard_map/ppermute | solution.py:37
  (19 other events, 68.7 us)

commit v2 on v1

--- a/solution.py
+++ b/solution.py
@@ -140,57 +140,85 @@
     )(*parts, mine, other)
 
 
+def head_cols(x, d):
+    return pl.ds(pl.multiple_of(lax.rem(x - d + 4, 4) * HEAD, HEAD), HEAD)
+
+
 def project_kernel(pos_ref, *refs):
-    blocks, weights, outs, total = refs[:4], refs[4:8], refs[8:12], refs[12]
-    x, y = pos_ref[0], pos_ref[1]
-    for w, weight in enumerate(weights):
-        acc = None
-        for d, block in enumerate(blocks):
-            cols = pl.ds(pl.multiple_of(lax.rem(x - d + 4, 4) * HEAD, HEAD), HEAD)
-            for kind in range(2):
-                term = dot(block[:, pl.ds(kind * HEAD, HEAD)], weight[pl.ds(kind * 256, 256), cols], NT)
-                acc = term if acc is None else acc + term
-        total[:, pl.ds(w * 256, 256)] = acc.astype(BF16)
-    for d, out in enumerate(outs):
-        out[...] = total[pl.ds(pl.multiple_of(lax.rem(y + d, 4) * 128, 128), 128), :]
+    blocks, weights, out = refs[:6], refs[6:8], refs[8]
+    for half in range(2):
+        for w, weight in enumerate(weights):
+            acc = None
+            for n, d in enumerate((0, 1, 3)):
+                for kind in range(2):
+                    block = blocks[2 * n + half][:, pl.ds(kind * HEAD, HEAD)]
+                    term = dot(block, weight[pl.ds(kind * 256, 256), head_cols(pos_ref[0], d)], NT)
+                    acc = term if acc is None else acc + term
+            out[pl.ds(half * 512, 512), pl.ds(w * 256, 256)] = acc.astype(out.dtype)
 
 
 def project(pos, blocks, weights):
     return pl.pallas_call(
         project_kernel,
-        out_shape=(jax.ShapeDtypeStruct((128, 1024), BF16),) * 4,
+        out_shape=jax.ShapeDtypeStruct((1024, 512), BF16),
         in_specs=[pl.BlockSpec(memory_space=pltpu.SMEM)] + [pl.BlockSpec(memory_space=pltpu.VMEM)] * 8,
-        out_specs=(pl.BlockSpec(memory_space=pltpu.VMEM),) * 4,
-        scratch_shapes=[pltpu.VMEM((512, 1024), BF16)],
+        out_specs=pl.BlockSpec(memory_space=pltpu.VMEM),
         compiler_params=pltpu.CompilerParams(vmem_limit_bytes=8 * 2**20),
-        cost_estimate=pl.CostEstimate(flops=512 * 1024 * 2048 * 2, bytes_accessed=7 * 2**20, transcendentals=0),
+        cost_estimate=pl.CostEstimate(flops=1024 * 512 * 1536 * 2, bytes_accessed=6 * 2**20, transcendentals=0),
         name="project",
     )(pos, *blocks, *weights)
 
 
-def sum_y_kernel(a, b, c, d, stay, leave):
-    total = ((a[...].astype(F32) + b[...].astype(F32)) + (c[...].astype(F32) + d[...].astype(F32))).astype(BF16)
-    stay[...] = total[:, :512]
-    leave[...] = total[:, 512:]
+def finish_kernel(pos_ref, part, low, high, w0, w1, *refs):
+    outs, total = refs[:4], refs[4]
+    x, y = pos_ref[0], pos_ref[1]
+    for half, block in enumerate((low, high)):
+        for w, weight in enumerate((w0, w1)):
+            spot = (pl.ds(half * 512, 512), pl.ds(w * 256, 256))
+            acc = part[spot].astype(F32)
+            for kind in range(2):
+                acc = acc + dot(block[:, pl.ds(kind * HEAD, HEAD)], weight[pl.ds(kind * 256, 256), head_cols(x, 2)], NT)
+            total[spot] = acc.astype(BF16)
+    for d, out in enumerate(outs):
+        out[...] = total[pl.ds(pl.multiple_of(lax.rem(y + d, 4) * 256, 256), 256), :]
+
+
+def finish(pos, part, low, high, weights):
+    return pl.pallas_call(
+        finish_kernel,
+        out_shape=(jax.ShapeDtypeStruct((256, 512), BF16),) * 4,
+        in_specs=[pl.BlockSpec(memory_space=pltpu.SMEM)] + [pl.BlockSpec(memory_space=pltpu.VMEM)] * 5,
+        out_specs=(pl.BlockSpec(memory_space=pltpu.VMEM),) * 4,
+        scratch_shapes=[pltpu.VMEM((1024, 512), BF16)],
+        compiler_params=pltpu.CompilerParams(vmem_limit_bytes=8 * 2**20),
+        cost_estimate=pl.CostEstimate(flops=1024 * 512 * 512 * 2, bytes_accessed=5 * 2**20, transcendentals=0),
+        name="finish",
+    )(pos, part, low, high, *weights)
+
+
+def sum_y_kernel(a, b, c, d, out):
+    out[...] = ((a[...].astype(F32) + b[...].astype(F32)) + (c[...].astype(F32) + d[...].astype(F32))).astype(BF16)
 
 
 def sum_y(terms):
     return pl.pallas_call(
         sum_y_kernel,
-        out_shape=(jax.ShapeDtypeStruct((128, 512), BF16),) * 2,
+        out_shape=jax.ShapeDtypeStruct((256, 512), BF16),
         in_specs=[pl.BlockSpec(memory_space=pltpu.VMEM)] * 4,
-        out_specs=(pl.BlockSpec(memory_space=pltpu.VMEM),) * 2,
+        out_specs=pl.BlockSpec(memory_space=pltpu.VMEM),
         compiler_params=pltpu.CompilerParams(vmem_limit_bytes=4 * 2**20),
-        cost_estimate=pl.CostEstimate(flops=2**20, bytes_accessed=5 * 2**19, transcendentals=0),
+        cost_estimate=pl.CostEstimate(flops=2**19, bytes_accessed=5 * 2**18, transcendentals=0),
         name="sum_y",
     )(*terms)
 
 
-def sum_pair_kernel(pos_ref, a, b, c, d, *refs):
-    outs, total = refs[:4], refs[4]
+def sum_pair_kernel(pos_ref, *refs):
+    terms, outs, total = refs[:5], refs[5:9], refs[9]
     h = pos_ref[5]
-    total[pl.ds(0, 128), :] = (a[...].astype(F32) + b[...].astype(F32)).astype(BF16)
-    total[pl.ds(128, 128), :] = (c[...].astype(F32) + d[...].astype(F32)).astype(BF16)
+    acc = terms[0][...].astype(F32)
+    for term in terms[1:]:
+        acc = acc + term[...].astype(F32)
+    total[...] = acc.astype(BF16)
     for d, out in enumerate(outs):
         out[...] = total[pl.ds(pl.multiple_of(lax.rem(h + d, 4) * 64, 64), 64), :]
 
@@ -199,11 +227,11 @@
     return pl.pallas_call(
         sum_pair_kernel,
         out_shape=(jax.ShapeDtypeStruct((64, 512), BF16),) * 4,
-        in_specs=[pl.BlockSpec(memory_space=pltpu.SMEM)] + [pl.BlockSpec(memory_space=pltpu.VMEM)] * 4,
+        in_specs=[pl.BlockSpec(memory_space=pltpu.SMEM)] + [pl.BlockSpec(memory_space=pltpu.VMEM)] * 5,
         out_specs=(pl.BlockSpec(memory_space=pltpu.VMEM),) * 4,
         scratch_shapes=[pltpu.VMEM((256, 512), BF16)],
-        compiler_params=pltpu.CompilerParams(vmem_limit_bytes=2 * 2**20),
-        cost_estimate=pl.CostEstimate(flops=2**18, bytes_accessed=2**19, transcendentals=0),
+        compiler_params=pltpu.CompilerParams(vmem_limit_bytes=4 * 2**20),
+        cost_estimate=pl.CostEstimate(flops=2**19, bytes_accessed=5 * 2**18, transcendentals=0),
         name="sum_pair",
     )(pos, *terms)
 
@@ -232,9 +260,7 @@
         for e in range(4):
             piece = lax.rem(h - e + 4, 4)
             for i in range(2):
-                from_y = lax.rem(y - d + 4, 4)
-                at = (lax.div(piece, 2) * 2 + lax.div(from_y, 2)) * 512 + lax.rem(from_y, 2) * 256
-                at += lax.rem(c + i, 2) * 128 + lax.rem(piece, 2) * 64
+                at = lax.rem(y - d + 4, 4) * 512 + lax.div(piece, 2) * 256 + lax.rem(c + i, 2) * 128 + lax.rem(piece, 2) * 64
                 value = got[e, :, pl.ds(i * 256, 256)]
                 out_ref[pl.ds(pl.multiple_of(at, 64), 64), :] = jnp.where(mine == 1, value, jnp.zeros_like(value))
 
@@ -282,20 +308,18 @@
 
     low, high = grads(0, parts, mine, other), grads(1, parts, mine, other)
     low_r, low_l = along_seq(low, dx=1), along_seq(low, dx=3)
-    low_r, low_l, high = tie((low_r, low_l, high))
-    low_o, high_l = along_seq(low_r, dx=1), along_seq(high, dx=3)
-    low_o, high_l, weight_z = tie((low_o, high_l, weight_z))
-    high_r, high_o = along_seq(high, dx=1), along_seq(high_l, dx=3)
-    weights = (weight, weight_c, weight_z, along_seq(weight_z, dc=1))
-
-    def sum_two(pieces):
-        stay, leave = sum_y([pieces[0]] + [along_section(pieces[d], dy=d) for d in (1, 2, 3)])
-        return [stay, along_seq(leave, dz=1)]
-
-    low_pieces = project(pos, (low, low_r, low_o, low_l), weights)
-    high_r, high_o, first = tie((high_r, high_o, low_pieces[0]))
-    high_pieces = project(pos, (high, high_r, high_o, high_l), weights)
-    terms = sum_two([first, *low_pieces[1:]]) + sum_two(high_pieces)
+    high_r, high_l = along_seq(high, dx=1), along_seq(high, dx=3)
+    low_r, low_l, high_r, high_l, weight_z = tie((low_r, low_l, high_r, high_l, weight_z))
+    low_o, high_o = along_seq(low_r, dx=1), along_seq(high_l, dx=3)
+    weight_zc = along_seq(weight_z, dc=1)
+    blocks = (low, high, low_r, high_r, low_l, high_l)
+    stay, leave = project(pos, blocks, (weight, weight_c)), project(pos, blocks, (weight_z, weight_zc))
+
+    def to_y(pieces):
+        return [pieces[0]] + [along_section(pieces[d], dy=d) for d in (1, 2, 3)]
+
+    leave = sum_y(to_y(finish(pos, leave, low_o, high_o, (weight_z, weight_zc))))
+    terms = to_y(finish(pos, stay, low_o, high_o, (weight, weight_c))) + [along_seq(leave, dz=1)]
 
     pieces = sum_pair(pos, terms)
     cols = sum_z([pieces[0]] + [along_section(pieces[d], dh=d) for d in (1, 2, 3)])

time: 171 us -> 162 us (0.947)
  waiting for transfers between devices: 75.1 us -> 59.6 us
  local copies, waits for them, and re-layouts: 8.29 us -> 12.1 us
    ppermute x14 -> x13, waiting for transfers between devices: 38.8 us -> 26.5 us  [along_seq(): return lax.ppermute(value, 'seq', seq_moves(dx, dz, dc))]
    unnamed x29 -> x39, local copies, waits for them, and re-layouts: 7.96 us -> 11.7 us
    ppermute x15, waiting for transfers between devices: 36.3 us -> 33.1 us  [along_section(): return lax.ppermute(value, 'section', section_moves(dh, dy))]
    pallas_call x4 -> x5, Pallas kernels: 8.97 us -> 11.1 us  [the longest x2 6.43 us: project(): pl.pallas_call(project_kernel, out_shape=jax.ShapeDtypeStruct((1024, 512)...]
    ppermute x14 -> x13, starting transfers between devices: 11.2 us -> 13.2 us  [along_seq(): return lax.ppermute(value, 'seq', seq_moves(dx, dz, dc))]
  transfers between devices with their start and end apart: 29 -> 28, of which waited for: 21 -> 19; matrix products, arithmetic and copies ran while one was open for 0% -> 0% of each run, Pallas kernels for 4% -> 10%
where the time goes in v2:
time: 162 us; the launch traced here: 161 us
  waiting for transfers between devices  59.6 us (37%)
  starting transfers between devices  44.9 us (28%)
  blocking collectives  25.1 us (15%)
  Pallas kernels  18.7 us (12%)
  local copies, waits for them, and re-layouts  12.1 us (7%)
    ppermute x15, waiting for transfers between devices, along_section(): return lax.ppermute(value, 'section', section_moves(dh, dy))  33.1 us
    ppermute x15, starting transfers between devices, along_section(): return lax.ppermute(value, 'section', section_moves(dh, dy))  31.7 us
    ppermute x13, waiting for transfers between devices, along_seq(): return lax.ppermute(value, 'seq', seq_moves(dx, dz, dc))  26.5 us
    all_to_all x1, blocking collectives, local(): mine = lax.all_to_all(rows, 'seq', 0, 0, axis_index_groups=groups)  25.1 us
    ppermute x13, starting transfers between devices, along_seq(): return lax.ppermute(value, 'seq', seq_moves(dx, dz, dc))  13.2 us
    unnamed x39, local copies, waits for them, and re-layouts  11.7 us
    pallas_call x2, Pallas kernels, project(): pl.pallas_call(project_kernel, out_shape=jax.ShapeDtypeStruct((1024, 512)...  6.43 us
    pallas_call x2, Pallas kernels, finish(): pl.pallas_call(finish_kernel, out_shape=(jax.ShapeDtypeStruct((256, 512),...  4.51 us
  transfers between devices with their start and end apart: 28, of which 19 were waited for; matrix products, arithmetic and copies ran while one was open for 0% of the time, Pallas kernels for 10%

profile of v2, /device:TPU:6, one launch (start us, length us, event | category | flops | bytes accessed | tf_op | source)
XLA Modules:
  0.0 161.4 jit_solution(10281246578255105473)
XLA Ops:
  4.2 25.1 %all_to_all.5.m_ref = bf16[8,384,256]{2,1,0:T(8,128)(2,1)S(1)} all-to-all(bf16[8,384,256]{2,1,0:T(8,128)(2,1)S(1)} %pack.1), channel_id=1, replica_groups={{0,2,4,6,8,10,12,14},{1,3,5,7,9,11,13,15},{16,18,20,22,24,26,28,30},{17..., dimensions={0} | all-to-all | bytes 3145728 | tf_op jit(solution)/shard_map/all_to_all | solution.py:295
  38.3 2.3 %collective-permute-start.2 = (bf16[512,512]{1,0:T(8,128)(2,1)S(1)}, bf16[512,512]{1,0:T(8,128)(2,1)}, u32[]{:S(2)}, u32[]{:S(2)}) collective-permute-start(bf16[512,512]{1,0:T(8,128)(2,1)S(1)} %grads.2.refs_0_), channel_id=1, source_target_pairs={{0,4},{1,5},{2,6},{3,7},{4,8},{5,9},{6,10},{7,11},{8,12},{9,13},{1... | collective-permute-start | bytes 1572872 | tf_op jit(solution)/shard_map/ppermute | solution.py:33
  42.0 3.2 %collective-permute-start.4 = (bf16[512,512]{1,0:T(8,128)(2,1)S(1)}, bf16[512,512]{1,0:T(8,128)(2,1)S(1)}, u32[]{:S(2)}, u32[]{:S(2)}) collective-permute-start(bf16[512,512]{1,0:T(8,128)(2,1)S(1)} %grads.3.refs_1_), channel_id=1, source_target_pairs={{0,4},{1,5},{2,6},{3,7},{4,8},{5,9},{6,10},{7,11},{8,12},{9,13},{1... | collective-permute-start | bytes 1572872 | tf_op jit(solution)/shard_map/ppermute | solution.py:33
  46.1 10.4 %collective-permute-done.6.refs_6_.w0 = bf16[512,1024]{1,0:T(8,128)(2,1)S(1)} collective-permute-done((bf16[512,1024]{1,0:T(8,128)(2,1)S(1)}, bf16[512,1024]{1,0:T(8,128)(2,1)S(1)}, u32[]{:S(2)}, u32[]{:S(2)}) %collective-permute-start.6) | collective-permute-done | bytes 1048608 | tf_op jit(solution)/shard_map/ppermute | solution.py:33
  57.2 6.7 %collective-permute-done.5.refs_5_ = bf16[512,512]{1,0:T(8,128)(2,1)} collective-permute-done((bf16[512,512]{1,0:T(8,128)(2,1)S(1)}, bf16[512,512]{1,0:T(8,128)(2,1)}, u32[]{:S(2)}, u32[]{:S(2)}) %collective-permute-start.5) | collective-permute-done | bytes 524320 | tf_op jit(solution)/shard_map/ppermute | solution.py:33
  65.5 2.8 %collective-permute-start.8 = (bf16[512,512]{1,0:T(8,128)(2,1)}, bf16[512,512]{1,0:T(8,128)(2,1)}, u32[]{:S(2)}, u32[]{:S(2)}) collective-permute-start(bf16[512,512]{1,0:T(8,128)(2,1)} %collective-permute-done.2.refs_2_), channel_id=1, source_target_pairs={{0,4},{1,5},{2,6},{3,7},{4,8},{5,9},{6,10},{7,11},{8,12},{9,13},{1... | collective-permute-start | bytes 1572872 | tf_op jit(solution)/shard_map/ppermute | solution.py:33
  73.2 3.4 %project.3.part = bf16[1024,512]{1,0:T(8,128)(2,1)S(1)} custom-call(s32[6]{0:T(128)S(1)} %stack.46.pos_ref, bf16[512,512]{1,0:T(8,128)(2,1)S(1)} %copy-done.3, bf16[512,512]{1,0:T(8,128)(2,1)S(1)} %copy-done.9, bf16[512,512]{1,0:T(8,128)(2,1)} %collective-permute-done.2.refs_2_, bf16[512,512]{1,0:T(8,128)(2,1)S(1)} %copy-done.12, ...), custom_call_target="tpu_custom_call" | custom-call | flops 1610612736 | bytes 6291456 | tf_op jit(solution)/shard_map/project/pallas_call | solution.py:161
  76.7 3.4 %collective-permute-done.8.low = bf16[512,512]{1,0:T(8,128)(2,1)} collective-permute-done((bf16[512,512]{1,0:T(8,128)(2,1)}, bf16[512,512]{1,0:T(8,128)(2,1)}, u32[]{:S(2)}, u32[]{:S(2)}) %collective-permute-start.8) | collective-permute-done | bytes 524320 | tf_op jit(solution)/shard_map/ppermute | solution.py:33
  80.1 3.4 %collective-permute-done.9.high = bf16[512,512]{1,0:T(8,128)(2,1)} collective-permute-done((bf16[512,512]{1,0:T(8,128)(2,1)}, bf16[512,512]{1,0:T(8,128)(2,1)}, u32[]{:S(2)}, u32[]{:S(2)}) %collective-permute-start.9) | collective-permute-done | bytes 524320 | tf_op jit(solution)/shard_map/ppermute | solution.py:33
  83.5 2.4 %finish.3 = (bf16[256,512]{1,0:T(8,128)(2,1)S(1)}, bf16[256,512]{1,0:T(8,128)(2,1)S(1)}, bf16[256,512]{1,0:T(8,128)(2,1)S(1)}, bf16[256,512]{1,0:T(8,128)(2,1)S(1)}) custom-call(s32[6]{0:T(128)S(1)} %stack.46.pos_ref, bf16[1024,512]{1,0:T(8,128)(2,1)S(1)} %project.3.part, bf16[512,512]{1,0:T(8,128)(2,1)} %collective-permute-done.8.low, ...), custom_call_target="tpu_custom_call" | custom-call | flops 536870912 | bytes 5242880 | tf_op jit(solution)/shard_map/finish/pallas_call | solution.py:187
  87.6 2.9 %collective-permute-start.15 = (bf16[256,512]{1,0:T(8,128)(2,1)S(1)}, bf16[256,512]{1,0:T(8,128)(2,1)S(1)}, u32[]{:S(2)}, u32[]{:S(2)}) collective-permute-start(bf16[256,512]{1,0:T(8,128)(2,1)S(1)} %get-tuple-element.41), channel_id=1, source_target_pairs={{0,32},{16,48},{32,0},{48,16},{64,96},{80,112},{96,64},{112,80},{1... | collective-permute-start | bytes 786440 | tf_op jit(solution)/shard_map/ppermute | solution.py:37
  91.8 3.0 %project.2.part = bf16[1024,512]{1,0:T(8,128)(2,1)S(1)} custom-call(s32[6]{0:T(128)S(1)} %stack.46.pos_ref, bf16[512,512]{1,0:T(8,128)(2,1)S(1)} %copy-done.4, bf16[512,512]{1,0:T(8,128)(2,1)S(1)} %copy-done.10, bf16[512,512]{1,0:T(8,128)(2,1)} %collective-permute-done.2.refs_2_, bf16[512,512]{1,0:T(8,128)(2,1)S(1)} %copy-done.12, ...), custom_call_target="tpu_custom_call" | custom-call | flops 1610612736 | bytes 6291456 | tf_op jit(solution)/shard_map/project/pallas_call | solution.py:161
  100.5 2.8 %collective-permute-done.15.c = bf16[256,512]{1,0:T(8,128)(2,1)S(1)} collective-permute-done((bf16[256,512]{1,0:T(8,128)(2,1)S(1)}, bf16[256,512]{1,0:T(8,128)(2,1)S(1)}, u32[]{:S(2)}, u32[]{:S(2)}) %collective-permute-start.15) | collective-permute-done | bytes 262176 | tf_op jit(solution)/shard_map/ppermute | solution.py:37
  105.3 3.6 %collective-permute-done.10.refs_1_ = bf16[256,512]{1,0:T(8,128)(2,1)S(1)} collective-permute-done((bf16[256,512]{1,0:T(8,128)(2,1)S(1)}, bf16[256,512]{1,0:T(8,128)(2,1)S(1)}, u32[]{:S(2)}, u32[]{:S(2)}) %collective-permute-start.10) | collective-permute-done | bytes 262176 | tf_op jit(solution)/shard_map/ppermute | solution.py:37
  108.9 3.5 %collective-permute-done.11.refs_2_ = bf16[256,512]{1,0:T(8,128)(2,1)S(1)} collective-permute-done((bf16[256,512]{1,0:T(8,128)(2,1)S(1)}, bf16[256,512]{1,0:T(8,128)(2,1)S(1)}, u32[]{:S(2)}, u32[]{:S(2)}) %collective-permute-start.11) | collective-permute-done | bytes 262176 | tf_op jit(solution)/shard_map/ppermute | solution.py:37
  113.3 3.3 %collective-permute-start.18 = (bf16[64,512]{1,0:T(8,128)(2,1)S(1)}, bf16[64,512]{1,0:T(8,128)(2,1)S(1)}, u32[]{:S(2)}, u32[]{:S(2)}) collective-permute-start(bf16[64,512]{1,0:T(8,128)(2,1)S(1)} %get-tuple-element.44), channel_id=1, source_target_pairs={{0,64},{16,80},{32,96},{48,112},{64,128},{80,144},{96,160},{112,17... | collective-permute-start | bytes 196616 | tf_op jit(solution)/shard_map/ppermute | solution.py:37
  116.6 4.5 %collective-permute-start.19 = (bf16[64,512]{1,0:T(8,128)(2,1)S(1)}, bf16[64,512]{1,0:T(8,128)(2,1)S(1)}, u32[]{:S(2)}, u32[]{:S(2)}) collective-permute-start(bf16[64,512]{1,0:T(8,128)(2,1)S(1)} %get-tuple-element.45), channel_id=1, source_target_pairs={{0,128},{16,144},{32,160},{48,176},{64,192},{80,208},{96,224},{112... | collective-permute-start | bytes 196616 | tf_op jit(solution)/shard_map/ppermute | solution.py:37
  121.1 2.7 %collective-permute-start.20 = (bf16[64,512]{1,0:T(8,128)(2,1)S(1)}, bf16[64,512]{1,0:T(8,128)(2,1)S(1)}, u32[]{:S(2)}, u32[]{:S(2)}) collective-permute-start(bf16[64,512]{1,0:T(8,128)(2,1)S(1)} %get-tuple-element.46), channel_id=1, source_target_pairs={{0,192},{16,208},{32,224},{48,240},{64,0},{80,16},{96,32},{112,48}... | collective-permute-start | bytes 196616 | tf_op jit(solution)/shard_map/ppermute | solution.py:37
  128.6 3.4 %collective-permute-start.24 = (bf16[64,512]{1,0:T(8,128)(2,1)S(1)}, bf16[64,512]{1,0:T(8,128)(2,1)S(1)}, u32[]{:S(2)}, u32[]{:S(2)}) collective-permute-start(bf16[64,512]{1,0:T(8,128)(2,1)S(1)} %constant_dynamic-update-slice_fusion), channel_id=1, source_target_pairs={{0,192},{16,208},{32,224},{48,240},{64,0},{80,16},{96,32},{112,48}... | collective-permute-start | bytes 196616 | tf_op jit(solution)/shard_map/ppermute | solution.py:37
  134.4 3.6 %collective-permute-done.24 = bf16[64,512]{1,0:T(8,128)(2,1)S(1)} collective-permute-done((bf16[64,512]{1,0:T(8,128)(2,1)S(1)}, bf16[64,512]{1,0:T(8,128)(2,1)S(1)}, u32[]{:S(2)}, u32[]{:S(2)}) %collective-permute-start.24) | collective-permute-done | bytes 65568 | tf_op jit(solution)/shard_map/ppermute | solution.py:37
  137.9 3.2 %collective-permute-done.23 = bf16[64,512]{1,0:T(8,128)(2,1)S(1)} collective-permute-done((bf16[64,512]{1,0:T(8,128)(2,1)S(1)}, bf16[64,512]{1,0:T(8,128)(2,1)S(1)}, u32[]{:S(2)}, u32[]{:S(2)}) %collective-permute-start.23) | collective-permute-done | bytes 65568 | tf_op jit(solution)/shard_map/ppermute | solution.py:37
  141.3 5.1 %collective-permute-start.27 = (bf16[4,64,512]{2,1,0:T(8,128)(2,1)S(1)}, bf16[4,64,512]{2,1,0:T(8,128)(2,1)S(1)}, u32[]{:S(2)}, u32[]{:S(2)}) collective-permute-start(bf16[4,64,512]{2,1,0:T(8,128)(2,1)S(1)} %pad_maximum_fusion.2.g0), channel_id=1, source_target_pairs={{0,48},{16,0},{32,16},{48,32},{64,112},{80,64},{96,80},{112,96},{1... | collective-permute-start | bytes 786440 | tf_op jit(solution)/shard_map/ppermute | solution.py:37
  147.3 8.7 %collective-permute-done.27.g3 = bf16[4,64,512]{2,1,0:T(8,128)(2,1)S(1)} collective-permute-done((bf16[4,64,512]{2,1,0:T(8,128)(2,1)S(1)}, bf16[4,64,512]{2,1,0:T(8,128)(2,1)S(1)}, u32[]{:S(2)}, u32[]{:S(2)}) %collective-permute-start.27) | collective-permute-done | bytes 262176 | tf_op jit(solution)/shard_map/ppermute | solution.py:37
  156.9 2.7 %collective-permute-done.25.g1 = bf16[4,64,512]{2,1,0:T(8,128)(2,1)S(1)} collective-permute-done((bf16[4,64,512]{2,1,0:T(8,128)(2,1)S(1)}, bf16[4,64,512]{2,1,0:T(8,128)(2,1)S(1)}, u32[]{:S(2)}, u32[]{:S(2)}) %collective-permute-start.25) | collective-permute-done | bytes 262176 | tf_op jit(solution)/shard_map/ppermute | solution.py:37
  (91 shorter events, 44.1 us)
Async XLA Ops:
  30.8 25.6 %collective-permute-start.6 = (bf16[512,1024]{1,0:T(8,128)(2,1)S(1)}, bf16[512,1024]{1,0:T(8,128)(2,1)S(1)}, u32[]{:S(2)}, u32[]{:S(2)}) collective-permute-start(bf16[512,1024]{1,0:T(8,128)(2,1)S(1)} %pad_maximum_fusion), channel_id=1, source_target_pairs={{0,2},{1,3},{2,0},{3,1},{4,6},{5,7},{6,4},{7,5},{8,10},{9,11},{10,... | collective-permute-start | bytes 3145736 | tf_op jit(solution)/shard_map/ppermute | solution.py:33
  37.3 19.1 %collective-permute-start.3 = (bf16[512,512]{1,0:T(8,128)(2,1)S(1)}, bf16[512,512]{1,0:T(8,128)(2,1)S(1)}, u32[]{:S(2)}, u32[]{:S(2)}) collective-permute-start(bf16[512,512]{1,0:T(8,128)(2,1)S(1)} %grads.2.refs_0_), channel_id=1, source_target_pairs={{0,12},{1,13},{2,14},{3,15},{4,0},{5,1},{6,2},{7,3},{8,4},{9,5},{1... | collective-permute-start | bytes 1572872 | tf_op jit(solution)/shard_map/ppermute | solution.py:33
  38.3 18.9 %collective-permute-start.2 = (bf16[512,512]{1,0:T(8,128)(2,1)S(1)}, bf16[512,512]{1,0:T(8,128)(2,1)}, u32[]{:S(2)}, u32[]{:S(2)}) collective-permute-start(bf16[512,512]{1,0:T(8,128)(2,1)S(1)} %grads.2.refs_0_), channel_id=1, source_target_pairs={{0,4},{1,5},{2,6},{3,7},{4,8},{5,9},{6,10},{7,11},{8,12},{9,13},{1... | collective-permute-start | bytes 1572872 | tf_op jit(solution)/shard_map/ppermute | solution.py:33
  42.0 22.0 %collective-permute-start.5 = (bf16[512,512]{1,0:T(8,128)(2,1)S(1)}, bf16[512,512]{1,0:T(8,128)(2,1)}, u32[]{:S(2)}, u32[]{:S(2)}) collective-permute-start(bf16[512,512]{1,0:T(8,128)(2,1)S(1)} %grads.3.refs_1_), channel_id=1, source_target_pairs={{0,12},{1,13},{2,14},{3,15},{4,0},{5,1},{6,2},{7,3},{8,4},{9,5},{1... | collective-permute-start | bytes 1572872 | tf_op jit(solution)/shard_map/ppermute | solution.py:33
  42.0 22.0 %collective-permute-start.4 = (bf16[512,512]{1,0:T(8,128)(2,1)S(1)}, bf16[512,512]{1,0:T(8,128)(2,1)S(1)}, u32[]{:S(2)}, u32[]{:S(2)}) collective-permute-start(bf16[512,512]{1,0:T(8,128)(2,1)S(1)} %grads.3.refs_1_), channel_id=1, source_target_pairs={{0,4},{1,5},{2,6},{3,7},{4,8},{5,9},{6,10},{7,11},{8,12},{9,13},{1... | collective-permute-start | bytes 1572872 | tf_op jit(solution)/shard_map/ppermute | solution.py:33
  64.9 26.9 %collective-permute-start.7 = (bf16[512,1024]{1,0:T(8,128)(2,1)S(1)}, bf16[512,1024]{1,0:T(8,128)(2,1)S(1)}, u32[]{:S(2)}, u32[]{:S(2)}) collective-permute-start(bf16[512,1024]{1,0:T(8,128)(2,1)S(1)} %pad_maximum_fusion.1.refs_6_.w0), channel_id=1, source_target_pairs={{0,1},{1,0},{2,3},{3,2},{4,5},{5,4},{6,7},{7,6},{8,9},{9,8},{10,11... | collective-permute-start | bytes 3145736 | tf_op jit(solution)/shard_map/ppermute | solution.py:33
  65.5 14.6 %collective-permute-start.8 = (bf16[512,512]{1,0:T(8,128)(2,1)}, bf16[512,512]{1,0:T(8,128)(2,1)}, u32[]{:S(2)}, u32[]{:S(2)}) collective-permute-start(bf16[512,512]{1,0:T(8,128)(2,1)} %collective-permute-done.2.refs_2_), channel_id=1, source_target_pairs={{0,4},{1,5},{2,6},{3,7},{4,8},{5,9},{6,10},{7,11},{8,12},{9,13},{1... | collective-permute-start | bytes 1572872 | tf_op jit(solution)/shard_map/ppermute | solution.py:33
  68.3 15.2 %collective-permute-start.9 = (bf16[512,512]{1,0:T(8,128)(2,1)}, bf16[512,512]{1,0:T(8,128)(2,1)}, u32[]{:S(2)}, u32[]{:S(2)}) collective-permute-start(bf16[512,512]{1,0:T(8,128)(2,1)} %collective-permute-done.5.refs_5_), channel_id=1, source_target_pairs={{0,12},{1,13},{2,14},{3,15},{4,0},{5,1},{6,2},{7,3},{8,4},{9,5},{1... | collective-permute-start | bytes 1572872 | tf_op jit(solution)/shard_map/ppermute | solution.py:33
  85.9 12.6 %collective-permute-start.14 = (bf16[256,512]{1,0:T(8,128)(2,1)S(1)}, bf16[256,512]{1,0:T(8,128)(2,1)S(1)}, u32[]{:S(2)}, u32[]{:S(2)}) collective-permute-start(bf16[256,512]{1,0:T(8,128)(2,1)S(1)} %get-tuple-element.40), channel_id=1, source_target_pairs={{0,16},{16,32},{32,48},{48,0},{64,80},{80,96},{96,112},{112,64},{1... | collective-permute-start | bytes 786440 | tf_op jit(solution)/shard_map/ppermute | solution.py:37
  87.6 15.7 %collective-permute-start.15 = (bf16[256,512]{1,0:T(8,128)(2,1)S(1)}, bf16[256,512]{1,0:T(8,128)(2,1)S(1)}, u32[]{:S(2)}, u32[]{:S(2)}) collective-permute-start(bf16[256,512]{1,0:T(8,128)(2,1)S(1)} %get-tuple-element.41), channel_id=1, source_target_pairs={{0,32},{16,48},{32,0},{48,16},{64,96},{80,112},{96,64},{112,80},{1... | collective-permute-start | bytes 786440 | tf_op jit(solution)/shard_map/ppermute | solution.py:37
  90.5 13.4 %collective-permute-start.16 = (bf16[256,512]{1,0:T(8,128)(2,1)S(1)}, bf16[256,512]{1,0:T(8,128)(2,1)S(1)}, u32[]{:S(2)}, u32[]{:S(2)}) collective-permute-start(bf16[256,512]{1,0:T(8,128)(2,1)S(1)} %get-tuple-element.42), channel_id=1, source_target_pairs={{0,48},{16,0},{32,16},{48,32},{64,112},{80,64},{96,80},{112,96},{1... | collective-permute-start | bytes 786440 | tf_op jit(solution)/shard_map/ppermute | solution.py:37
  97.0 11.9 %collective-permute-start.10 = (bf16[256,512]{1,0:T(8,128)(2,1)S(1)}, bf16[256,512]{1,0:T(8,128)(2,1)S(1)}, u32[]{:S(2)}, u32[]{:S(2)}) collective-permute-start(bf16[256,512]{1,0:T(8,128)(2,1)S(1)} %get-tuple-element.35), channel_id=1, source_target_pairs={{0,16},{16,32},{32,48},{48,0},{64,80},{80,96},{96,112},{112,64},{1... | collective-permute-start | bytes 786440 | tf_op jit(solution)/shard_map/ppermute | solution.py:37
  97.7 14.7 %collective-permute-start.11 = (bf16[256,512]{1,0:T(8,128)(2,1)S(1)}, bf16[256,512]{1,0:T(8,128)(2,1)S(1)}, u32[]{:S(2)}, u32[]{:S(2)}) collective-permute-start(bf16[256,512]{1,0:T(8,128)(2,1)S(1)} %get-tuple-element.36), channel_id=1, source_target_pairs={{0,32},{16,48},{32,0},{48,16},{64,96},{80,112},{96,64},{112,80},{1... | collective-permute-start | bytes 786440 | tf_op jit(solution)/shard_map/ppermute | solution.py:37
  98.5 13.9 %collective-permute-start.12 = (bf16[256,512]{1,0:T(8,128)(2,1)S(1)}, bf16[256,512]{1,0:T(8,128)(2,1)S(1)}, u32[]{:S(2)}, u32[]{:S(2)}) collective-permute-start(bf16[256,512]{1,0:T(8,128)(2,1)S(1)} %get-tuple-element.37), channel_id=1, source_target_pairs={{0,48},{16,0},{32,16},{48,32},{64,112},{80,64},{96,80},{112,96},{1... | collective-permute-start | bytes 786440 | tf_op jit(solution)/shard_map/ppermute | solution.py:37
  104.0 8.4 %collective-permute-start.17 = (bf16[256,512]{1,0:T(8,128)(2,1)S(1)}, bf16[256,512]{1,0:T(8,128)(2,1)S(1)}, u32[]{:S(2)}, u32[]{:S(2)}) collective-permute-start(bf16[256,512]{1,0:T(8,128)(2,1)S(1)} %sum_y.1), channel_id=1, source_target_pairs={{0,2},{1,3},{2,0},{3,1},{4,6},{5,7},{6,4},{7,5},{8,10},{9,11},{10,... | collective-permute-start | bytes 786440 | tf_op jit(solution)/shard_map/ppermute | solution.py:33
  113.3 10.5 %collective-permute-start.18 = (bf16[64,512]{1,0:T(8,128)(2,1)S(1)}, bf16[64,512]{1,0:T(8,128)(2,1)S(1)}, u32[]{:S(2)}, u32[]{:S(2)}) collective-permute-start(bf16[64,512]{1,0:T(8,128)(2,1)S(1)} %get-tuple-element.44), channel_id=1, source_target_pairs={{0,64},{16,80},{32,96},{48,112},{64,128},{80,144},{96,160},{112,17... | collective-permute-start | bytes 196616 | tf_op jit(solution)/shard_map/ppermute | solution.py:37
  116.6 8.7 %collective-permute-start.19 = (bf16[64,512]{1,0:T(8,128)(2,1)S(1)}, bf16[64,512]{1,0:T(8,128)(2,1)S(1)}, u32[]{:S(2)}, u32[]{:S(2)}) collective-permute-start(bf16[64,512]{1,0:T(8,128)(2,1)S(1)} %get-tuple-element.45), channel_id=1, source_target_pairs={{0,128},{16,144},{32,160},{48,176},{64,192},{80,208},{96,224},{112... | collective-permute-start | bytes 196616 | tf_op jit(solution)/shard_map/ppermute | solution.py:37
  121.1 5.9 %collective-permute-start.20 = (bf16[64,512]{1,0:T(8,128)(2,1)S(1)}, bf16[64,512]{1,0:T(8,128)(2,1)S(1)}, u32[]{:S(2)}, u32[]{:S(2)}) collective-permute-start(bf16[64,512]{1,0:T(8,128)(2,1)S(1)} %get-tuple-element.46), channel_id=1, source_target_pairs={{0,192},{16,208},{32,224},{48,240},{64,0},{80,16},{96,32},{112,48}... | collective-permute-start | bytes 196616 | tf_op jit(solution)/shard_map/ppermute | solution.py:37
  128.6 9.3 %collective-permute-start.24 = (bf16[64,512]{1,0:T(8,128)(2,1)S(1)}, bf16[64,512]{1,0:T(8,128)(2,1)S(1)}, u32[]{:S(2)}, u32[]{:S(2)}) collective-permute-start(bf16[64,512]{1,0:T(8,128)(2,1)S(1)} %constant_dynamic-update-slice_fusion), channel_id=1, source_target_pairs={{0,192},{16,208},{32,224},{48,240},{64,0},{80,16},{96,32},{112,48}... | collective-permute-start | bytes 196616 | tf_op jit(solution)/shard_map/ppermute | solution.py:37
  132.0 9.1 %collective-permute-start.23 = (bf16[64,512]{1,0:T(8,128)(2,1)S(1)}, bf16[64,512]{1,0:T(8,128)(2,1)S(1)}, u32[]{:S(2)}, u32[]{:S(2)}) collective-permute-start(bf16[64,512]{1,0:T(8,128)(2,1)S(1)} %constant_dynamic-update-slice_fusion), channel_id=1, source_target_pairs={{0,128},{16,144},{32,160},{48,176},{64,192},{80,208},{96,224},{112... | collective-permute-start | bytes 196616 | tf_op jit(solution)/shard_map/ppermute | solution.py:37
  133.6 7.7 %collective-permute-start.22 = (bf16[64,512]{1,0:T(8,128)(2,1)S(1)}, bf16[64,512]{1,0:T(8,128)(2,1)S(1)}, u32[]{:S(2)}, u32[]{:S(2)}) collective-permute-start(bf16[64,512]{1,0:T(8,128)(2,1)S(1)} %constant_dynamic-update-slice_fusion), channel_id=1, source_target_pairs={{0,64},{16,80},{32,96},{48,112},{64,128},{80,144},{96,160},{112,17... | collective-permute-start | bytes 196616 | tf_op jit(solution)/shard_map/ppermute | solution.py:37
  141.3 14.7 %collective-permute-start.27 = (bf16[4,64,512]{2,1,0:T(8,128)(2,1)S(1)}, bf16[4,64,512]{2,1,0:T(8,128)(2,1)S(1)}, u32[]{:S(2)}, u32[]{:S(2)}) collective-permute-start(bf16[4,64,512]{2,1,0:T(8,128)(2,1)S(1)} %pad_maximum_fusion.2.g0), channel_id=1, source_target_pairs={{0,48},{16,0},{32,16},{48,32},{64,112},{80,64},{96,80},{112,96},{1... | collective-permute-start | bytes 786440 | tf_op jit(solution)/shard_map/ppermute | solution.py:37
  146.3 10.6 %collective-permute-start.26 = (bf16[4,64,512]{2,1,0:T(8,128)(2,1)S(1)}, bf16[4,64,512]{2,1,0:T(8,128)(2,1)S(1)}, u32[]{:S(2)}, u32[]{:S(2)}) collective-permute-start(bf16[4,64,512]{2,1,0:T(8,128)(2,1)S(1)} %pad_maximum_fusion.2.g0), channel_id=1, source_target_pairs={{0,32},{16,48},{32,0},{48,16},{64,96},{80,112},{96,64},{112,80},{1... | collective-permute-start | bytes 786440 | tf_op jit(solution)/shard_map/ppermute | solution.py:37
  147.2 12.5 %collective-permute-start.25 = (bf16[4,64,512]{2,1,0:T(8,128)(2,1)S(1)}, bf16[4,64,512]{2,1,0:T(8,128)(2,1)S(1)}, u32[]{:S(2)}, u32[]{:S(2)}) collective-permute-start(bf16[4,64,512]{2,1,0:T(8,128)(2,1)S(1)} %pad_maximum_fusion.2.g0), channel_id=1, source_target_pairs={{0,16},{16,32},{32,48},{48,0},{64,80},{80,96},{96,112},{112,64},{1... | collective-permute-start | bytes 786440 | tf_op jit(solution)/shard_map/ppermute | solution.py:37
  (23 other events, 125.3 us)

commit v3 on v2

--- a/solution.py
+++ b/solution.py
@@ -46,25 +46,21 @@
     return lax.dot_general(a, b, dims, preferred_element_type=F32)
 
 
-def pack_kernel(q_ref, g_ref, k_ref, v_ref, out_ref):
+def pack_kernel(rows_ref, out_ref):
     for to in range(8):
-        cols = pl.ds(((to % 2) * 4 + to // 2) * HEAD, HEAD)
-        out_ref[to, pl.ds(0, 64), :] = q_ref[:, cols]
-        out_ref[to, pl.ds(64, 64), :] = g_ref[:, cols]
-        out_ref[to, pl.ds(128, 128), :] = k_ref[:, cols]
-        out_ref[to, pl.ds(256, 128), :] = v_ref[:, cols]
-
-
-def pack(q, g, k, v):
+        out_ref[to] = rows_ref[:, pl.ds(((to % 2) * 4 + to // 2) * HEAD, HEAD)]
+
+
+def pack(rows):
     return pl.pallas_call(
         pack_kernel,
         out_shape=jax.ShapeDtypeStruct((8, 384, HEAD), BF16),
-        in_specs=[pl.BlockSpec(memory_space=pltpu.VMEM)] * 4,
+        in_specs=[pl.BlockSpec(memory_space=pltpu.VMEM)],
         out_specs=pl.BlockSpec(memory_space=pltpu.VMEM),
         compiler_params=pltpu.CompilerParams(vmem_limit_bytes=4 * 2**20),
         cost_estimate=pl.CostEstimate(flops=0, bytes_accessed=2**22, transcendentals=0),
         name="pack",
-    )(q, g, k, v)
+    )(rows)
 
 
 def query_quarter(mine, other, j, first):
@@ -290,11 +286,14 @@
     pos = jnp.stack([x, y, z, c, (section == owner[0]).astype(jnp.int32), h]).astype(jnp.int32)
 
     tie = lax.optimization_barrier
-    rows = pack(q, g, k, v)
+    rows = pack(jnp.concatenate([q, g, k, v], axis=0))
     groups = [[xx * 4 + zz * 2 + cc for xx in range(4) for zz in range(2)] for cc in range(2)]
     mine = lax.all_to_all(rows, "seq", 0, 0, axis_index_groups=groups)
-    mine, kw, vw = tie((mine, kw, vw))
     other = along_seq(mine[:, :128], dc=1)
+
+    own = stats(mine, other)
+    own, kw, vw = tie((own, kw, vw))
+    parts = [own, along_seq(own, dc=1)]
 
     def half(matrix, at):
         return lax.dynamic_slice(matrix, (jnp.int32(0), at * 1024), (256, 1024))
@@ -302,9 +301,6 @@
     weight = jnp.concatenate([half(kw, z), half(vw, z)], axis=0)
     weight_z = along_seq(jnp.concatenate([half(kw, 1 - z), half(vw, 1 - z)], axis=0), dz=1)
     weight_c = along_seq(weight, dc=1)
-
-    own = stats(mine, other)
-    parts = [own, along_seq(own, dc=1)]
 
     low, high = grads(0, parts, mine, other), grads(1, parts, mine, other)
     low_r, low_l = along_seq(low, dx=1), along_seq(low, dx=3)

time: 162 us -> 160 us (0.988); the launches traced: 161 us -> 157 us
  local copies, waits for them, and re-layouts: 12.1 us -> 6.98 us
  starting transfers between devices: 44.9 us -> 43.2 us
    unnamed x39 -> x31, local copies, waits for them, and re-layouts: 11.7 us -> 6.62 us
    ppermute x13, waiting for transfers between devices: 26.5 us -> 28.1 us  [along_seq(): return lax.ppermute(value, 'seq', seq_moves(dx, dz, dc))]
  transfers between devices with their start and end apart: 28 -> 28, of which waited for: 19 -> 18; matrix products, arithmetic and copies ran while one was open for 0% -> 0% of each run, Pallas kernels for 10% -> 9%
where the time goes in v3:
time: 160 us; the launch traced here: 157 us
  waiting for transfers between devices  60.9 us (38%)
  starting transfers between devices  43.2 us (27%)
  blocking collectives  25 us (16%)
  Pallas kernels  18.6 us (12%)
  local copies, waits for them, and re-layouts  6.98 us (4%)
  other arithmetic  1.62 us (1%)
    ppermute x15, waiting for transfers between devices, along_section(): return lax.ppermute(value, 'section', section_moves(dh, dy))  32.7 us
    ppermute x15, starting transfers between devices, along_section(): return lax.ppermute(value, 'section', section_moves(dh, dy))  30.6 us
    ppermute x13, waiting for transfers between devices, along_seq(): return lax.ppermute(value, 'seq', seq_moves(dx, dz, dc))  28.1 us
    all_to_all x1, blocking collectives, local(): mine = lax.all_to_all(rows, 'seq', 0, 0, axis_index_groups=groups)  25 us
    ppermute x13, starting transfers between devices, along_seq(): return lax.ppermute(value, 'seq', seq_moves(dx, dz, dc))  12.7 us
    unnamed x31, local copies, waits for them, and re-layouts  6.62 us
    pallas_call x2, Pallas kernels, project(): pl.pallas_call(project_kernel, out_shape=jax.ShapeDtypeStruct((1024, 512)...  6.44 us
    pallas_call x2, Pallas kernels, finish(): pl.pallas_call(finish_kernel, out_shape=(jax.ShapeDtypeStruct((256, 512),...  4.52 us
  transfers between devices with their start and end apart: 28, of which 18 were waited for; matrix products, arithmetic and copies ran while one was open for 0% of the time, Pallas kernels for 9%

profile of v3, /device:TPU:6, one launch (start us, length us, event | category | flops | bytes accessed | tf_op | source)
XLA Modules:
  0.0 157.2 jit_solution(11346379828750162569)
XLA Ops:
  1.6 25.0 %all_to_all.5.m_ref = bf16[8,384,256]{2,1,0:T(8,128)(2,1)S(1)} all-to-all(bf16[8,384,256]{2,1,0:T(8,128)(2,1)S(1)} %pack.1), channel_id=1, replica_groups={{0,2,4,6,8,10,12,14},{1,3,5,7,9,11,13,15},{16,18,20,22,24,26,28,30},{17..., dimensions={0} | all-to-all | bytes 3145728 | tf_op jit(solution)/shard_map/all_to_all | solution.py:291
  28.6 2.2 %stats.1.s0 = f32[8,1024]{1,0:T(8,128)S(1)} custom-call(bf16[8,384,256]{2,1,0:T(8,128)(2,1)S(1)} %all_to_all.5.m_ref, bf16[8,128,256]{2,1,0:T(8,128)(2,1)S(1)} %collective-permute-done.o_ref), custom_call_target="tpu_custom_call" | custom-call | flops 1000000000 | bytes 4194304 | tf_op jit(solution)/shard_map/stats/pallas_call | solution.py:90
  35.1 3.2 %collective-permute-start.2 = (bf16[512,512]{1,0:T(8,128)(2,1)S(1)}, bf16[512,512]{1,0:T(8,128)(2,1)}, u32[]{:S(2)}, u32[]{:S(2)}) collective-permute-start(bf16[512,512]{1,0:T(8,128)(2,1)S(1)} %grads.2.refs_0_), channel_id=1, source_target_pairs={{0,4},{1,5},{2,6},{3,7},{4,8},{5,9},{6,10},{7,11},{8,12},{9,13},{1... | collective-permute-start | bytes 1572872 | tf_op jit(solution)/shard_map/ppermute | solution.py:33
  39.7 3.2 %collective-permute-start.4 = (bf16[512,512]{1,0:T(8,128)(2,1)S(1)}, bf16[512,512]{1,0:T(8,128)(2,1)S(1)}, u32[]{:S(2)}, u32[]{:S(2)}) collective-permute-start(bf16[512,512]{1,0:T(8,128)(2,1)S(1)} %grads.3.refs_1_), channel_id=1, source_target_pairs={{0,4},{1,5},{2,6},{3,7},{4,8},{5,9},{6,10},{7,11},{8,12},{9,13},{1... | collective-permute-start | bytes 1572872 | tf_op jit(solution)/shard_map/ppermute | solution.py:33
  43.7 7.3 %collective-permute-done.3.refs_4_ = bf16[512,512]{1,0:T(8,128)(2,1)S(1)} collective-permute-done((bf16[512,512]{1,0:T(8,128)(2,1)S(1)}, bf16[512,512]{1,0:T(8,128)(2,1)S(1)}, u32[]{:S(2)}, u32[]{:S(2)}) %collective-permute-start.3) | collective-permute-done | bytes 524320 | tf_op jit(solution)/shard_map/ppermute | solution.py:33
  51.8 9.8 %collective-permute-done.5.refs_5_ = bf16[512,512]{1,0:T(8,128)(2,1)} collective-permute-done((bf16[512,512]{1,0:T(8,128)(2,1)S(1)}, bf16[512,512]{1,0:T(8,128)(2,1)}, u32[]{:S(2)}, u32[]{:S(2)}) %collective-permute-start.5) | collective-permute-done | bytes 524320 | tf_op jit(solution)/shard_map/ppermute | solution.py:33
  63.1 2.8 %collective-permute-start.8 = (bf16[512,512]{1,0:T(8,128)(2,1)}, bf16[512,512]{1,0:T(8,128)(2,1)}, u32[]{:S(2)}, u32[]{:S(2)}) collective-permute-start(bf16[512,512]{1,0:T(8,128)(2,1)} %collective-permute-done.2.refs_2_), channel_id=1, source_target_pairs={{0,4},{1,5},{2,6},{3,7},{4,8},{5,9},{6,10},{7,11},{8,12},{9,13},{1... | collective-permute-start | bytes 1572872 | tf_op jit(solution)/shard_map/ppermute | solution.py:33
  70.9 3.4 %project.3.part = bf16[1024,512]{1,0:T(8,128)(2,1)S(1)} custom-call(s32[6]{0:T(128)S(1)} %stack.46.pos_ref, bf16[512,512]{1,0:T(8,128)(2,1)S(1)} %copy-done.3, bf16[512,512]{1,0:T(8,128)(2,1)S(1)} %copy-done.9, bf16[512,512]{1,0:T(8,128)(2,1)} %collective-permute-done.2.refs_2_, bf16[512,512]{1,0:T(8,128)(2,1)S(1)} %copy-done.12, ...), custom_call_target="tpu_custom_call" | custom-call | flops 1610612736 | bytes 6291456 | tf_op jit(solution)/shard_map/project/pallas_call | solution.py:157
  74.3 3.4 %collective-permute-done.8.low = bf16[512,512]{1,0:T(8,128)(2,1)} collective-permute-done((bf16[512,512]{1,0:T(8,128)(2,1)}, bf16[512,512]{1,0:T(8,128)(2,1)}, u32[]{:S(2)}, u32[]{:S(2)}) %collective-permute-start.8) | collective-permute-done | bytes 524320 | tf_op jit(solution)/shard_map/ppermute | solution.py:33
  77.7 3.4 %collective-permute-done.9.high = bf16[512,512]{1,0:T(8,128)(2,1)} collective-permute-done((bf16[512,512]{1,0:T(8,128)(2,1)}, bf16[512,512]{1,0:T(8,128)(2,1)}, u32[]{:S(2)}, u32[]{:S(2)}) %collective-permute-start.9) | collective-permute-done | bytes 524320 | tf_op jit(solution)/shard_map/ppermute | solution.py:33
  81.1 2.4 %finish.3 = (bf16[256,512]{1,0:T(8,128)(2,1)S(1)}, bf16[256,512]{1,0:T(8,128)(2,1)S(1)}, bf16[256,512]{1,0:T(8,128)(2,1)S(1)}, bf16[256,512]{1,0:T(8,128)(2,1)S(1)}) custom-call(s32[6]{0:T(128)S(1)} %stack.46.pos_ref, bf16[1024,512]{1,0:T(8,128)(2,1)S(1)} %project.3.part, bf16[512,512]{1,0:T(8,128)(2,1)} %collective-permute-done.8.low, ...), custom_call_target="tpu_custom_call" | custom-call | flops 536870912 | bytes 5242880 | tf_op jit(solution)/shard_map/finish/pallas_call | solution.py:183
  85.2 2.9 %collective-permute-start.15 = (bf16[256,512]{1,0:T(8,128)(2,1)S(1)}, bf16[256,512]{1,0:T(8,128)(2,1)S(1)}, u32[]{:S(2)}, u32[]{:S(2)}) collective-permute-start(bf16[256,512]{1,0:T(8,128)(2,1)S(1)} %get-tuple-element.41), channel_id=1, source_target_pairs={{0,32},{16,48},{32,0},{48,16},{64,96},{80,112},{96,64},{112,80},{1... | collective-permute-start | bytes 786440 | tf_op jit(solution)/shard_map/ppermute | solution.py:37
  89.5 3.0 %project.2.part = bf16[1024,512]{1,0:T(8,128)(2,1)S(1)} custom-call(s32[6]{0:T(128)S(1)} %stack.46.pos_ref, bf16[512,512]{1,0:T(8,128)(2,1)S(1)} %copy-done.4, bf16[512,512]{1,0:T(8,128)(2,1)S(1)} %copy-done.10, bf16[512,512]{1,0:T(8,128)(2,1)} %collective-permute-done.2.refs_2_, bf16[512,512]{1,0:T(8,128)(2,1)S(1)} %copy-done.12, ...), custom_call_target="tpu_custom_call" | custom-call | flops 1610612736 | bytes 6291456 | tf_op jit(solution)/shard_map/project/pallas_call | solution.py:157
  98.1 2.8 %collective-permute-done.15.c = bf16[256,512]{1,0:T(8,128)(2,1)S(1)} collective-permute-done((bf16[256,512]{1,0:T(8,128)(2,1)S(1)}, bf16[256,512]{1,0:T(8,128)(2,1)S(1)}, u32[]{:S(2)}, u32[]{:S(2)}) %collective-permute-start.15) | collective-permute-done | bytes 262176 | tf_op jit(solution)/shard_map/ppermute | solution.py:37
  102.6 4.0 %collective-permute-done.10.refs_1_ = bf16[256,512]{1,0:T(8,128)(2,1)S(1)} collective-permute-done((bf16[256,512]{1,0:T(8,128)(2,1)S(1)}, bf16[256,512]{1,0:T(8,128)(2,1)S(1)}, u32[]{:S(2)}, u32[]{:S(2)}) %collective-permute-start.10) | collective-permute-done | bytes 262176 | tf_op jit(solution)/shard_map/ppermute | solution.py:37
  106.6 3.5 %collective-permute-done.11.refs_2_ = bf16[256,512]{1,0:T(8,128)(2,1)S(1)} collective-permute-done((bf16[256,512]{1,0:T(8,128)(2,1)S(1)}, bf16[256,512]{1,0:T(8,128)(2,1)S(1)}, u32[]{:S(2)}, u32[]{:S(2)}) %collective-permute-start.11) | collective-permute-done | bytes 262176 | tf_op jit(solution)/shard_map/ppermute | solution.py:37
  110.9 3.3 %collective-permute-start.18 = (bf16[64,512]{1,0:T(8,128)(2,1)S(1)}, bf16[64,512]{1,0:T(8,128)(2,1)S(1)}, u32[]{:S(2)}, u32[]{:S(2)}) collective-permute-start(bf16[64,512]{1,0:T(8,128)(2,1)S(1)} %get-tuple-element.44), channel_id=1, source_target_pairs={{0,64},{16,80},{32,96},{48,112},{64,128},{80,144},{96,160},{112,17... | collective-permute-start | bytes 196616 | tf_op jit(solution)/shard_map/ppermute | solution.py:37
  114.3 4.5 %collective-permute-start.19 = (bf16[64,512]{1,0:T(8,128)(2,1)S(1)}, bf16[64,512]{1,0:T(8,128)(2,1)S(1)}, u32[]{:S(2)}, u32[]{:S(2)}) collective-permute-start(bf16[64,512]{1,0:T(8,128)(2,1)S(1)} %get-tuple-element.45), channel_id=1, source_target_pairs={{0,128},{16,144},{32,160},{48,176},{64,192},{80,208},{96,224},{112... | collective-permute-start | bytes 196616 | tf_op jit(solution)/shard_map/ppermute | solution.py:37
  118.8 2.7 %collective-permute-start.20 = (bf16[64,512]{1,0:T(8,128)(2,1)S(1)}, bf16[64,512]{1,0:T(8,128)(2,1)S(1)}, u32[]{:S(2)}, u32[]{:S(2)}) collective-permute-start(bf16[64,512]{1,0:T(8,128)(2,1)S(1)} %get-tuple-element.46), channel_id=1, source_target_pairs={{0,192},{16,208},{32,224},{48,240},{64,0},{80,16},{96,32},{112,48}... | collective-permute-start | bytes 196616 | tf_op jit(solution)/shard_map/ppermute | solution.py:37
  126.5 3.3 %collective-permute-start.24 = (bf16[64,512]{1,0:T(8,128)(2,1)S(1)}, bf16[64,512]{1,0:T(8,128)(2,1)S(1)}, u32[]{:S(2)}, u32[]{:S(2)}) collective-permute-start(bf16[64,512]{1,0:T(8,128)(2,1)S(1)} %constant_dynamic-update-slice_fusion), channel_id=1, source_target_pairs={{0,192},{16,208},{32,224},{48,240},{64,0},{80,16},{96,32},{112,48}... | collective-permute-start | bytes 196616 | tf_op jit(solution)/shard_map/ppermute | solution.py:37
  132.8 7.0 %collective-permute-done.23 = bf16[64,512]{1,0:T(8,128)(2,1)S(1)} collective-permute-done((bf16[64,512]{1,0:T(8,128)(2,1)S(1)}, bf16[64,512]{1,0:T(8,128)(2,1)S(1)}, u32[]{:S(2)}, u32[]{:S(2)}) %collective-permute-start.23) | collective-permute-done | bytes 65568 | tf_op jit(solution)/shard_map/ppermute | solution.py:37
  139.8 2.6 %collective-permute-start.27 = (bf16[4,64,512]{2,1,0:T(8,128)(2,1)S(1)}, bf16[4,64,512]{2,1,0:T(8,128)(2,1)S(1)}, u32[]{:S(2)}, u32[]{:S(2)}) collective-permute-start(bf16[4,64,512]{2,1,0:T(8,128)(2,1)S(1)} %pad_maximum_fusion.3.g0), channel_id=1, source_target_pairs={{0,48},{16,0},{32,16},{48,32},{64,112},{80,64},{96,80},{112,96},{1... | collective-permute-start | bytes 786440 | tf_op jit(solution)/shard_map/ppermute | solution.py:37
  144.3 7.5 %collective-permute-done.27.g3 = bf16[4,64,512]{2,1,0:T(8,128)(2,1)S(1)} collective-permute-done((bf16[4,64,512]{2,1,0:T(8,128)(2,1)S(1)}, bf16[4,64,512]{2,1,0:T(8,128)(2,1)S(1)}, u32[]{:S(2)}, u32[]{:S(2)}) %collective-permute-start.27) | collective-permute-done | bytes 262176 | tf_op jit(solution)/shard_map/ppermute | solution.py:37
  152.8 2.7 %collective-permute-done.25.g1 = bf16[4,64,512]{2,1,0:T(8,128)(2,1)S(1)} collective-permute-done((bf16[4,64,512]{2,1,0:T(8,128)(2,1)S(1)}, bf16[4,64,512]{2,1,0:T(8,128)(2,1)S(1)}, u32[]{:S(2)}, u32[]{:S(2)}) %collective-permute-start.25) | collective-permute-done | bytes 262176 | tf_op jit(solution)/shard_map/ppermute | solution.py:37
  (84 shorter events, 40.2 us)
Async XLA Ops:
  31.2 31.2 %collective-permute-start.6 = (bf16[512,1024]{1,0:T(8,128)(2,1)S(1)}, bf16[512,1024]{1,0:T(8,128)(2,1)S(1)}, u32[]{:S(2)}, u32[]{:S(2)}) collective-permute-start(bf16[512,1024]{1,0:T(8,128)(2,1)S(1)} %pad_maximum_fusion.1), channel_id=1, source_target_pairs={{0,2},{1,3},{2,0},{3,1},{4,6},{5,7},{6,4},{7,5},{8,10},{9,11},{10,... | collective-permute-start | bytes 3145736 | tf_op jit(solution)/shard_map/ppermute | solution.py:33
  35.0 16.1 %collective-permute-start.3 = (bf16[512,512]{1,0:T(8,128)(2,1)S(1)}, bf16[512,512]{1,0:T(8,128)(2,1)S(1)}, u32[]{:S(2)}, u32[]{:S(2)}) collective-permute-start(bf16[512,512]{1,0:T(8,128)(2,1)S(1)} %grads.2.refs_0_), channel_id=1, source_target_pairs={{0,12},{1,13},{2,14},{3,15},{4,0},{5,1},{6,2},{7,3},{8,4},{9,5},{1... | collective-permute-start | bytes 1572872 | tf_op jit(solution)/shard_map/ppermute | solution.py:33
  35.1 16.7 %collective-permute-start.2 = (bf16[512,512]{1,0:T(8,128)(2,1)S(1)}, bf16[512,512]{1,0:T(8,128)(2,1)}, u32[]{:S(2)}, u32[]{:S(2)}) collective-permute-start(bf16[512,512]{1,0:T(8,128)(2,1)S(1)} %grads.2.refs_0_), channel_id=1, source_target_pairs={{0,4},{1,5},{2,6},{3,7},{4,8},{5,9},{6,10},{7,11},{8,12},{9,13},{1... | collective-permute-start | bytes 1572872 | tf_op jit(solution)/shard_map/ppermute | solution.py:33
  39.6 22.0 %collective-permute-start.5 = (bf16[512,512]{1,0:T(8,128)(2,1)S(1)}, bf16[512,512]{1,0:T(8,128)(2,1)}, u32[]{:S(2)}, u32[]{:S(2)}) collective-permute-start(bf16[512,512]{1,0:T(8,128)(2,1)S(1)} %grads.3.refs_1_), channel_id=1, source_target_pairs={{0,12},{1,13},{2,14},{3,15},{4,0},{5,1},{6,2},{7,3},{8,4},{9,5},{1... | collective-permute-start | bytes 1572872 | tf_op jit(solution)/shard_map/ppermute | solution.py:33
  39.7 21.9 %collective-permute-start.4 = (bf16[512,512]{1,0:T(8,128)(2,1)S(1)}, bf16[512,512]{1,0:T(8,128)(2,1)S(1)}, u32[]{:S(2)}, u32[]{:S(2)}) collective-permute-start(bf16[512,512]{1,0:T(8,128)(2,1)S(1)} %grads.3.refs_1_), channel_id=1, source_target_pairs={{0,4},{1,5},{2,6},{3,7},{4,8},{5,9},{6,10},{7,11},{8,12},{9,13},{1... | collective-permute-start | bytes 1572872 | tf_op jit(solution)/shard_map/ppermute | solution.py:33
  62.5 27.0 %collective-permute-start.7 = (bf16[512,1024]{1,0:T(8,128)(2,1)S(1)}, bf16[512,1024]{1,0:T(8,128)(2,1)S(1)}, u32[]{:S(2)}, u32[]{:S(2)}) collective-permute-start(bf16[512,1024]{1,0:T(8,128)(2,1)S(1)} %pad_maximum_fusion.2.refs_6_.w0), channel_id=1, source_target_pairs={{0,1},{1,0},{2,3},{3,2},{4,5},{5,4},{6,7},{7,6},{8,9},{9,8},{10,11... | collective-permute-start | bytes 3145736 | tf_op jit(solution)/shard_map/ppermute | solution.py:33
  63.1 14.6 %collective-permute-start.8 = (bf16[512,512]{1,0:T(8,128)(2,1)}, bf16[512,512]{1,0:T(8,128)(2,1)}, u32[]{:S(2)}, u32[]{:S(2)}) collective-permute-start(bf16[512,512]{1,0:T(8,128)(2,1)} %collective-permute-done.2.refs_2_), channel_id=1, source_target_pairs={{0,4},{1,5},{2,6},{3,7},{4,8},{5,9},{6,10},{7,11},{8,12},{9,13},{1... | collective-permute-start | bytes 1572872 | tf_op jit(solution)/shard_map/ppermute | solution.py:33
  65.9 15.2 %collective-permute-start.9 = (bf16[512,512]{1,0:T(8,128)(2,1)}, bf16[512,512]{1,0:T(8,128)(2,1)}, u32[]{:S(2)}, u32[]{:S(2)}) collective-permute-start(bf16[512,512]{1,0:T(8,128)(2,1)} %collective-permute-done.5.refs_5_), channel_id=1, source_target_pairs={{0,12},{1,13},{2,14},{3,15},{4,0},{5,1},{6,2},{7,3},{8,4},{9,5},{1... | collective-permute-start | bytes 1572872 | tf_op jit(solution)/shard_map/ppermute | solution.py:33
  83.5 12.6 %collective-permute-start.14 = (bf16[256,512]{1,0:T(8,128)(2,1)S(1)}, bf16[256,512]{1,0:T(8,128)(2,1)S(1)}, u32[]{:S(2)}, u32[]{:S(2)}) collective-permute-start(bf16[256,512]{1,0:T(8,128)(2,1)S(1)} %get-tuple-element.40), channel_id=1, source_target_pairs={{0,16},{16,32},{32,48},{48,0},{64,80},{80,96},{96,112},{112,64},{1... | collective-permute-start | bytes 786440 | tf_op jit(solution)/shard_map/ppermute | solution.py:37
  85.2 15.7 %collective-permute-start.15 = (bf16[256,512]{1,0:T(8,128)(2,1)S(1)}, bf16[256,512]{1,0:T(8,128)(2,1)S(1)}, u32[]{:S(2)}, u32[]{:S(2)}) collective-permute-start(bf16[256,512]{1,0:T(8,128)(2,1)S(1)} %get-tuple-element.41), channel_id=1, source_target_pairs={{0,32},{16,48},{32,0},{48,16},{64,96},{80,112},{96,64},{112,80},{1... | collective-permute-start | bytes 786440 | tf_op jit(solution)/shard_map/ppermute | solution.py:37
  88.1 13.4 %collective-permute-start.16 = (bf16[256,512]{1,0:T(8,128)(2,1)S(1)}, bf16[256,512]{1,0:T(8,128)(2,1)S(1)}, u32[]{:S(2)}, u32[]{:S(2)}) collective-permute-start(bf16[256,512]{1,0:T(8,128)(2,1)S(1)} %get-tuple-element.42), channel_id=1, source_target_pairs={{0,48},{16,0},{32,16},{48,32},{64,112},{80,64},{96,80},{112,96},{1... | collective-permute-start | bytes 786440 | tf_op jit(solution)/shard_map/ppermute | solution.py:37
  94.6 11.9 %collective-permute-start.10 = (bf16[256,512]{1,0:T(8,128)(2,1)S(1)}, bf16[256,512]{1,0:T(8,128)(2,1)S(1)}, u32[]{:S(2)}, u32[]{:S(2)}) collective-permute-start(bf16[256,512]{1,0:T(8,128)(2,1)S(1)} %get-tuple-element.35), channel_id=1, source_target_pairs={{0,16},{16,32},{32,48},{48,0},{64,80},{80,96},{96,112},{112,64},{1... | collective-permute-start | bytes 786440 | tf_op jit(solution)/shard_map/ppermute | solution.py:37
  95.4 14.7 %collective-permute-start.11 = (bf16[256,512]{1,0:T(8,128)(2,1)S(1)}, bf16[256,512]{1,0:T(8,128)(2,1)S(1)}, u32[]{:S(2)}, u32[]{:S(2)}) collective-permute-start(bf16[256,512]{1,0:T(8,128)(2,1)S(1)} %get-tuple-element.36), channel_id=1, source_target_pairs={{0,32},{16,48},{32,0},{48,16},{64,96},{80,112},{96,64},{112,80},{1... | collective-permute-start | bytes 786440 | tf_op jit(solution)/shard_map/ppermute | solution.py:37
  96.2 13.9 %collective-permute-start.12 = (bf16[256,512]{1,0:T(8,128)(2,1)S(1)}, bf16[256,512]{1,0:T(8,128)(2,1)S(1)}, u32[]{:S(2)}, u32[]{:S(2)}) collective-permute-start(bf16[256,512]{1,0:T(8,128)(2,1)S(1)} %get-tuple-element.37), channel_id=1, source_target_pairs={{0,48},{16,0},{32,16},{48,32},{64,112},{80,64},{96,80},{112,96},{1... | collective-permute-start | bytes 786440 | tf_op jit(solution)/shard_map/ppermute | solution.py:37
  101.7 8.4 %collective-permute-start.17 = (bf16[256,512]{1,0:T(8,128)(2,1)S(1)}, bf16[256,512]{1,0:T(8,128)(2,1)S(1)}, u32[]{:S(2)}, u32[]{:S(2)}) collective-permute-start(bf16[256,512]{1,0:T(8,128)(2,1)S(1)} %sum_y.1), channel_id=1, source_target_pairs={{0,2},{1,3},{2,0},{3,1},{4,6},{5,7},{6,4},{7,5},{8,10},{9,11},{10,... | collective-permute-start | bytes 786440 | tf_op jit(solution)/shard_map/ppermute | solution.py:33
  110.9 10.5 %collective-permute-start.18 = (bf16[64,512]{1,0:T(8,128)(2,1)S(1)}, bf16[64,512]{1,0:T(8,128)(2,1)S(1)}, u32[]{:S(2)}, u32[]{:S(2)}) collective-permute-start(bf16[64,512]{1,0:T(8,128)(2,1)S(1)} %get-tuple-element.44), channel_id=1, source_target_pairs={{0,64},{16,80},{32,96},{48,112},{64,128},{80,144},{96,160},{112,17... | collective-permute-start | bytes 196616 | tf_op jit(solution)/shard_map/ppermute | solution.py:37
  114.3 8.9 %collective-permute-start.19 = (bf16[64,512]{1,0:T(8,128)(2,1)S(1)}, bf16[64,512]{1,0:T(8,128)(2,1)S(1)}, u32[]{:S(2)}, u32[]{:S(2)}) collective-permute-start(bf16[64,512]{1,0:T(8,128)(2,1)S(1)} %get-tuple-element.45), channel_id=1, source_target_pairs={{0,128},{16,144},{32,160},{48,176},{64,192},{80,208},{96,224},{112... | collective-permute-start | bytes 196616 | tf_op jit(solution)/shard_map/ppermute | solution.py:37
  118.8 6.2 %collective-permute-start.20 = (bf16[64,512]{1,0:T(8,128)(2,1)S(1)}, bf16[64,512]{1,0:T(8,128)(2,1)S(1)}, u32[]{:S(2)}, u32[]{:S(2)}) collective-permute-start(bf16[64,512]{1,0:T(8,128)(2,1)S(1)} %get-tuple-element.46), channel_id=1, source_target_pairs={{0,192},{16,208},{32,224},{48,240},{64,0},{80,16},{96,32},{112,48}... | collective-permute-start | bytes 196616 | tf_op jit(solution)/shard_map/ppermute | solution.py:37
  126.5 6.3 %collective-permute-start.24 = (bf16[64,512]{1,0:T(8,128)(2,1)S(1)}, bf16[64,512]{1,0:T(8,128)(2,1)S(1)}, u32[]{:S(2)}, u32[]{:S(2)}) collective-permute-start(bf16[64,512]{1,0:T(8,128)(2,1)S(1)} %constant_dynamic-update-slice_fusion), channel_id=1, source_target_pairs={{0,192},{16,208},{32,224},{48,240},{64,0},{80,16},{96,32},{112,48}... | collective-permute-start | bytes 196616 | tf_op jit(solution)/shard_map/ppermute | solution.py:37
  129.8 10.0 %collective-permute-start.23 = (bf16[64,512]{1,0:T(8,128)(2,1)S(1)}, bf16[64,512]{1,0:T(8,128)(2,1)S(1)}, u32[]{:S(2)}, u32[]{:S(2)}) collective-permute-start(bf16[64,512]{1,0:T(8,128)(2,1)S(1)} %constant_dynamic-update-slice_fusion), channel_id=1, source_target_pairs={{0,128},{16,144},{32,160},{48,176},{64,192},{80,208},{96,224},{112... | collective-permute-start | bytes 196616 | tf_op jit(solution)/shard_map/ppermute | solution.py:37
  131.3 8.5 %collective-permute-start.22 = (bf16[64,512]{1,0:T(8,128)(2,1)S(1)}, bf16[64,512]{1,0:T(8,128)(2,1)S(1)}, u32[]{:S(2)}, u32[]{:S(2)}) collective-permute-start(bf16[64,512]{1,0:T(8,128)(2,1)S(1)} %constant_dynamic-update-slice_fusion), channel_id=1, source_target_pairs={{0,64},{16,80},{32,96},{48,112},{64,128},{80,144},{96,160},{112,17... | collective-permute-start | bytes 196616 | tf_op jit(solution)/shard_map/ppermute | solution.py:37
  139.8 12.0 %collective-permute-start.27 = (bf16[4,64,512]{2,1,0:T(8,128)(2,1)S(1)}, bf16[4,64,512]{2,1,0:T(8,128)(2,1)S(1)}, u32[]{:S(2)}, u32[]{:S(2)}) collective-permute-start(bf16[4,64,512]{2,1,0:T(8,128)(2,1)S(1)} %pad_maximum_fusion.3.g0), channel_id=1, source_target_pairs={{0,48},{16,0},{32,16},{48,32},{64,112},{80,64},{96,80},{112,96},{1... | collective-permute-start | bytes 786440 | tf_op jit(solution)/shard_map/ppermute | solution.py:37
  142.5 10.3 %collective-permute-start.26 = (bf16[4,64,512]{2,1,0:T(8,128)(2,1)S(1)}, bf16[4,64,512]{2,1,0:T(8,128)(2,1)S(1)}, u32[]{:S(2)}, u32[]{:S(2)}) collective-permute-start(bf16[4,64,512]{2,1,0:T(8,128)(2,1)S(1)} %pad_maximum_fusion.3.g0), channel_id=1, source_target_pairs={{0,32},{16,48},{32,0},{48,16},{64,96},{80,112},{96,64},{112,80},{1... | collective-permute-start | bytes 786440 | tf_op jit(solution)/shard_map/ppermute | solution.py:37
  144.3 11.2 %collective-permute-start.25 = (bf16[4,64,512]{2,1,0:T(8,128)(2,1)S(1)}, bf16[4,64,512]{2,1,0:T(8,128)(2,1)S(1)}, u32[]{:S(2)}, u32[]{:S(2)}) collective-permute-start(bf16[4,64,512]{2,1,0:T(8,128)(2,1)S(1)} %pad_maximum_fusion.3.g0), channel_id=1, source_target_pairs={{0,16},{16,32},{32,48},{48,0},{64,80},{80,96},{96,112},{112,64},{1... | collective-permute-start | bytes 786440 | tf_op jit(solution)/shard_map/ppermute | solution.py:37
  (19 other events, 80.8 us)

commit v4 on v3

--- a/solution.py
+++ b/solution.py
@@ -98,40 +98,42 @@
     )(mine, other)
 
 
-def grads_kernel(half, s0, s1, m_ref, o_ref, out, p_s, d_s, q_s, g_s):
+def grads_kernel(s0, s1, m_ref, o_ref, out, p_s, d_s, q_s, g_s):
     for j in range(4):
         q_s[pl.ds(j * 256, 256), :] = query_quarter(m_ref, o_ref, j, 0)
         g_s[pl.ds(j * 256, 256), :] = query_quarter(m_ref, o_ref, j, 64)
-    blocks = range(half * 4, half * 4 + 4)
-    k, v = key_rows(m_ref, 128, blocks), key_rows(m_ref, 256, blocks)
-    for j in range(4):
-        rows = pl.ds(j * 256, 256)
-        there = pl.ds((j ^ 2) * 256, 256)
-        own, far = s0[pl.ds(0, 1), rows], s1[pl.ds(0, 1), there]
-        peak = jnp.maximum(own, far)
-        own, far = jnp.exp(own - peak), jnp.exp(far - peak)
-        total = s0[pl.ds(1, 1), rows] * own + s1[pl.ds(1, 1), there] * far
-        weighted = s0[pl.ds(2, 1), rows] * own + s1[pl.ds(2, 1), there] * far
-        lse = peak + jnp.log(total)
-        delta = weighted / total
-        s = dot(k, q_s[rows, :], NT) * SCALE
-        gp = dot(v, g_s[rows, :], NT)
-        p = jnp.exp(s - lse)
-        p_s[:, rows] = p.astype(BF16)
-        d_s[:, rows] = (p * (gp - delta)).astype(BF16)
-    out[:, pl.ds(0, HEAD)] = (dot(d_s[...], q_s[...], NN) * SCALE).astype(BF16)
-    out[:, pl.ds(HEAD, HEAD)] = dot(p_s[...], g_s[...], NN).astype(BF16)
-
-
-def grads(half, parts, mine, other):
-    return pl.pallas_call(
-        functools.partial(grads_kernel, half),
-        out_shape=jax.ShapeDtypeStruct((512, 2 * HEAD), BF16),
+    for half in range(2):
+        spot = pl.ds(half * 512, 512)
+        blocks = range(half * 4, half * 4 + 4)
+        k, v = key_rows(m_ref, 128, blocks), key_rows(m_ref, 256, blocks)
+        for j in range(4):
+            rows = pl.ds(j * 256, 256)
+            there = pl.ds((j ^ 2) * 256, 256)
+            own, far = s0[pl.ds(0, 1), rows], s1[pl.ds(0, 1), there]
+            peak = jnp.maximum(own, far)
+            own, far = jnp.exp(own - peak), jnp.exp(far - peak)
+            total = s0[pl.ds(1, 1), rows] * own + s1[pl.ds(1, 1), there] * far
+            weighted = s0[pl.ds(2, 1), rows] * own + s1[pl.ds(2, 1), there] * far
+            lse = peak + jnp.log(total)
+            delta = weighted / total
+            s = dot(k, q_s[rows, :], NT) * SCALE
+            gp = dot(v, g_s[rows, :], NT)
+            p = jnp.exp(s - lse)
+            p_s[:, rows] = p.astype(BF16)
+            d_s[:, rows] = (p * (gp - delta)).astype(BF16)
+        out[spot, pl.ds(0, HEAD)] = (dot(d_s[...], q_s[...], NN) * SCALE).astype(BF16)
+        out[spot, pl.ds(HEAD, HEAD)] = dot(p_s[...], g_s[...], NN).astype(BF16)
+
+
+def grads(parts, mine, other):
+    return pl.pallas_call(
+        grads_kernel,
+        out_shape=jax.ShapeDtypeStruct((1024, 2 * HEAD), BF16),
         in_specs=[pl.BlockSpec(memory_space=pltpu.VMEM)] * 4,
         out_specs=pl.BlockSpec(memory_space=pltpu.VMEM),
         scratch_shapes=[pltpu.VMEM((512, 1024), BF16)] * 2 + [pltpu.VMEM((1024, HEAD), BF16)] * 2,
         compiler_params=pltpu.CompilerParams(vmem_limit_bytes=8 * 2**20),
-        cost_estimate=pl.CostEstimate(flops=10**9, bytes_accessed=2**22, transcendentals=2**19),
+        cost_estimate=pl.CostEstimate(flops=2 * 10**9, bytes_accessed=2**22, transcendentals=2**20),
         name="grads",
     )(*parts, mine, other)
 
@@ -141,13 +143,13 @@
 
 
 def project_kernel(pos_ref, *refs):
-    blocks, weights, out = refs[:6], refs[6:8], refs[8]
+    blocks, weights, out = refs[:3], refs[3:5], refs[5]
     for half in range(2):
         for w, weight in enumerate(weights):
             acc = None
             for n, d in enumerate((0, 1, 3)):
                 for kind in range(2):
-                    block = blocks[2 * n + half][:, pl.ds(kind * HEAD, HEAD)]
+                    block = blocks[n][pl.ds(half * 512, 512), pl.ds(kind * HEAD, HEAD)]
                     term = dot(block, weight[pl.ds(kind * 256, 256), head_cols(pos_ref[0], d)], NT)
                     acc = term if acc is None else acc + term
             out[pl.ds(half * 512, 512), pl.ds(w * 256, 256)] = acc.astype(out.dtype)
@@ -157,7 +159,7 @@
     return pl.pallas_call(
         project_kernel,
         out_shape=jax.ShapeDtypeStruct((1024, 512), BF16),
-        in_specs=[pl.BlockSpec(memory_space=pltpu.SMEM)] + [pl.BlockSpec(memory_space=pltpu.VMEM)] * 8,
+        in_specs=[pl.BlockSpec(memory_space=pltpu.SMEM)] + [pl.BlockSpec(memory_space=pltpu.VMEM)] * 5,
         out_specs=pl.BlockSpec(memory_space=pltpu.VMEM),
         compiler_params=pltpu.CompilerParams(vmem_limit_bytes=8 * 2**20),
         cost_estimate=pl.CostEstimate(flops=1024 * 512 * 1536 * 2, bytes_accessed=6 * 2**20, transcendentals=0),
@@ -302,13 +304,12 @@
     weight_z = along_seq(jnp.concatenate([half(kw, 1 - z), half(vw, 1 - z)], axis=0), dz=1)
     weight_c = along_seq(weight, dc=1)
 
-    low, high = grads(0, parts, mine, other), grads(1, parts, mine, other)
-    low_r, low_l = along_seq(low, dx=1), along_seq(low, dx=3)
-    high_r, high_l = along_seq(high, dx=1), along_seq(high, dx=3)
-    low_r, low_l, high_r, high_l, weight_z = tie((low_r, low_l, high_r, high_l, weight_z))
-    low_o, high_o = along_seq(low_r, dx=1), along_seq(high_l, dx=3)
+    own = grads(parts, mine, other)
+    right, left = along_seq(own, dx=1), along_seq(own, dx=3)
+    right, left, weight_z = tie((right, left, weight_z))
+    low_o, high_o = along_seq(right[:512], dx=1), along_seq(left[512:], dx=3)
     weight_zc = along_seq(weight_z, dc=1)
-    blocks = (low, high, low_r, high_r, low_l, high_l)
+    blocks = (own, right, left)
     stay, leave = project(pos, blocks, (weight, weight_c)), project(pos, blocks, (weight_z, weight_zc))
 
     def to_y(pieces):

time: 160 us -> 158 us (0.988)
  waiting for transfers between devices: 60.9 us -> 65.2 us
  local copies, waits for them, and re-layouts: 6.98 us -> 4.27 us
  starting transfers between devices: 43.2 us -> 40.8 us
    unnamed x31 -> x11, local copies, waits for them, and re-layouts: 6.62 us -> 2.22 us
    ppermute x13 -> x11, waiting for transfers between devices: 28.1 us -> 32 us  [along_seq(): return lax.ppermute(value, 'seq', seq_moves(dx, dz, dc))]
    ppermute x13 -> x11, starting transfers between devices: 12.7 us -> 9.76 us  [along_seq(): return lax.ppermute(value, 'seq', seq_moves(dx, dz, dc))]
    slice x0 -> x2, local copies, waits for them, and re-layouts: none -> 1.7 us  [local(): low_o, high_o = (along_seq(right[:512], dx=1), along_seq(left[512:], dx=3))]
  transfers between devices with their start and end apart: 28 -> 26, of which waited for: 18 -> 15; matrix products, arithmetic and copies ran while one was open for 0% -> 1% of each run, Pallas kernels for 9% -> 9%
where the time goes in v4:
time: 158 us; the launch traced here: 157 us
  waiting for transfers between devices  65.2 us (41%)
  starting transfers between devices  40.8 us (26%)
  blocking collectives  25 us (16%)
  Pallas kernels  19.1 us (12%)
  local copies, waits for them, and re-layouts  4.27 us (3%)
  other arithmetic  1.62 us (1%)
    ppermute x15, waiting for transfers between devices, along_section(): return lax.ppermute(value, 'section', section_moves(dh, dy))  33.2 us
    ppermute x11, waiting for transfers between devices, along_seq(): return lax.ppermute(value, 'seq', seq_moves(dx, dz, dc))  32 us
    ppermute x15, starting transfers between devices, along_section(): return lax.ppermute(value, 'section', section_moves(dh, dy))  31.1 us
    all_to_all x1, blocking collectives, local(): mine = lax.all_to_all(rows, 'seq', 0, 0, axis_index_groups=groups)  25 us
    ppermute x11, starting transfers between devices, along_seq(): return lax.ppermute(value, 'seq', seq_moves(dx, dz, dc))  9.76 us
    pallas_call x2, Pallas kernels, project(): pl.pallas_call(project_kernel, out_shape=jax.ShapeDtypeStruct((1024, 512)...  6.46 us
    pallas_call x2, Pallas kernels, finish(): pl.pallas_call(finish_kernel, out_shape=(jax.ShapeDtypeStruct((256, 512),...  5.18 us
  transfers between devices with their start and end apart: 26, of which 15 were waited for; matrix products, arithmetic and copies ran while one was open for 1% of the time, Pallas kernels for 9%

profile of v4, /device:TPU:6, one launch (start us, length us, event | category | flops | bytes accessed | tf_op | source)
XLA Modules:
  0.0 156.8 jit_solution(9167283066851452858)
XLA Ops:
  1.6 25.0 %all_to_all.5.m_ref = bf16[8,384,256]{2,1,0:T(8,128)(2,1)S(1)} all-to-all(bf16[8,384,256]{2,1,0:T(8,128)(2,1)S(1)} %pack.1), channel_id=1, replica_groups={{0,2,4,6,8,10,12,14},{1,3,5,7,9,11,13,15},{16,18,20,22,24,26,28,30},{17..., dimensions={0} | all-to-all | bytes 3145728 | tf_op jit(solution)/shard_map/all_to_all | solution.py:293
  28.6 2.2 %stats.1.s0 = f32[8,1024]{1,0:T(8,128)S(1)} custom-call(bf16[8,384,256]{2,1,0:T(8,128)(2,1)S(1)} %all_to_all.5.m_ref, bf16[8,128,256]{2,1,0:T(8,128)(2,1)S(1)} %collective-permute-done.o_ref), custom_call_target="tpu_custom_call" | custom-call | flops 1000000000 | bytes 4194304 | tf_op jit(solution)/shard_map/stats/pallas_call | solution.py:90
  32.7 2.4 %grads.1.refs_0_ = bf16[1024,512]{1,0:T(8,128)(2,1)S(1)} custom-call(f32[8,1024]{1,0:T(8,128)S(1)} %stats.1.s0, f32[8,1024]{1,0:T(8,128)S(1)} %collective-permute-done.1.s1, bf16[8,384,256]{2,1,0:T(8,128)(2,1)S(1)} %all_to_all.5.m_ref, bf16[8,128,256]{2,1,0:T(8,128)(2,1)S(1)} %collective-permute-done.o_ref), custom_call_target="tpu_custom_call" | custom-call | flops 2000000000 | bytes 4194304 | tf_op jit(solution)/shard_map/grads/pallas_call | solution.py:129
  35.5 2.8 %collective-permute-start.2 = (bf16[1024,512]{1,0:T(8,128)(2,1)S(1)}, bf16[1024,512]{1,0:T(8,128)(2,1)S(1)}, u32[]{:S(2)}, u32[]{:S(2)}) collective-permute-start(bf16[1024,512]{1,0:T(8,128)(2,1)S(1)} %grads.1.refs_0_), channel_id=1, source_target_pairs={{0,4},{1,5},{2,6},{3,7},{4,8},{5,9},{6,10},{7,11},{8,12},{9,13},{1... | collective-permute-start | bytes 3145736 | tf_op jit(solution)/shard_map/ppermute | solution.py:33
  39.3 17.7 %collective-permute-done.4.refs_3_.w0 = bf16[512,1024]{1,0:T(8,128)(2,1)} collective-permute-done((bf16[512,1024]{1,0:T(8,128)(2,1)S(1)}, bf16[512,1024]{1,0:T(8,128)(2,1)}, u32[]{:S(2)}, u32[]{:S(2)}) %collective-permute-start.4) | collective-permute-done | bytes 1048608 | tf_op jit(solution)/shard_map/ppermute | solution.py:33
  57.0 4.5 %collective-permute-done.3.refs_2_ = bf16[1024,512]{1,0:T(8,128)(2,1)S(1)} collective-permute-done((bf16[1024,512]{1,0:T(8,128)(2,1)S(1)}, bf16[1024,512]{1,0:T(8,128)(2,1)S(1)}, u32[]{:S(2)}, u32[]{:S(2)}) %collective-permute-start.3) | collective-permute-done | bytes 1048608 | tf_op jit(solution)/shard_map/ppermute | solution.py:33
  64.3 2.8 %collective-permute-start.6 = (bf16[512,512]{1,0:T(8,128)(2,1)}, bf16[512,512]{1,0:T(8,128)(2,1)}, u32[]{:S(2)}, u32[]{:S(2)}) collective-permute-start(bf16[512,512]{1,0:T(8,128)(2,1)} %slice.10), channel_id=1, source_target_pairs={{0,4},{1,5},{2,6},{3,7},{4,8},{5,9},{6,10},{7,11},{8,12},{9,13},{1... | collective-permute-start | bytes 1572872 | tf_op jit(solution)/shard_map/ppermute | solution.py:33
  69.1 3.4 %project.3.part = bf16[1024,512]{1,0:T(8,128)(2,1)S(1)} custom-call(s32[6]{0:T(128)S(1)} %stack.46.pos_ref, bf16[1024,512]{1,0:T(8,128)(2,1)S(1)} %copy-done.1, bf16[1024,512]{1,0:T(8,128)(2,1)S(1)} %collective-permute-done.2.refs_1_, bf16[1024,512]{1,0:T(8,128)(2,1)S(1)} %collective-permute-done.3.refs_2_, ...), custom_call_target="tpu_custom_call" | custom-call | flops 1610612736 | bytes 6291456 | tf_op jit(solution)/shard_map/project/pallas_call | solution.py:159
  72.5 6.8 %collective-permute-done.7.high = bf16[512,512]{1,0:T(8,128)(2,1)} collective-permute-done((bf16[512,512]{1,0:T(8,128)(2,1)}, bf16[512,512]{1,0:T(8,128)(2,1)}, u32[]{:S(2)}, u32[]{:S(2)}) %collective-permute-start.7) | collective-permute-done | bytes 524320 | tf_op jit(solution)/shard_map/ppermute | solution.py:33
  79.2 2.7 %finish.3 = (bf16[256,512]{1,0:T(8,128)(2,1)S(1)}, bf16[256,512]{1,0:T(8,128)(2,1)S(1)}, bf16[256,512]{1,0:T(8,128)(2,1)S(1)}, bf16[256,512]{1,0:T(8,128)(2,1)S(1)}) custom-call(s32[6]{0:T(128)S(1)} %stack.46.pos_ref, bf16[1024,512]{1,0:T(8,128)(2,1)S(1)} %project.3.part, bf16[512,512]{1,0:T(8,128)(2,1)} %collective-permute-done.6.low, ...), custom_call_target="tpu_custom_call" | custom-call | flops 536870912 | bytes 5242880 | tf_op jit(solution)/shard_map/finish/pallas_call | solution.py:185
  83.6 2.9 %collective-permute-start.13 = (bf16[256,512]{1,0:T(8,128)(2,1)S(1)}, bf16[256,512]{1,0:T(8,128)(2,1)S(1)}, u32[]{:S(2)}, u32[]{:S(2)}) collective-permute-start(bf16[256,512]{1,0:T(8,128)(2,1)S(1)} %get-tuple-element.37), channel_id=1, source_target_pairs={{0,32},{16,48},{32,0},{48,16},{64,96},{80,112},{96,64},{112,80},{1... | collective-permute-start | bytes 786440 | tf_op jit(solution)/shard_map/ppermute | solution.py:37
  87.9 3.1 %project.2.part = bf16[1024,512]{1,0:T(8,128)(2,1)S(1)} custom-call(s32[6]{0:T(128)S(1)} %stack.46.pos_ref, bf16[1024,512]{1,0:T(8,128)(2,1)S(1)} %copy-done.2, bf16[1024,512]{1,0:T(8,128)(2,1)S(1)} %collective-permute-done.2.refs_1_, bf16[1024,512]{1,0:T(8,128)(2,1)S(1)} %collective-permute-done.3.refs_2_, ...), custom_call_target="tpu_custom_call" | custom-call | flops 1610612736 | bytes 6291456 | tf_op jit(solution)/shard_map/project/pallas_call | solution.py:159
  91.0 2.4 %finish.2 = (bf16[256,512]{1,0:T(8,128)(2,1)S(1)}, bf16[256,512]{1,0:T(8,128)(2,1)S(1)}, bf16[256,512]{1,0:T(8,128)(2,1)S(1)}, bf16[256,512]{1,0:T(8,128)(2,1)S(1)}) custom-call(s32[6]{0:T(128)S(1)} %stack.46.pos_ref, bf16[1024,512]{1,0:T(8,128)(2,1)S(1)} %project.2.part, bf16[512,512]{1,0:T(8,128)(2,1)} %collective-permute-done.6.low, ...), custom_call_target="tpu_custom_call" | custom-call | flops 536870912 | bytes 5242880 | tf_op jit(solution)/shard_map/finish/pallas_call | solution.py:185
  97.0 2.4 %collective-permute-done.13.c = bf16[256,512]{1,0:T(8,128)(2,1)S(1)} collective-permute-done((bf16[256,512]{1,0:T(8,128)(2,1)S(1)}, bf16[256,512]{1,0:T(8,128)(2,1)S(1)}, u32[]{:S(2)}, u32[]{:S(2)}) %collective-permute-start.13) | collective-permute-done | bytes 262176 | tf_op jit(solution)/shard_map/ppermute | solution.py:37
  100.5 4.5 %collective-permute-done.8.refs_1_ = bf16[256,512]{1,0:T(8,128)(2,1)S(1)} collective-permute-done((bf16[256,512]{1,0:T(8,128)(2,1)S(1)}, bf16[256,512]{1,0:T(8,128)(2,1)S(1)}, u32[]{:S(2)}, u32[]{:S(2)}) %collective-permute-start.8) | collective-permute-done | bytes 262176 | tf_op jit(solution)/shard_map/ppermute | solution.py:37
  105.0 3.8 %collective-permute-done.9.refs_2_ = bf16[256,512]{1,0:T(8,128)(2,1)S(1)} collective-permute-done((bf16[256,512]{1,0:T(8,128)(2,1)S(1)}, bf16[256,512]{1,0:T(8,128)(2,1)S(1)}, u32[]{:S(2)}, u32[]{:S(2)}) %collective-permute-start.9) | collective-permute-done | bytes 262176 | tf_op jit(solution)/shard_map/ppermute | solution.py:37
  109.6 3.3 %collective-permute-start.16 = (bf16[64,512]{1,0:T(8,128)(2,1)S(1)}, bf16[64,512]{1,0:T(8,128)(2,1)S(1)}, u32[]{:S(2)}, u32[]{:S(2)}) collective-permute-start(bf16[64,512]{1,0:T(8,128)(2,1)S(1)} %get-tuple-element.40), channel_id=1, source_target_pairs={{0,64},{16,80},{32,96},{48,112},{64,128},{80,144},{96,160},{112,17... | collective-permute-start | bytes 196616 | tf_op jit(solution)/shard_map/ppermute | solution.py:37
  113.0 4.5 %collective-permute-start.17 = (bf16[64,512]{1,0:T(8,128)(2,1)S(1)}, bf16[64,512]{1,0:T(8,128)(2,1)S(1)}, u32[]{:S(2)}, u32[]{:S(2)}) collective-permute-start(bf16[64,512]{1,0:T(8,128)(2,1)S(1)} %get-tuple-element.41), channel_id=1, source_target_pairs={{0,128},{16,144},{32,160},{48,176},{64,192},{80,208},{96,224},{112... | collective-permute-start | bytes 196616 | tf_op jit(solution)/shard_map/ppermute | solution.py:37
  117.4 2.7 %collective-permute-start.18 = (bf16[64,512]{1,0:T(8,128)(2,1)S(1)}, bf16[64,512]{1,0:T(8,128)(2,1)S(1)}, u32[]{:S(2)}, u32[]{:S(2)}) collective-permute-start(bf16[64,512]{1,0:T(8,128)(2,1)S(1)} %get-tuple-element.42), channel_id=1, source_target_pairs={{0,192},{16,208},{32,224},{48,240},{64,0},{80,16},{96,32},{112,48}... | collective-permute-start | bytes 196616 | tf_op jit(solution)/shard_map/ppermute | solution.py:37
  124.9 3.3 %collective-permute-start.22 = (bf16[64,512]{1,0:T(8,128)(2,1)S(1)}, bf16[64,512]{1,0:T(8,128)(2,1)S(1)}, u32[]{:S(2)}, u32[]{:S(2)}) collective-permute-start(bf16[64,512]{1,0:T(8,128)(2,1)S(1)} %constant_dynamic-update-slice_fusion), channel_id=1, source_target_pairs={{0,192},{16,208},{32,224},{48,240},{64,0},{80,16},{96,32},{112,48}... | collective-permute-start | bytes 196616 | tf_op jit(solution)/shard_map/ppermute | solution.py:37
  131.4 6.0 %collective-permute-done.21 = bf16[64,512]{1,0:T(8,128)(2,1)S(1)} collective-permute-done((bf16[64,512]{1,0:T(8,128)(2,1)S(1)}, bf16[64,512]{1,0:T(8,128)(2,1)S(1)}, u32[]{:S(2)}, u32[]{:S(2)}) %collective-permute-start.21) | collective-permute-done | bytes 65568 | tf_op jit(solution)/shard_map/ppermute | solution.py:37
  137.4 3.6 %collective-permute-start.25 = (bf16[4,64,512]{2,1,0:T(8,128)(2,1)S(1)}, bf16[4,64,512]{2,1,0:T(8,128)(2,1)S(1)}, u32[]{:S(2)}, u32[]{:S(2)}) collective-permute-start(bf16[4,64,512]{2,1,0:T(8,128)(2,1)S(1)} %pad_maximum_fusion.3.g0), channel_id=1, source_target_pairs={{0,48},{16,0},{32,16},{48,32},{64,112},{80,64},{96,80},{112,96},{1... | collective-permute-start | bytes 786440 | tf_op jit(solution)/shard_map/ppermute | solution.py:37
  142.8 8.9 %collective-permute-done.25.g3 = bf16[4,64,512]{2,1,0:T(8,128)(2,1)S(1)} collective-permute-done((bf16[4,64,512]{2,1,0:T(8,128)(2,1)S(1)}, bf16[4,64,512]{2,1,0:T(8,128)(2,1)S(1)}, u32[]{:S(2)}, u32[]{:S(2)}) %collective-permute-start.25) | collective-permute-done | bytes 262176 | tf_op jit(solution)/shard_map/ppermute | solution.py:37
  151.8 3.3 %collective-permute-done.23.g1 = bf16[4,64,512]{2,1,0:T(8,128)(2,1)S(1)} collective-permute-done((bf16[4,64,512]{2,1,0:T(8,128)(2,1)S(1)}, bf16[4,64,512]{2,1,0:T(8,128)(2,1)S(1)}, u32[]{:S(2)}, u32[]{:S(2)}) %collective-permute-start.23) | collective-permute-done | bytes 262176 | tf_op jit(solution)/shard_map/ppermute | solution.py:37
  (61 shorter events, 31.0 us)
Async XLA Ops:
  26.6 2.0 %collective-permute-start = (bf16[8,128,256]{2,1,0:T(8,128)(2,1)S(1)}, bf16[8,128,256]{2,1,0:T(8,128)(2,1)S(1)}, u32[]{:S(2)}, u32[]{:S(2)}) collective-permute-start(bf16[8,128,256]{2,1,0:T(8,128)(2,1)S(1)} %slice.12), channel_id=1, source_target_pairs={{0,1},{1,0},{2,3},{3,2},{4,5},{5,4},{6,7},{7,6},{8,9},{9,8},{10,11... | collective-permute-start | bytes 1572872 | tf_op jit(solution)/shard_map/ppermute | solution.py:33
  31.4 25.6 %collective-permute-start.4 = (bf16[512,1024]{1,0:T(8,128)(2,1)S(1)}, bf16[512,1024]{1,0:T(8,128)(2,1)}, u32[]{:S(2)}, u32[]{:S(2)}) collective-permute-start(bf16[512,1024]{1,0:T(8,128)(2,1)S(1)} %pad_maximum_fusion.1), channel_id=1, source_target_pairs={{0,2},{1,3},{2,0},{3,1},{4,6},{5,7},{6,4},{7,5},{8,10},{9,11},{10,... | collective-permute-start | bytes 3145736 | tf_op jit(solution)/shard_map/ppermute | solution.py:33
  35.0 26.4 %collective-permute-start.3 = (bf16[1024,512]{1,0:T(8,128)(2,1)S(1)}, bf16[1024,512]{1,0:T(8,128)(2,1)S(1)}, u32[]{:S(2)}, u32[]{:S(2)}) collective-permute-start(bf16[1024,512]{1,0:T(8,128)(2,1)S(1)} %grads.1.refs_0_), channel_id=1, source_target_pairs={{0,12},{1,13},{2,14},{3,15},{4,0},{5,1},{6,2},{7,3},{8,4},{9,5},{1... | collective-permute-start | bytes 3145736 | tf_op jit(solution)/shard_map/ppermute | solution.py:33
  35.5 26.0 %collective-permute-start.2 = (bf16[1024,512]{1,0:T(8,128)(2,1)S(1)}, bf16[1024,512]{1,0:T(8,128)(2,1)S(1)}, u32[]{:S(2)}, u32[]{:S(2)}) collective-permute-start(bf16[1024,512]{1,0:T(8,128)(2,1)S(1)} %grads.1.refs_0_), channel_id=1, source_target_pairs={{0,4},{1,5},{2,6},{3,7},{4,8},{5,9},{6,10},{7,11},{8,12},{9,13},{1... | collective-permute-start | bytes 3145736 | tf_op jit(solution)/shard_map/ppermute | solution.py:33
  61.5 6.4 %collective-permute-start.11 = (bf16[512,1024]{1,0:T(8,128)(2,1)}, bf16[512,1024]{1,0:T(8,128)(2,1)}, u32[]{:S(2)}, u32[]{:S(2)}) collective-permute-start(bf16[512,1024]{1,0:T(8,128)(2,1)} %collective-permute-done.4.refs_3_.w0), channel_id=1, source_target_pairs={{0,1},{1,0},{2,3},{3,2},{4,5},{5,4},{6,7},{7,6},{8,9},{9,8},{10,11... | collective-permute-start | bytes 3145736 | tf_op jit(solution)/shard_map/ppermute | solution.py:33
  61.6 26.3 %collective-permute-start.5 = (bf16[512,1024]{1,0:T(8,128)(2,1)S(1)}, bf16[512,1024]{1,0:T(8,128)(2,1)}, u32[]{:S(2)}, u32[]{:S(2)}) collective-permute-start(bf16[512,1024]{1,0:T(8,128)(2,1)S(1)} %pad_maximum_fusion.2.refs_3_.w0), channel_id=1, source_target_pairs={{0,1},{1,0},{2,3},{3,2},{4,5},{5,4},{6,7},{7,6},{8,9},{9,8},{10,11... | collective-permute-start | bytes 3145736 | tf_op jit(solution)/shard_map/ppermute | solution.py:33
  63.9 15.4 %collective-permute-start.7 = (bf16[512,512]{1,0:T(8,128)(2,1)}, bf16[512,512]{1,0:T(8,128)(2,1)}, u32[]{:S(2)}, u32[]{:S(2)}) collective-permute-start(bf16[512,512]{1,0:T(8,128)(2,1)} %slice.11), channel_id=1, source_target_pairs={{0,12},{1,13},{2,14},{3,15},{4,0},{5,1},{6,2},{7,3},{8,4},{9,5},{1... | collective-permute-start | bytes 1572872 | tf_op jit(solution)/shard_map/ppermute | solution.py:33
  64.3 15.0 %collective-permute-start.6 = (bf16[512,512]{1,0:T(8,128)(2,1)}, bf16[512,512]{1,0:T(8,128)(2,1)}, u32[]{:S(2)}, u32[]{:S(2)}) collective-permute-start(bf16[512,512]{1,0:T(8,128)(2,1)} %slice.10), channel_id=1, source_target_pairs={{0,4},{1,5},{2,6},{3,7},{4,8},{5,9},{6,10},{7,11},{8,12},{9,13},{1... | collective-permute-start | bytes 1572872 | tf_op jit(solution)/shard_map/ppermute | solution.py:33
  82.0 13.0 %collective-permute-start.12 = (bf16[256,512]{1,0:T(8,128)(2,1)S(1)}, bf16[256,512]{1,0:T(8,128)(2,1)S(1)}, u32[]{:S(2)}, u32[]{:S(2)}) collective-permute-start(bf16[256,512]{1,0:T(8,128)(2,1)S(1)} %get-tuple-element.36), channel_id=1, source_target_pairs={{0,16},{16,32},{32,48},{48,0},{64,80},{80,96},{96,112},{112,64},{1... | collective-permute-start | bytes 786440 | tf_op jit(solution)/shard_map/ppermute | solution.py:37
  83.6 15.7 %collective-permute-start.13 = (bf16[256,512]{1,0:T(8,128)(2,1)S(1)}, bf16[256,512]{1,0:T(8,128)(2,1)S(1)}, u32[]{:S(2)}, u32[]{:S(2)}) collective-permute-start(bf16[256,512]{1,0:T(8,128)(2,1)S(1)} %get-tuple-element.37), channel_id=1, source_target_pairs={{0,32},{16,48},{32,0},{48,16},{64,96},{80,112},{96,64},{112,80},{1... | collective-permute-start | bytes 786440 | tf_op jit(solution)/shard_map/ppermute | solution.py:37
  86.5 12.8 %collective-permute-start.14 = (bf16[256,512]{1,0:T(8,128)(2,1)S(1)}, bf16[256,512]{1,0:T(8,128)(2,1)S(1)}, u32[]{:S(2)}, u32[]{:S(2)}) collective-permute-start(bf16[256,512]{1,0:T(8,128)(2,1)S(1)} %get-tuple-element.38), channel_id=1, source_target_pairs={{0,48},{16,0},{32,16},{48,32},{64,112},{80,64},{96,80},{112,96},{1... | collective-permute-start | bytes 786440 | tf_op jit(solution)/shard_map/ppermute | solution.py:37
  93.4 11.6 %collective-permute-start.8 = (bf16[256,512]{1,0:T(8,128)(2,1)S(1)}, bf16[256,512]{1,0:T(8,128)(2,1)S(1)}, u32[]{:S(2)}, u32[]{:S(2)}) collective-permute-start(bf16[256,512]{1,0:T(8,128)(2,1)S(1)} %get-tuple-element.31), channel_id=1, source_target_pairs={{0,16},{16,32},{32,48},{48,0},{64,80},{80,96},{96,112},{112,64},{1... | collective-permute-start | bytes 786440 | tf_op jit(solution)/shard_map/ppermute | solution.py:37
  94.2 14.6 %collective-permute-start.9 = (bf16[256,512]{1,0:T(8,128)(2,1)S(1)}, bf16[256,512]{1,0:T(8,128)(2,1)S(1)}, u32[]{:S(2)}, u32[]{:S(2)}) collective-permute-start(bf16[256,512]{1,0:T(8,128)(2,1)S(1)} %get-tuple-element.32), channel_id=1, source_target_pairs={{0,32},{16,48},{32,0},{48,16},{64,96},{80,112},{96,64},{112,80},{1... | collective-permute-start | bytes 786440 | tf_op jit(solution)/shard_map/ppermute | solution.py:37
  95.0 13.8 %collective-permute-start.10 = (bf16[256,512]{1,0:T(8,128)(2,1)S(1)}, bf16[256,512]{1,0:T(8,128)(2,1)S(1)}, u32[]{:S(2)}, u32[]{:S(2)}) collective-permute-start(bf16[256,512]{1,0:T(8,128)(2,1)S(1)} %get-tuple-element.33), channel_id=1, source_target_pairs={{0,48},{16,0},{32,16},{48,32},{64,112},{80,64},{96,80},{112,96},{1... | collective-permute-start | bytes 786440 | tf_op jit(solution)/shard_map/ppermute | solution.py:37
  99.5 9.2 %collective-permute-start.15 = (bf16[256,512]{1,0:T(8,128)(2,1)S(1)}, bf16[256,512]{1,0:T(8,128)(2,1)S(1)}, u32[]{:S(2)}, u32[]{:S(2)}) collective-permute-start(bf16[256,512]{1,0:T(8,128)(2,1)S(1)} %sum_y.1), channel_id=1, source_target_pairs={{0,2},{1,3},{2,0},{3,1},{4,6},{5,7},{6,4},{7,5},{8,10},{9,11},{10,... | collective-permute-start | bytes 786440 | tf_op jit(solution)/shard_map/ppermute | solution.py:33
  109.6 10.5 %collective-permute-start.16 = (bf16[64,512]{1,0:T(8,128)(2,1)S(1)}, bf16[64,512]{1,0:T(8,128)(2,1)S(1)}, u32[]{:S(2)}, u32[]{:S(2)}) collective-permute-start(bf16[64,512]{1,0:T(8,128)(2,1)S(1)} %get-tuple-element.40), channel_id=1, source_target_pairs={{0,64},{16,80},{32,96},{48,112},{64,128},{80,144},{96,160},{112,17... | collective-permute-start | bytes 196616 | tf_op jit(solution)/shard_map/ppermute | solution.py:37
  113.0 8.8 %collective-permute-start.17 = (bf16[64,512]{1,0:T(8,128)(2,1)S(1)}, bf16[64,512]{1,0:T(8,128)(2,1)S(1)}, u32[]{:S(2)}, u32[]{:S(2)}) collective-permute-start(bf16[64,512]{1,0:T(8,128)(2,1)S(1)} %get-tuple-element.41), channel_id=1, source_target_pairs={{0,128},{16,144},{32,160},{48,176},{64,192},{80,208},{96,224},{112... | collective-permute-start | bytes 196616 | tf_op jit(solution)/shard_map/ppermute | solution.py:37
  117.4 6.1 %collective-permute-start.18 = (bf16[64,512]{1,0:T(8,128)(2,1)S(1)}, bf16[64,512]{1,0:T(8,128)(2,1)S(1)}, u32[]{:S(2)}, u32[]{:S(2)}) collective-permute-start(bf16[64,512]{1,0:T(8,128)(2,1)S(1)} %get-tuple-element.42), channel_id=1, source_target_pairs={{0,192},{16,208},{32,224},{48,240},{64,0},{80,16},{96,32},{112,48}... | collective-permute-start | bytes 196616 | tf_op jit(solution)/shard_map/ppermute | solution.py:37
  124.9 6.6 %collective-permute-start.22 = (bf16[64,512]{1,0:T(8,128)(2,1)S(1)}, bf16[64,512]{1,0:T(8,128)(2,1)S(1)}, u32[]{:S(2)}, u32[]{:S(2)}) collective-permute-start(bf16[64,512]{1,0:T(8,128)(2,1)S(1)} %constant_dynamic-update-slice_fusion), channel_id=1, source_target_pairs={{0,192},{16,208},{32,224},{48,240},{64,0},{80,16},{96,32},{112,48}... | collective-permute-start | bytes 196616 | tf_op jit(solution)/shard_map/ppermute | solution.py:37
  128.2 9.2 %collective-permute-start.21 = (bf16[64,512]{1,0:T(8,128)(2,1)S(1)}, bf16[64,512]{1,0:T(8,128)(2,1)S(1)}, u32[]{:S(2)}, u32[]{:S(2)}) collective-permute-start(bf16[64,512]{1,0:T(8,128)(2,1)S(1)} %constant_dynamic-update-slice_fusion), channel_id=1, source_target_pairs={{0,128},{16,144},{32,160},{48,176},{64,192},{80,208},{96,224},{112... | collective-permute-start | bytes 196616 | tf_op jit(solution)/shard_map/ppermute | solution.py:37
  129.8 7.6 %collective-permute-start.20 = (bf16[64,512]{1,0:T(8,128)(2,1)S(1)}, bf16[64,512]{1,0:T(8,128)(2,1)S(1)}, u32[]{:S(2)}, u32[]{:S(2)}) collective-permute-start(bf16[64,512]{1,0:T(8,128)(2,1)S(1)} %constant_dynamic-update-slice_fusion), channel_id=1, source_target_pairs={{0,64},{16,80},{32,96},{48,112},{64,128},{80,144},{96,160},{112,17... | collective-permute-start | bytes 196616 | tf_op jit(solution)/shard_map/ppermute | solution.py:37
  137.4 14.2 %collective-permute-start.25 = (bf16[4,64,512]{2,1,0:T(8,128)(2,1)S(1)}, bf16[4,64,512]{2,1,0:T(8,128)(2,1)S(1)}, u32[]{:S(2)}, u32[]{:S(2)}) collective-permute-start(bf16[4,64,512]{2,1,0:T(8,128)(2,1)S(1)} %pad_maximum_fusion.3.g0), channel_id=1, source_target_pairs={{0,48},{16,0},{32,16},{48,32},{64,112},{80,64},{96,80},{112,96},{1... | collective-permute-start | bytes 786440 | tf_op jit(solution)/shard_map/ppermute | solution.py:37
  141.0 10.7 %collective-permute-start.24 = (bf16[4,64,512]{2,1,0:T(8,128)(2,1)S(1)}, bf16[4,64,512]{2,1,0:T(8,128)(2,1)S(1)}, u32[]{:S(2)}, u32[]{:S(2)}) collective-permute-start(bf16[4,64,512]{2,1,0:T(8,128)(2,1)S(1)} %pad_maximum_fusion.3.g0), channel_id=1, source_target_pairs={{0,32},{16,48},{32,0},{48,16},{64,96},{80,112},{96,64},{112,80},{1... | collective-permute-start | bytes 786440 | tf_op jit(solution)/shard_map/ppermute | solution.py:37
  142.8 12.3 %collective-permute-start.23 = (bf16[4,64,512]{2,1,0:T(8,128)(2,1)S(1)}, bf16[4,64,512]{2,1,0:T(8,128)(2,1)S(1)}, u32[]{:S(2)}, u32[]{:S(2)}) collective-permute-start(bf16[4,64,512]{2,1,0:T(8,128)(2,1)S(1)} %pad_maximum_fusion.3.g0), channel_id=1, source_target_pairs={{0,16},{16,32},{32,48},{48,0},{64,80},{80,96},{96,112},{112,64},{1... | collective-permute-start | bytes 786440 | tf_op jit(solution)/shard_map/ppermute | solution.py:37
  (7 other events, 29.4 us)

commit v5 on v4

--- a/solution.py
+++ b/solution.py
@@ -72,13 +72,13 @@
     return jnp.concatenate([mine[i, pl.ds(first, 128), :] for i in blocks], axis=0)
 
 
-def stats_kernel(m_ref, o_ref, out_ref):
+def stats_kernel(first, m_ref, q_ref, out_ref):
     out_ref[...] = jnp.zeros_like(out_ref)
     k, v = key_rows(m_ref, 128, range(8)), key_rows(m_ref, 256, range(8))
-    for j in range(4):
+    for j in range(2):
         spot = pl.ds(j * 256, 256)
-        s = dot(k, query_quarter(m_ref, o_ref, j, 0), NT) * SCALE
-        gp = dot(v, query_quarter(m_ref, o_ref, j, 64), NT)
+        s = dot(k, query_quarter(m_ref, q_ref, first + j, 0), NT) * SCALE
+        gp = dot(v, query_quarter(m_ref, q_ref, first + j, 64), NT)
         peak = jnp.max(s, axis=0, keepdims=True)
         p = jnp.exp(s - peak)
         out_ref[pl.ds(0, 1), spot] = peak
@@ -86,19 +86,19 @@
         out_ref[pl.ds(2, 1), spot] = jnp.sum(p * gp, axis=0, keepdims=True)
 
 
-def stats(mine, other):
-    return pl.pallas_call(
-        stats_kernel,
-        out_shape=jax.ShapeDtypeStruct((8, 1024), F32),
+def stats(first, mine, other):
+    return pl.pallas_call(
+        functools.partial(stats_kernel, first),
+        out_shape=jax.ShapeDtypeStruct((8, 512), F32),
         in_specs=[pl.BlockSpec(memory_space=pltpu.VMEM)] * 2,
         out_specs=pl.BlockSpec(memory_space=pltpu.VMEM),
         compiler_params=pltpu.CompilerParams(vmem_limit_bytes=8 * 2**20),
-        cost_estimate=pl.CostEstimate(flops=10**9, bytes_accessed=2**22, transcendentals=2**20),
+        cost_estimate=pl.CostEstimate(flops=10**9, bytes_accessed=2**21, transcendentals=2**19),
         name="stats",
     )(mine, other)
 
 
-def grads_kernel(s0, s1, m_ref, o_ref, out, p_s, d_s, q_s, g_s):
+def grads_kernel(a0, b0, a1, b1, m_ref, o_ref, out, p_s, d_s, q_s, g_s):
     for j in range(4):
         q_s[pl.ds(j * 256, 256), :] = query_quarter(m_ref, o_ref, j, 0)
         g_s[pl.ds(j * 256, 256), :] = query_quarter(m_ref, o_ref, j, 64)
@@ -108,12 +108,13 @@
         k, v = key_rows(m_ref, 128, blocks), key_rows(m_ref, 256, blocks)
         for j in range(4):
             rows = pl.ds(j * 256, 256)
-            there = pl.ds((j ^ 2) * 256, 256)
-            own, far = s0[pl.ds(0, 1), rows], s1[pl.ds(0, 1), there]
+            here, there = (a0, b1) if j < 2 else (b0, a1)
+            part = pl.ds((j % 2) * 256, 256)
+            own, far = here[pl.ds(0, 1), part], there[pl.ds(0, 1), part]
             peak = jnp.maximum(own, far)
             own, far = jnp.exp(own - peak), jnp.exp(far - peak)
-            total = s0[pl.ds(1, 1), rows] * own + s1[pl.ds(1, 1), there] * far
-            weighted = s0[pl.ds(2, 1), rows] * own + s1[pl.ds(2, 1), there] * far
+            total = here[pl.ds(1, 1), part] * own + there[pl.ds(1, 1), part] * far
+            weighted = here[pl.ds(2, 1), part] * own + there[pl.ds(2, 1), part] * far
             lse = peak + jnp.log(total)
             delta = weighted / total
             s = dot(k, q_s[rows, :], NT) * SCALE
@@ -129,7 +130,7 @@
     return pl.pallas_call(
         grads_kernel,
         out_shape=jax.ShapeDtypeStruct((1024, 2 * HEAD), BF16),
-        in_specs=[pl.BlockSpec(memory_space=pltpu.VMEM)] * 4,
+        in_specs=[pl.BlockSpec(memory_space=pltpu.VMEM)] * 6,
         out_specs=pl.BlockSpec(memory_space=pltpu.VMEM),
         scratch_shapes=[pltpu.VMEM((512, 1024), BF16)] * 2 + [pltpu.VMEM((1024, HEAD), BF16)] * 2,
         compiler_params=pltpu.CompilerParams(vmem_limit_bytes=8 * 2**20),
@@ -293,9 +294,9 @@
     mine = lax.all_to_all(rows, "seq", 0, 0, axis_index_groups=groups)
     other = along_seq(mine[:, :128], dc=1)
 
-    own = stats(mine, other)
-    own, kw, vw = tie((own, kw, vw))
-    parts = [own, along_seq(own, dc=1)]
+    first, second = stats(0, mine, mine), stats(2, mine, other)
+    second, kw, vw = tie((second, kw, vw))
+    parts = [first, second, along_seq(first, dc=1), along_seq(second, dc=1)]
 
     def half(matrix, at):
         return lax.dynamic_slice(matrix, (jnp.int32(0), at * 1024), (256, 1024))

time: 158 us -> 157 us (level)
  waiting for transfers between devices: 65.2 us -> 63.3 us
    ppermute x11 -> x12, waiting for transfers between devices: 32 us -> 30.2 us  [along_seq(): return lax.ppermute(value, 'seq', seq_moves(dx, dz, dc))]
    ppermute x11 -> x12, starting transfers between devices: 9.76 us -> 10.3 us  [along_seq(): return lax.ppermute(value, 'seq', seq_moves(dx, dz, dc))]
  transfers between devices with their start and end apart: 26 -> 27, of which waited for: 15 -> 14; matrix products, arithmetic and copies ran while one was open for 1% -> 1% of each run, Pallas kernels for 9% -> 11%
where the time goes in v5:
time: 157 us; the launch traced here: 156 us
  waiting for transfers between devices  63.3 us (40%)
  starting transfers between devices  41.4 us (26%)
  blocking collectives  25 us (16%)
  Pallas kernels  19.5 us (12%)
  local copies, waits for them, and re-layouts  4.25 us (3%)
  other arithmetic  1.62 us (1%)
    ppermute x15, waiting for transfers between devices, along_section(): return lax.ppermute(value, 'section', section_moves(dh, dy))  33.1 us
    ppermute x15, starting transfers between devices, along_section(): return lax.ppermute(value, 'section', section_moves(dh, dy))  31.1 us
    ppermute x12, waiting for transfers between devices, along_seq(): return lax.ppermute(value, 'seq', seq_moves(dx, dz, dc))  30.2 us
    all_to_all x1, blocking collectives, local(): mine = lax.all_to_all(rows, 'seq', 0, 0, axis_index_groups=groups)  25 us
    ppermute x12, starting transfers between devices, along_seq(): return lax.ppermute(value, 'seq', seq_moves(dx, dz, dc))  10.3 us
    pallas_call x2, Pallas kernels, project(): pl.pallas_call(project_kernel, out_shape=jax.ShapeDtypeStruct((1024, 512)...  6.46 us
    pallas_call x2, Pallas kernels, finish(): pl.pallas_call(finish_kernel, out_shape=(jax.ShapeDtypeStruct((256, 512),...  5.18 us
  transfers between devices with their start and end apart: 27, of which 14 were waited for; matrix products, arithmetic and copies ran while one was open for 1% of the time, Pallas kernels for 11%

profile of v5, /device:TPU:6, one launch (start us, length us, event | category | flops | bytes accessed | tf_op | source)
XLA Modules:
  0.0 155.9 jit_solution(3452870365888769635)
XLA Ops:
  1.6 25.0 %all_to_all.5.m_ref.q_ref = bf16[8,384,256]{2,1,0:T(8,128)(2,1)S(1)} all-to-all(bf16[8,384,256]{2,1,0:T(8,128)(2,1)S(1)} %pack.1), channel_id=1, replica_groups={{0,2,4,6,8,10,12,14},{1,3,5,7,9,11,13,15},{16,18,20,22,24,26,28,30},{17..., dimensions={0} | all-to-all | bytes 3145728 | tf_op jit(solution)/shard_map/all_to_all | solution.py:294
  31.7 2.4 %grads.1.refs_0_ = bf16[1024,512]{1,0:T(8,128)(2,1)S(1)} custom-call(f32[8,512]{1,0:T(8,128)S(1)} %stats.2.a0, f32[8,512]{1,0:T(8,128)S(1)} %stats.3.b0, f32[8,512]{1,0:T(8,128)S(1)} %collective-permute-done.1.a1, f32[8,512]{1,0:T(8,128)S(1)} %collective-permute-done.2.b1, bf16[8,384,256]{2,1,0:T(8,128)(2,1)S(1)} %all_to_all.5.m_ref.q_ref, ...), custom_call_target="tpu_custom_call" | custom-call | flops 2000000000 | bytes 4194304 | tf_op jit(solution)/shard_map/grads/pallas_call | solution.py:130
  34.6 2.8 %collective-permute-start.3 = (bf16[1024,512]{1,0:T(8,128)(2,1)S(1)}, bf16[1024,512]{1,0:T(8,128)(2,1)S(1)}, u32[]{:S(2)}, u32[]{:S(2)}) collective-permute-start(bf16[1024,512]{1,0:T(8,128)(2,1)S(1)} %grads.1.refs_0_), channel_id=1, source_target_pairs={{0,4},{1,5},{2,6},{3,7},{4,8},{5,9},{6,10},{7,11},{8,12},{9,13},{1... | collective-permute-start | bytes 3145736 | tf_op jit(solution)/shard_map/ppermute | solution.py:33
  38.4 17.7 %collective-permute-done.5.refs_3_.w0 = bf16[512,1024]{1,0:T(8,128)(2,1)} collective-permute-done((bf16[512,1024]{1,0:T(8,128)(2,1)S(1)}, bf16[512,1024]{1,0:T(8,128)(2,1)}, u32[]{:S(2)}, u32[]{:S(2)}) %collective-permute-start.5) | collective-permute-done | bytes 1048608 | tf_op jit(solution)/shard_map/ppermute | solution.py:33
  56.1 4.5 %collective-permute-done.4.refs_2_ = bf16[1024,512]{1,0:T(8,128)(2,1)S(1)} collective-permute-done((bf16[1024,512]{1,0:T(8,128)(2,1)S(1)}, bf16[1024,512]{1,0:T(8,128)(2,1)S(1)}, u32[]{:S(2)}, u32[]{:S(2)}) %collective-permute-start.4) | collective-permute-done | bytes 1048608 | tf_op jit(solution)/shard_map/ppermute | solution.py:33
  63.4 2.8 %collective-permute-start.7 = (bf16[512,512]{1,0:T(8,128)(2,1)}, bf16[512,512]{1,0:T(8,128)(2,1)}, u32[]{:S(2)}, u32[]{:S(2)}) collective-permute-start(bf16[512,512]{1,0:T(8,128)(2,1)} %slice.10), channel_id=1, source_target_pairs={{0,4},{1,5},{2,6},{3,7},{4,8},{5,9},{6,10},{7,11},{8,12},{9,13},{1... | collective-permute-start | bytes 1572872 | tf_op jit(solution)/shard_map/ppermute | solution.py:33
  68.2 3.4 %project.3.part = bf16[1024,512]{1,0:T(8,128)(2,1)S(1)} custom-call(s32[6]{0:T(128)S(1)} %stack.46.pos_ref, bf16[1024,512]{1,0:T(8,128)(2,1)S(1)} %copy-done.1, bf16[1024,512]{1,0:T(8,128)(2,1)S(1)} %collective-permute-done.3.refs_1_, bf16[1024,512]{1,0:T(8,128)(2,1)S(1)} %collective-permute-done.4.refs_2_, ...), custom_call_target="tpu_custom_call" | custom-call | flops 1610612736 | bytes 6291456 | tf_op jit(solution)/shard_map/project/pallas_call | solution.py:160
  71.6 6.8 %collective-permute-done.8.high = bf16[512,512]{1,0:T(8,128)(2,1)} collective-permute-done((bf16[512,512]{1,0:T(8,128)(2,1)}, bf16[512,512]{1,0:T(8,128)(2,1)}, u32[]{:S(2)}, u32[]{:S(2)}) %collective-permute-start.8) | collective-permute-done | bytes 524320 | tf_op jit(solution)/shard_map/ppermute | solution.py:33
  78.4 2.7 %finish.3 = (bf16[256,512]{1,0:T(8,128)(2,1)S(1)}, bf16[256,512]{1,0:T(8,128)(2,1)S(1)}, bf16[256,512]{1,0:T(8,128)(2,1)S(1)}, bf16[256,512]{1,0:T(8,128)(2,1)S(1)}) custom-call(s32[6]{0:T(128)S(1)} %stack.46.pos_ref, bf16[1024,512]{1,0:T(8,128)(2,1)S(1)} %project.3.part, bf16[512,512]{1,0:T(8,128)(2,1)} %collective-permute-done.7.low, ...), custom_call_target="tpu_custom_call" | custom-call | flops 536870912 | bytes 5242880 | tf_op jit(solution)/shard_map/finish/pallas_call | solution.py:186
  82.8 2.9 %collective-permute-start.14 = (bf16[256,512]{1,0:T(8,128)(2,1)S(1)}, bf16[256,512]{1,0:T(8,128)(2,1)S(1)}, u32[]{:S(2)}, u32[]{:S(2)}) collective-permute-start(bf16[256,512]{1,0:T(8,128)(2,1)S(1)} %get-tuple-element.37), channel_id=1, source_target_pairs={{0,32},{16,48},{32,0},{48,16},{64,96},{80,112},{96,64},{112,80},{1... | collective-permute-start | bytes 786440 | tf_op jit(solution)/shard_map/ppermute | solution.py:37
  87.0 3.1 %project.2.part = bf16[1024,512]{1,0:T(8,128)(2,1)S(1)} custom-call(s32[6]{0:T(128)S(1)} %stack.46.pos_ref, bf16[1024,512]{1,0:T(8,128)(2,1)S(1)} %copy-done.2, bf16[1024,512]{1,0:T(8,128)(2,1)S(1)} %collective-permute-done.3.refs_1_, bf16[1024,512]{1,0:T(8,128)(2,1)S(1)} %collective-permute-done.4.refs_2_, ...), custom_call_target="tpu_custom_call" | custom-call | flops 1610612736 | bytes 6291456 | tf_op jit(solution)/shard_map/project/pallas_call | solution.py:160
  90.1 2.4 %finish.2 = (bf16[256,512]{1,0:T(8,128)(2,1)S(1)}, bf16[256,512]{1,0:T(8,128)(2,1)S(1)}, bf16[256,512]{1,0:T(8,128)(2,1)S(1)}, bf16[256,512]{1,0:T(8,128)(2,1)S(1)}) custom-call(s32[6]{0:T(128)S(1)} %stack.46.pos_ref, bf16[1024,512]{1,0:T(8,128)(2,1)S(1)} %project.2.part, bf16[512,512]{1,0:T(8,128)(2,1)} %collective-permute-done.7.low, ...), custom_call_target="tpu_custom_call" | custom-call | flops 536870912 | bytes 5242880 | tf_op jit(solution)/shard_map/finish/pallas_call | solution.py:186
  94.1 2.0 %collective-permute-start.11 = (bf16[256,512]{1,0:T(8,128)(2,1)S(1)}, bf16[256,512]{1,0:T(8,128)(2,1)S(1)}, u32[]{:S(2)}, u32[]{:S(2)}) collective-permute-start(bf16[256,512]{1,0:T(8,128)(2,1)S(1)} %get-tuple-element.33), channel_id=1, source_target_pairs={{0,48},{16,0},{32,16},{48,32},{64,112},{80,64},{96,80},{112,96},{1... | collective-permute-start | bytes 786440 | tf_op jit(solution)/shard_map/ppermute | solution.py:37
  96.1 2.4 %collective-permute-done.14.c = bf16[256,512]{1,0:T(8,128)(2,1)S(1)} collective-permute-done((bf16[256,512]{1,0:T(8,128)(2,1)S(1)}, bf16[256,512]{1,0:T(8,128)(2,1)S(1)}, u32[]{:S(2)}, u32[]{:S(2)}) %collective-permute-start.14) | collective-permute-done | bytes 262176 | tf_op jit(solution)/shard_map/ppermute | solution.py:37
  99.6 4.5 %collective-permute-done.9.refs_1_ = bf16[256,512]{1,0:T(8,128)(2,1)S(1)} collective-permute-done((bf16[256,512]{1,0:T(8,128)(2,1)S(1)}, bf16[256,512]{1,0:T(8,128)(2,1)S(1)}, u32[]{:S(2)}, u32[]{:S(2)}) %collective-permute-start.9) | collective-permute-done | bytes 262176 | tf_op jit(solution)/shard_map/ppermute | solution.py:37
  104.1 3.7 %collective-permute-done.10.refs_2_ = bf16[256,512]{1,0:T(8,128)(2,1)S(1)} collective-permute-done((bf16[256,512]{1,0:T(8,128)(2,1)S(1)}, bf16[256,512]{1,0:T(8,128)(2,1)S(1)}, u32[]{:S(2)}, u32[]{:S(2)}) %collective-permute-start.10) | collective-permute-done | bytes 262176 | tf_op jit(solution)/shard_map/ppermute | solution.py:37
  108.7 3.4 %collective-permute-start.17 = (bf16[64,512]{1,0:T(8,128)(2,1)S(1)}, bf16[64,512]{1,0:T(8,128)(2,1)S(1)}, u32[]{:S(2)}, u32[]{:S(2)}) collective-permute-start(bf16[64,512]{1,0:T(8,128)(2,1)S(1)} %get-tuple-element.40), channel_id=1, source_target_pairs={{0,64},{16,80},{32,96},{48,112},{64,128},{80,144},{96,160},{112,17... | collective-permute-start | bytes 196616 | tf_op jit(solution)/shard_map/ppermute | solution.py:37
  112.1 4.5 %collective-permute-start.18 = (bf16[64,512]{1,0:T(8,128)(2,1)S(1)}, bf16[64,512]{1,0:T(8,128)(2,1)S(1)}, u32[]{:S(2)}, u32[]{:S(2)}) collective-permute-start(bf16[64,512]{1,0:T(8,128)(2,1)S(1)} %get-tuple-element.41), channel_id=1, source_target_pairs={{0,128},{16,144},{32,160},{48,176},{64,192},{80,208},{96,224},{112... | collective-permute-start | bytes 196616 | tf_op jit(solution)/shard_map/ppermute | solution.py:37
  116.6 2.7 %collective-permute-start.19 = (bf16[64,512]{1,0:T(8,128)(2,1)S(1)}, bf16[64,512]{1,0:T(8,128)(2,1)S(1)}, u32[]{:S(2)}, u32[]{:S(2)}) collective-permute-start(bf16[64,512]{1,0:T(8,128)(2,1)S(1)} %get-tuple-element.42), channel_id=1, source_target_pairs={{0,192},{16,208},{32,224},{48,240},{64,0},{80,16},{96,32},{112,48}... | collective-permute-start | bytes 196616 | tf_op jit(solution)/shard_map/ppermute | solution.py:37
  124.0 3.3 %collective-permute-start.23 = (bf16[64,512]{1,0:T(8,128)(2,1)S(1)}, bf16[64,512]{1,0:T(8,128)(2,1)S(1)}, u32[]{:S(2)}, u32[]{:S(2)}) collective-permute-start(bf16[64,512]{1,0:T(8,128)(2,1)S(1)} %constant_dynamic-update-slice_fusion), channel_id=1, source_target_pairs={{0,192},{16,208},{32,224},{48,240},{64,0},{80,16},{96,32},{112,48}... | collective-permute-start | bytes 196616 | tf_op jit(solution)/shard_map/ppermute | solution.py:37
  130.5 6.0 %collective-permute-done.22 = bf16[64,512]{1,0:T(8,128)(2,1)S(1)} collective-permute-done((bf16[64,512]{1,0:T(8,128)(2,1)S(1)}, bf16[64,512]{1,0:T(8,128)(2,1)S(1)}, u32[]{:S(2)}, u32[]{:S(2)}) %collective-permute-start.22) | collective-permute-done | bytes 65568 | tf_op jit(solution)/shard_map/ppermute | solution.py:37
  136.6 3.6 %collective-permute-start.26 = (bf16[4,64,512]{2,1,0:T(8,128)(2,1)S(1)}, bf16[4,64,512]{2,1,0:T(8,128)(2,1)S(1)}, u32[]{:S(2)}, u32[]{:S(2)}) collective-permute-start(bf16[4,64,512]{2,1,0:T(8,128)(2,1)S(1)} %pad_maximum_fusion.3.g0), channel_id=1, source_target_pairs={{0,48},{16,0},{32,16},{48,32},{64,112},{80,64},{96,80},{112,96},{1... | collective-permute-start | bytes 786440 | tf_op jit(solution)/shard_map/ppermute | solution.py:37
  141.9 8.9 %collective-permute-done.26.g3 = bf16[4,64,512]{2,1,0:T(8,128)(2,1)S(1)} collective-permute-done((bf16[4,64,512]{2,1,0:T(8,128)(2,1)S(1)}, bf16[4,64,512]{2,1,0:T(8,128)(2,1)S(1)}, u32[]{:S(2)}, u32[]{:S(2)}) %collective-permute-start.26) | collective-permute-done | bytes 262176 | tf_op jit(solution)/shard_map/ppermute | solution.py:37
  150.9 3.4 %collective-permute-done.24.g1 = bf16[4,64,512]{2,1,0:T(8,128)(2,1)S(1)} collective-permute-done((bf16[4,64,512]{2,1,0:T(8,128)(2,1)S(1)}, bf16[4,64,512]{2,1,0:T(8,128)(2,1)S(1)}, u32[]{:S(2)}, u32[]{:S(2)}) %collective-permute-start.24) | collective-permute-done | bytes 262176 | tf_op jit(solution)/shard_map/ppermute | solution.py:37
  (64 shorter events, 30.3 us)
Async XLA Ops:
  28.1 3.6 %collective-permute-start.1 = (f32[8,512]{1,0:T(8,128)S(1)}, f32[8,512]{1,0:T(8,128)S(1)}, u32[]{:S(2)}, u32[]{:S(2)}) collective-permute-start(f32[8,512]{1,0:T(8,128)S(1)} %stats.2.a0), channel_id=1, source_target_pairs={{0,1},{1,0},{2,3},{3,2},{4,5},{5,4},{6,7},{7,6},{8,9},{9,8},{10,11... | collective-permute-start | bytes 49160 | tf_op jit(solution)/shard_map/ppermute | solution.py:33
  30.5 25.7 %collective-permute-start.5 = (bf16[512,1024]{1,0:T(8,128)(2,1)S(1)}, bf16[512,1024]{1,0:T(8,128)(2,1)}, u32[]{:S(2)}, u32[]{:S(2)}) collective-permute-start(bf16[512,1024]{1,0:T(8,128)(2,1)S(1)} %pad_maximum_fusion.1), channel_id=1, source_target_pairs={{0,2},{1,3},{2,0},{3,1},{4,6},{5,7},{6,4},{7,5},{8,10},{9,11},{10,... | collective-permute-start | bytes 3145736 | tf_op jit(solution)/shard_map/ppermute | solution.py:33
  34.1 26.5 %collective-permute-start.4 = (bf16[1024,512]{1,0:T(8,128)(2,1)S(1)}, bf16[1024,512]{1,0:T(8,128)(2,1)S(1)}, u32[]{:S(2)}, u32[]{:S(2)}) collective-permute-start(bf16[1024,512]{1,0:T(8,128)(2,1)S(1)} %grads.1.refs_0_), channel_id=1, source_target_pairs={{0,12},{1,13},{2,14},{3,15},{4,0},{5,1},{6,2},{7,3},{8,4},{9,5},{1... | collective-permute-start | bytes 3145736 | tf_op jit(solution)/shard_map/ppermute | solution.py:33
  34.6 26.0 %collective-permute-start.3 = (bf16[1024,512]{1,0:T(8,128)(2,1)S(1)}, bf16[1024,512]{1,0:T(8,128)(2,1)S(1)}, u32[]{:S(2)}, u32[]{:S(2)}) collective-permute-start(bf16[1024,512]{1,0:T(8,128)(2,1)S(1)} %grads.1.refs_0_), channel_id=1, source_target_pairs={{0,4},{1,5},{2,6},{3,7},{4,8},{5,9},{6,10},{7,11},{8,12},{9,13},{1... | collective-permute-start | bytes 3145736 | tf_op jit(solution)/shard_map/ppermute | solution.py:33
  60.6 6.3 %collective-permute-start.12 = (bf16[512,1024]{1,0:T(8,128)(2,1)}, bf16[512,1024]{1,0:T(8,128)(2,1)}, u32[]{:S(2)}, u32[]{:S(2)}) collective-permute-start(bf16[512,1024]{1,0:T(8,128)(2,1)} %collective-permute-done.5.refs_3_.w0), channel_id=1, source_target_pairs={{0,1},{1,0},{2,3},{3,2},{4,5},{5,4},{6,7},{7,6},{8,9},{9,8},{10,11... | collective-permute-start | bytes 3145736 | tf_op jit(solution)/shard_map/ppermute | solution.py:33
  60.7 26.3 %collective-permute-start.6 = (bf16[512,1024]{1,0:T(8,128)(2,1)S(1)}, bf16[512,1024]{1,0:T(8,128)(2,1)}, u32[]{:S(2)}, u32[]{:S(2)}) collective-permute-start(bf16[512,1024]{1,0:T(8,128)(2,1)S(1)} %pad_maximum_fusion.2.refs_3_.w0), channel_id=1, source_target_pairs={{0,1},{1,0},{2,3},{3,2},{4,5},{5,4},{6,7},{7,6},{8,9},{9,8},{10,11... | collective-permute-start | bytes 3145736 | tf_op jit(solution)/shard_map/ppermute | solution.py:33
  63.0 15.4 %collective-permute-start.8 = (bf16[512,512]{1,0:T(8,128)(2,1)}, bf16[512,512]{1,0:T(8,128)(2,1)}, u32[]{:S(2)}, u32[]{:S(2)}) collective-permute-start(bf16[512,512]{1,0:T(8,128)(2,1)} %slice.11), channel_id=1, source_target_pairs={{0,12},{1,13},{2,14},{3,15},{4,0},{5,1},{6,2},{7,3},{8,4},{9,5},{1... | collective-permute-start | bytes 1572872 | tf_op jit(solution)/shard_map/ppermute | solution.py:33
  63.4 15.0 %collective-permute-start.7 = (bf16[512,512]{1,0:T(8,128)(2,1)}, bf16[512,512]{1,0:T(8,128)(2,1)}, u32[]{:S(2)}, u32[]{:S(2)}) collective-permute-start(bf16[512,512]{1,0:T(8,128)(2,1)} %slice.10), channel_id=1, source_target_pairs={{0,4},{1,5},{2,6},{3,7},{4,8},{5,9},{6,10},{7,11},{8,12},{9,13},{1... | collective-permute-start | bytes 1572872 | tf_op jit(solution)/shard_map/ppermute | solution.py:33
  81.1 12.9 %collective-permute-start.13 = (bf16[256,512]{1,0:T(8,128)(2,1)S(1)}, bf16[256,512]{1,0:T(8,128)(2,1)S(1)}, u32[]{:S(2)}, u32[]{:S(2)}) collective-permute-start(bf16[256,512]{1,0:T(8,128)(2,1)S(1)} %get-tuple-element.36), channel_id=1, source_target_pairs={{0,16},{16,32},{32,48},{48,0},{64,80},{80,96},{96,112},{112,64},{1... | collective-permute-start | bytes 786440 | tf_op jit(solution)/shard_map/ppermute | solution.py:37
  82.8 15.7 %collective-permute-start.14 = (bf16[256,512]{1,0:T(8,128)(2,1)S(1)}, bf16[256,512]{1,0:T(8,128)(2,1)S(1)}, u32[]{:S(2)}, u32[]{:S(2)}) collective-permute-start(bf16[256,512]{1,0:T(8,128)(2,1)S(1)} %get-tuple-element.37), channel_id=1, source_target_pairs={{0,32},{16,48},{32,0},{48,16},{64,96},{80,112},{96,64},{112,80},{1... | collective-permute-start | bytes 786440 | tf_op jit(solution)/shard_map/ppermute | solution.py:37
  85.6 12.8 %collective-permute-start.15 = (bf16[256,512]{1,0:T(8,128)(2,1)S(1)}, bf16[256,512]{1,0:T(8,128)(2,1)S(1)}, u32[]{:S(2)}, u32[]{:S(2)}) collective-permute-start(bf16[256,512]{1,0:T(8,128)(2,1)S(1)} %get-tuple-element.38), channel_id=1, source_target_pairs={{0,48},{16,0},{32,16},{48,32},{64,112},{80,64},{96,80},{112,96},{1... | collective-permute-start | bytes 786440 | tf_op jit(solution)/shard_map/ppermute | solution.py:37
  92.5 11.6 %collective-permute-start.9 = (bf16[256,512]{1,0:T(8,128)(2,1)S(1)}, bf16[256,512]{1,0:T(8,128)(2,1)S(1)}, u32[]{:S(2)}, u32[]{:S(2)}) collective-permute-start(bf16[256,512]{1,0:T(8,128)(2,1)S(1)} %get-tuple-element.31), channel_id=1, source_target_pairs={{0,16},{16,32},{32,48},{48,0},{64,80},{80,96},{96,112},{112,64},{1... | collective-permute-start | bytes 786440 | tf_op jit(solution)/shard_map/ppermute | solution.py:37
  93.3 14.6 %collective-permute-start.10 = (bf16[256,512]{1,0:T(8,128)(2,1)S(1)}, bf16[256,512]{1,0:T(8,128)(2,1)S(1)}, u32[]{:S(2)}, u32[]{:S(2)}) collective-permute-start(bf16[256,512]{1,0:T(8,128)(2,1)S(1)} %get-tuple-element.32), channel_id=1, source_target_pairs={{0,32},{16,48},{32,0},{48,16},{64,96},{80,112},{96,64},{112,80},{1... | collective-permute-start | bytes 786440 | tf_op jit(solution)/shard_map/ppermute | solution.py:37
  94.1 13.8 %collective-permute-start.11 = (bf16[256,512]{1,0:T(8,128)(2,1)S(1)}, bf16[256,512]{1,0:T(8,128)(2,1)S(1)}, u32[]{:S(2)}, u32[]{:S(2)}) collective-permute-start(bf16[256,512]{1,0:T(8,128)(2,1)S(1)} %get-tuple-element.33), channel_id=1, source_target_pairs={{0,48},{16,0},{32,16},{48,32},{64,112},{80,64},{96,80},{112,96},{1... | collective-permute-start | bytes 786440 | tf_op jit(solution)/shard_map/ppermute | solution.py:37
  98.6 9.2 %collective-permute-start.16 = (bf16[256,512]{1,0:T(8,128)(2,1)S(1)}, bf16[256,512]{1,0:T(8,128)(2,1)S(1)}, u32[]{:S(2)}, u32[]{:S(2)}) collective-permute-start(bf16[256,512]{1,0:T(8,128)(2,1)S(1)} %sum_y.1), channel_id=1, source_target_pairs={{0,2},{1,3},{2,0},{3,1},{4,6},{5,7},{6,4},{7,5},{8,10},{9,11},{10,... | collective-permute-start | bytes 786440 | tf_op jit(solution)/shard_map/ppermute | solution.py:33
  108.7 10.6 %collective-permute-start.17 = (bf16[64,512]{1,0:T(8,128)(2,1)S(1)}, bf16[64,512]{1,0:T(8,128)(2,1)S(1)}, u32[]{:S(2)}, u32[]{:S(2)}) collective-permute-start(bf16[64,512]{1,0:T(8,128)(2,1)S(1)} %get-tuple-element.40), channel_id=1, source_target_pairs={{0,64},{16,80},{32,96},{48,112},{64,128},{80,144},{96,160},{112,17... | collective-permute-start | bytes 196616 | tf_op jit(solution)/shard_map/ppermute | solution.py:37
  112.1 8.9 %collective-permute-start.18 = (bf16[64,512]{1,0:T(8,128)(2,1)S(1)}, bf16[64,512]{1,0:T(8,128)(2,1)S(1)}, u32[]{:S(2)}, u32[]{:S(2)}) collective-permute-start(bf16[64,512]{1,0:T(8,128)(2,1)S(1)} %get-tuple-element.41), channel_id=1, source_target_pairs={{0,128},{16,144},{32,160},{48,176},{64,192},{80,208},{96,224},{112... | collective-permute-start | bytes 196616 | tf_op jit(solution)/shard_map/ppermute | solution.py:37
  116.6 6.1 %collective-permute-start.19 = (bf16[64,512]{1,0:T(8,128)(2,1)S(1)}, bf16[64,512]{1,0:T(8,128)(2,1)S(1)}, u32[]{:S(2)}, u32[]{:S(2)}) collective-permute-start(bf16[64,512]{1,0:T(8,128)(2,1)S(1)} %get-tuple-element.42), channel_id=1, source_target_pairs={{0,192},{16,208},{32,224},{48,240},{64,0},{80,16},{96,32},{112,48}... | collective-permute-start | bytes 196616 | tf_op jit(solution)/shard_map/ppermute | solution.py:37
  124.0 6.6 %collective-permute-start.23 = (bf16[64,512]{1,0:T(8,128)(2,1)S(1)}, bf16[64,512]{1,0:T(8,128)(2,1)S(1)}, u32[]{:S(2)}, u32[]{:S(2)}) collective-permute-start(bf16[64,512]{1,0:T(8,128)(2,1)S(1)} %constant_dynamic-update-slice_fusion), channel_id=1, source_target_pairs={{0,192},{16,208},{32,224},{48,240},{64,0},{80,16},{96,32},{112,48}... | collective-permute-start | bytes 196616 | tf_op jit(solution)/shard_map/ppermute | solution.py:37
  127.3 9.2 %collective-permute-start.22 = (bf16[64,512]{1,0:T(8,128)(2,1)S(1)}, bf16[64,512]{1,0:T(8,128)(2,1)S(1)}, u32[]{:S(2)}, u32[]{:S(2)}) collective-permute-start(bf16[64,512]{1,0:T(8,128)(2,1)S(1)} %constant_dynamic-update-slice_fusion), channel_id=1, source_target_pairs={{0,128},{16,144},{32,160},{48,176},{64,192},{80,208},{96,224},{112... | collective-permute-start | bytes 196616 | tf_op jit(solution)/shard_map/ppermute | solution.py:37
  128.9 7.6 %collective-permute-start.21 = (bf16[64,512]{1,0:T(8,128)(2,1)S(1)}, bf16[64,512]{1,0:T(8,128)(2,1)S(1)}, u32[]{:S(2)}, u32[]{:S(2)}) collective-permute-start(bf16[64,512]{1,0:T(8,128)(2,1)S(1)} %constant_dynamic-update-slice_fusion), channel_id=1, source_target_pairs={{0,64},{16,80},{32,96},{48,112},{64,128},{80,144},{96,160},{112,17... | collective-permute-start | bytes 196616 | tf_op jit(solution)/shard_map/ppermute | solution.py:37
  136.6 14.3 %collective-permute-start.26 = (bf16[4,64,512]{2,1,0:T(8,128)(2,1)S(1)}, bf16[4,64,512]{2,1,0:T(8,128)(2,1)S(1)}, u32[]{:S(2)}, u32[]{:S(2)}) collective-permute-start(bf16[4,64,512]{2,1,0:T(8,128)(2,1)S(1)} %pad_maximum_fusion.3.g0), channel_id=1, source_target_pairs={{0,48},{16,0},{32,16},{48,32},{64,112},{80,64},{96,80},{112,96},{1... | collective-permute-start | bytes 786440 | tf_op jit(solution)/shard_map/ppermute | solution.py:37
  140.1 10.7 %collective-permute-start.25 = (bf16[4,64,512]{2,1,0:T(8,128)(2,1)S(1)}, bf16[4,64,512]{2,1,0:T(8,128)(2,1)S(1)}, u32[]{:S(2)}, u32[]{:S(2)}) collective-permute-start(bf16[4,64,512]{2,1,0:T(8,128)(2,1)S(1)} %pad_maximum_fusion.3.g0), channel_id=1, source_target_pairs={{0,32},{16,48},{32,0},{48,16},{64,96},{80,112},{96,64},{112,80},{1... | collective-permute-start | bytes 786440 | tf_op jit(solution)/shard_map/ppermute | solution.py:37
  141.9 12.3 %collective-permute-start.24 = (bf16[4,64,512]{2,1,0:T(8,128)(2,1)S(1)}, bf16[4,64,512]{2,1,0:T(8,128)(2,1)S(1)}, u32[]{:S(2)}, u32[]{:S(2)}) collective-permute-start(bf16[4,64,512]{2,1,0:T(8,128)(2,1)S(1)} %pad_maximum_fusion.3.g0), channel_id=1, source_target_pairs={{0,16},{16,32},{32,48},{48,0},{64,80},{80,96},{96,112},{112,64},{1... | collective-permute-start | bytes 786440 | tf_op jit(solution)/shard_map/ppermute | solution.py:37
  (8 other events, 26.9 us)

commit v6 on v5

--- a/solution.py
+++ b/solution.py
@@ -144,7 +144,7 @@
 
 
 def project_kernel(pos_ref, *refs):
-    blocks, weights, out = refs[:3], refs[3:5], refs[5]
+    blocks, weights, outs = refs[:3], refs[3:7], refs[7:]
     for half in range(2):
         for w, weight in enumerate(weights):
             acc = None
@@ -153,17 +153,17 @@
                     block = blocks[n][pl.ds(half * 512, 512), pl.ds(kind * HEAD, HEAD)]
                     term = dot(block, weight[pl.ds(kind * 256, 256), head_cols(pos_ref[0], d)], NT)
                     acc = term if acc is None else acc + term
-            out[pl.ds(half * 512, 512), pl.ds(w * 256, 256)] = acc.astype(out.dtype)
+            outs[w // 2][pl.ds(half * 512, 512), pl.ds((w % 2) * 256, 256)] = acc.astype(BF16)
 
 
 def project(pos, blocks, weights):
     return pl.pallas_call(
         project_kernel,
-        out_shape=jax.ShapeDtypeStruct((1024, 512), BF16),
-        in_specs=[pl.BlockSpec(memory_space=pltpu.SMEM)] + [pl.BlockSpec(memory_space=pltpu.VMEM)] * 5,
-        out_specs=pl.BlockSpec(memory_space=pltpu.VMEM),
-        compiler_params=pltpu.CompilerParams(vmem_limit_bytes=8 * 2**20),
-        cost_estimate=pl.CostEstimate(flops=1024 * 512 * 1536 * 2, bytes_accessed=6 * 2**20, transcendentals=0),
+        out_shape=(jax.ShapeDtypeStruct((1024, 512), BF16),) * 2,
+        in_specs=[pl.BlockSpec(memory_space=pltpu.SMEM)] + [pl.BlockSpec(memory_space=pltpu.VMEM)] * 7,
+        out_specs=(pl.BlockSpec(memory_space=pltpu.VMEM),) * 2,
+        compiler_params=pltpu.CompilerParams(vmem_limit_bytes=10 * 2**20),
+        cost_estimate=pl.CostEstimate(flops=1024 * 1024 * 1536 * 2, bytes_accessed=9 * 2**20, transcendentals=0),
         name="project",
     )(pos, *blocks, *weights)
 
@@ -307,11 +307,11 @@
 
     own = grads(parts, mine, other)
     right, left = along_seq(own, dx=1), along_seq(own, dx=3)
-    right, left, weight_z = tie((right, left, weight_z))
-    low_o, high_o = along_seq(right[:512], dx=1), along_seq(left[512:], dx=3)
+    low_r, high_l, weight_z = tie((right[:512], left[512:], weight_z))
+    low_o, high_o = along_seq(low_r, dx=1), along_seq(high_l, dx=3)
     weight_zc = along_seq(weight_z, dc=1)
     blocks = (own, right, left)
-    stay, leave = project(pos, blocks, (weight, weight_c)), project(pos, blocks, (weight_z, weight_zc))
+    stay, leave = project(pos, blocks, (weight, weight_c, weight_z, weight_zc))
 
     def to_y(pieces):
         return [pieces[0]] + [along_section(pieces[d], dy=d) for d in (1, 2, 3)]

time: 157 us -> 158 us (level)
  Pallas kernels: 19.5 us -> 16.7 us
  waiting for transfers between devices: 63.3 us -> 65.6 us
  local copies, waits for them, and re-layouts: 4.25 us -> 6.08 us
    ppermute x15, waiting for transfers between devices: 33.1 us -> 36.1 us  [along_section(): return lax.ppermute(value, 'section', section_moves(dh, dy))]
    unnamed x11 -> x17, local copies, waits for them, and re-layouts: 2.22 us -> 3.93 us
    pallas_call x2 -> x1, Pallas kernels: 6.46 us -> 5 us  [project(): pl.pallas_call(project_kernel, out_shape=(jax.ShapeDtypeStruct((1024, 512...]
  transfers between devices with their start and end apart: 27 -> 27, of which waited for: 14 -> 17; matrix products, arithmetic and copies ran while one was open for 1% -> 1% of each run, Pallas kernels for 11% -> 6%
where the time goes in v6:
time: 158 us; the launch traced here: 157 us
  waiting for transfers between devices  65.6 us (42%)
  starting transfers between devices  41 us (26%)
  blocking collectives  25 us (16%)
  Pallas kernels  16.7 us (11%)
  local copies, waits for them, and re-layouts  6.08 us (4%)
  other arithmetic  1.62 us (1%)
    ppermute x15, waiting for transfers between devices, along_section(): return lax.ppermute(value, 'section', section_moves(dh, dy))  36.1 us
    ppermute x15, starting transfers between devices, along_section(): return lax.ppermute(value, 'section', section_moves(dh, dy))  32.1 us
    ppermute x12, waiting for transfers between devices, along_seq(): return lax.ppermute(value, 'seq', seq_moves(dx, dz, dc))  29.5 us
    all_to_all x1, blocking collectives, local(): mine = lax.all_to_all(rows, 'seq', 0, 0, axis_index_groups=groups)  25 us
    ppermute x12, starting transfers between devices, along_seq(): return lax.ppermute(value, 'seq', seq_moves(dx, dz, dc))  8.92 us
    pallas_call x1, Pallas kernels, project(): pl.pallas_call(project_kernel, out_shape=(jax.ShapeDtypeStruct((1024, 512...  5 us
    unnamed x17, local copies, waits for them, and re-layouts  3.93 us
    pallas_call x2, Pallas kernels, finish(): pl.pallas_call(finish_kernel, out_shape=(jax.ShapeDtypeStruct((256, 512),...  3.84 us
  transfers between devices with their start and end apart: 27, of which 17 were waited for; matrix products, arithmetic and copies ran while one was open for 1% of the time, Pallas kernels for 6%

profile of v6, /device:TPU:6, one launch (start us, length us, event | category | flops | bytes accessed | tf_op | source)
XLA Modules:
  0.0 156.8 jit_solution(4693473014450818145)
XLA Ops:
  1.6 25.0 %all_to_all.5.m_ref.q_ref = bf16[8,384,256]{2,1,0:T(8,128)(2,1)S(1)} all-to-all(bf16[8,384,256]{2,1,0:T(8,128)(2,1)S(1)} %pack.1), channel_id=1, replica_groups={{0,2,4,6,8,10,12,14},{1,3,5,7,9,11,13,15},{16,18,20,22,24,26,28,30},{17..., dimensions={0} | all-to-all | bytes 3145728 | tf_op jit(solution)/shard_map/all_to_all | solution.py:294
  31.2 2.4 %grads.1.refs_0_ = bf16[1024,512]{1,0:T(8,128)(2,1)S(1)} custom-call(f32[8,512]{1,0:T(8,128)S(1)} %stats.2.a0, f32[8,512]{1,0:T(8,128)S(1)} %stats.3.b0, f32[8,512]{1,0:T(8,128)S(1)} %collective-permute-done.1.a1, f32[8,512]{1,0:T(8,128)S(1)} %collective-permute-done.2.b1, bf16[8,384,256]{2,1,0:T(8,128)(2,1)S(1)} %all_to_all.5.m_ref.q_ref, ...), custom_call_target="tpu_custom_call" | custom-call | flops 2000000000 | bytes 4194304 | tf_op jit(solution)/shard_map/grads/pallas_call | solution.py:130
  34.6 2.3 %collective-permute-start.3 = (bf16[1024,512]{1,0:T(8,128)(2,1)S(1)}, bf16[1024,512]{1,0:T(8,128)(2,1)S(1)}, u32[]{:S(2)}, u32[]{:S(2)}) collective-permute-start(bf16[1024,512]{1,0:T(8,128)(2,1)S(1)} %grads.1.refs_0_), channel_id=1, source_target_pairs={{0,4},{1,5},{2,6},{3,7},{4,8},{5,9},{6,10},{7,11},{8,12},{9,13},{1... | collective-permute-start | bytes 3145736 | tf_op jit(solution)/shard_map/ppermute | solution.py:33
  38.5 21.7 %collective-permute-done.4.refs_2_ = bf16[1024,512]{1,0:T(8,128)(2,1)S(1)} collective-permute-done((bf16[1024,512]{1,0:T(8,128)(2,1)S(1)}, bf16[1024,512]{1,0:T(8,128)(2,1)S(1)}, u32[]{:S(2)}, u32[]{:S(2)}) %collective-permute-start.4) | collective-permute-done | bytes 1048608 | tf_op jit(solution)/shard_map/ppermute | solution.py:33
  62.2 2.1 %collective-permute-start.8 = (bf16[512,512]{1,0:T(8,128)(2,1)}, bf16[512,512]{1,0:T(8,128)(2,1)S(1)}, u32[]{:S(2)}, u32[]{:S(2)}) collective-permute-start(bf16[512,512]{1,0:T(8,128)(2,1)} %slice.13), channel_id=1, source_target_pairs={{0,4},{1,5},{2,6},{3,7},{4,8},{5,9},{6,10},{7,11},{8,12},{9,13},{1... | collective-permute-start | bytes 1572872 | tf_op jit(solution)/shard_map/ppermute | solution.py:33
  68.7 5.0 %project.1 = (bf16[1024,512]{1,0:T(8,128)(2,1)S(1)}, bf16[1024,512]{1,0:T(8,128)(2,1)S(1)}) custom-call(s32[6]{0:T(128)S(1)} %stack.46.pos_ref, bf16[1024,512]{1,0:T(8,128)(2,1)S(1)} %copy-done.5, bf16[1024,512]{1,0:T(8,128)(2,1)S(1)} %copy-done.3, bf16[1024,512]{1,0:T(8,128)(2,1)S(1)} %copy-done.1, bf16[512,1024]{1,0:T(8,128)(2,1)S(1)} %pad_maximum_fusion.1.refs_3_.w0, ...), custom_call_target="tpu_custom_call" | custom-call | flops 3221225472 | bytes 9437184 | tf_op jit(solution)/shard_map/project/pallas_call | solution.py:160
  73.7 2.8 %collective-permute-done.8.low = bf16[512,512]{1,0:T(8,128)(2,1)S(1)} collective-permute-done((bf16[512,512]{1,0:T(8,128)(2,1)}, bf16[512,512]{1,0:T(8,128)(2,1)S(1)}, u32[]{:S(2)}, u32[]{:S(2)}) %collective-permute-start.8) | collective-permute-done | bytes 524320 | tf_op jit(solution)/shard_map/ppermute | solution.py:33
  76.5 3.0 %collective-permute-done.9.high = bf16[512,512]{1,0:T(8,128)(2,1)S(1)} collective-permute-done((bf16[512,512]{1,0:T(8,128)(2,1)}, bf16[512,512]{1,0:T(8,128)(2,1)S(1)}, u32[]{:S(2)}, u32[]{:S(2)}) %collective-permute-start.9) | collective-permute-done | bytes 524320 | tf_op jit(solution)/shard_map/ppermute | solution.py:33
  79.5 2.4 %finish.3 = (bf16[256,512]{1,0:T(8,128)(2,1)S(1)}, bf16[256,512]{1,0:T(8,128)(2,1)S(1)}, bf16[256,512]{1,0:T(8,128)(2,1)S(1)}, bf16[256,512]{1,0:T(8,128)(2,1)S(1)}) custom-call(s32[6]{0:T(128)S(1)} %stack.46.pos_ref, bf16[1024,512]{1,0:T(8,128)(2,1)S(1)} %get-tuple-element.38.part, bf16[512,512]{1,0:T(8,128)(2,1)S(1)} %collective-permute-done.8.low, ...), custom_call_target="tpu_custom_call" | custom-call | flops 536870912 | bytes 5242880 | tf_op jit(solution)/shard_map/finish/pallas_call | solution.py:186
  83.6 2.9 %collective-permute-start.14 = (bf16[256,512]{1,0:T(8,128)(2,1)S(1)}, bf16[256,512]{1,0:T(8,128)(2,1)S(1)}, u32[]{:S(2)}, u32[]{:S(2)}) collective-permute-start(bf16[256,512]{1,0:T(8,128)(2,1)S(1)} %get-tuple-element.41), channel_id=1, source_target_pairs={{0,32},{16,48},{32,0},{48,16},{64,96},{80,112},{96,64},{112,80},{1... | collective-permute-start | bytes 786440 | tf_op jit(solution)/shard_map/ppermute | solution.py:37
  91.4 2.9 %collective-permute-start.12 = (bf16[256,512]{1,0:T(8,128)(2,1)S(1)}, bf16[256,512]{1,0:T(8,128)(2,1)S(1)}, u32[]{:S(2)}, u32[]{:S(2)}) collective-permute-start(bf16[256,512]{1,0:T(8,128)(2,1)S(1)} %get-tuple-element.37), channel_id=1, source_target_pairs={{0,48},{16,0},{32,16},{48,32},{64,112},{80,64},{96,80},{112,96},{1... | collective-permute-start | bytes 786440 | tf_op jit(solution)/shard_map/ppermute | solution.py:37
  94.3 5.1 %collective-permute-done.14.c = bf16[256,512]{1,0:T(8,128)(2,1)S(1)} collective-permute-done((bf16[256,512]{1,0:T(8,128)(2,1)S(1)}, bf16[256,512]{1,0:T(8,128)(2,1)S(1)}, u32[]{:S(2)}, u32[]{:S(2)}) %collective-permute-start.14) | collective-permute-done | bytes 262176 | tf_op jit(solution)/shard_map/ppermute | solution.py:37
  100.8 1.9 %collective-permute-done.10.refs_1_ = bf16[256,512]{1,0:T(8,128)(2,1)S(1)} collective-permute-done((bf16[256,512]{1,0:T(8,128)(2,1)S(1)}, bf16[256,512]{1,0:T(8,128)(2,1)S(1)}, u32[]{:S(2)}, u32[]{:S(2)}) %collective-permute-start.10) | collective-permute-done | bytes 262176 | tf_op jit(solution)/shard_map/ppermute | solution.py:37
  102.6 6.1 %collective-permute-done.11.refs_2_ = bf16[256,512]{1,0:T(8,128)(2,1)S(1)} collective-permute-done((bf16[256,512]{1,0:T(8,128)(2,1)S(1)}, bf16[256,512]{1,0:T(8,128)(2,1)S(1)}, u32[]{:S(2)}, u32[]{:S(2)}) %collective-permute-start.11) | collective-permute-done | bytes 262176 | tf_op jit(solution)/shard_map/ppermute | solution.py:37
  109.6 3.3 %collective-permute-start.17 = (bf16[64,512]{1,0:T(8,128)(2,1)S(1)}, bf16[64,512]{1,0:T(8,128)(2,1)S(1)}, u32[]{:S(2)}, u32[]{:S(2)}) collective-permute-start(bf16[64,512]{1,0:T(8,128)(2,1)S(1)} %get-tuple-element.44), channel_id=1, source_target_pairs={{0,64},{16,80},{32,96},{48,112},{64,128},{80,144},{96,160},{112,17... | collective-permute-start | bytes 196616 | tf_op jit(solution)/shard_map/ppermute | solution.py:37
  112.9 4.5 %collective-permute-start.18 = (bf16[64,512]{1,0:T(8,128)(2,1)S(1)}, bf16[64,512]{1,0:T(8,128)(2,1)S(1)}, u32[]{:S(2)}, u32[]{:S(2)}) collective-permute-start(bf16[64,512]{1,0:T(8,128)(2,1)S(1)} %get-tuple-element.45), channel_id=1, source_target_pairs={{0,128},{16,144},{32,160},{48,176},{64,192},{80,208},{96,224},{112... | collective-permute-start | bytes 196616 | tf_op jit(solution)/shard_map/ppermute | solution.py:37
  117.4 2.7 %collective-permute-start.19 = (bf16[64,512]{1,0:T(8,128)(2,1)S(1)}, bf16[64,512]{1,0:T(8,128)(2,1)S(1)}, u32[]{:S(2)}, u32[]{:S(2)}) collective-permute-start(bf16[64,512]{1,0:T(8,128)(2,1)S(1)} %get-tuple-element.46), channel_id=1, source_target_pairs={{0,192},{16,208},{32,224},{48,240},{64,0},{80,16},{96,32},{112,48}... | collective-permute-start | bytes 196616 | tf_op jit(solution)/shard_map/ppermute | solution.py:37
  121.7 2.0 %collective-permute-done.19.d = bf16[64,512]{1,0:T(8,128)(2,1)S(1)} collective-permute-done((bf16[64,512]{1,0:T(8,128)(2,1)S(1)}, bf16[64,512]{1,0:T(8,128)(2,1)S(1)}, u32[]{:S(2)}, u32[]{:S(2)}) %collective-permute-start.19) | collective-permute-done | bytes 65568 | tf_op jit(solution)/shard_map/ppermute | solution.py:37
  125.0 2.8 %collective-permute-start.23 = (bf16[64,512]{1,0:T(8,128)(2,1)S(1)}, bf16[64,512]{1,0:T(8,128)(2,1)S(1)}, u32[]{:S(2)}, u32[]{:S(2)}) collective-permute-start(bf16[64,512]{1,0:T(8,128)(2,1)S(1)} %constant_dynamic-update-slice_fusion), channel_id=1, source_target_pairs={{0,192},{16,208},{32,224},{48,240},{64,0},{80,16},{96,32},{112,48}... | collective-permute-start | bytes 196616 | tf_op jit(solution)/shard_map/ppermute | solution.py:37
  131.2 5.8 %collective-permute-done.22 = bf16[64,512]{1,0:T(8,128)(2,1)S(1)} collective-permute-done((bf16[64,512]{1,0:T(8,128)(2,1)S(1)}, bf16[64,512]{1,0:T(8,128)(2,1)S(1)}, u32[]{:S(2)}, u32[]{:S(2)}) %collective-permute-start.22) | collective-permute-done | bytes 65568 | tf_op jit(solution)/shard_map/ppermute | solution.py:37
  137.3 4.0 %collective-permute-start.26 = (bf16[4,64,512]{2,1,0:T(8,128)(2,1)S(1)}, bf16[4,64,512]{2,1,0:T(8,128)(2,1)S(1)}, u32[]{:S(2)}, u32[]{:S(2)}) collective-permute-start(bf16[4,64,512]{2,1,0:T(8,128)(2,1)S(1)} %pad_maximum_fusion.3.g0), channel_id=1, source_target_pairs={{0,48},{16,0},{32,16},{48,32},{64,112},{80,64},{96,80},{112,96},{1... | collective-permute-start | bytes 786440 | tf_op jit(solution)/shard_map/ppermute | solution.py:37
  141.3 1.9 %collective-permute-start.25 = (bf16[4,64,512]{2,1,0:T(8,128)(2,1)S(1)}, bf16[4,64,512]{2,1,0:T(8,128)(2,1)S(1)}, u32[]{:S(2)}, u32[]{:S(2)}) collective-permute-start(bf16[4,64,512]{2,1,0:T(8,128)(2,1)S(1)} %pad_maximum_fusion.3.g0), channel_id=1, source_target_pairs={{0,32},{16,48},{32,0},{48,16},{64,96},{80,112},{96,64},{112,80},{1... | collective-permute-start | bytes 786440 | tf_op jit(solution)/shard_map/ppermute | solution.py:37
  143.2 8.2 %collective-permute-done.26.g3 = bf16[4,64,512]{2,1,0:T(8,128)(2,1)S(1)} collective-permute-done((bf16[4,64,512]{2,1,0:T(8,128)(2,1)S(1)}, bf16[4,64,512]{2,1,0:T(8,128)(2,1)S(1)}, u32[]{:S(2)}, u32[]{:S(2)}) %collective-permute-start.26) | collective-permute-done | bytes 262176 | tf_op jit(solution)/shard_map/ppermute | solution.py:37
  152.1 3.0 %collective-permute-done.24.g1 = bf16[4,64,512]{2,1,0:T(8,128)(2,1)S(1)} collective-permute-done((bf16[4,64,512]{2,1,0:T(8,128)(2,1)S(1)}, bf16[4,64,512]{2,1,0:T(8,128)(2,1)S(1)}, u32[]{:S(2)}, u32[]{:S(2)}) %collective-permute-start.24) | collective-permute-done | bytes 262176 | tf_op jit(solution)/shard_map/ppermute | solution.py:37
  (69 shorter events, 32.1 us)
Async XLA Ops:
  28.1 2.3 %collective-permute-start.1 = (f32[8,512]{1,0:T(8,128)S(1)}, f32[8,512]{1,0:T(8,128)S(1)}, u32[]{:S(2)}, u32[]{:S(2)}) collective-permute-start(f32[8,512]{1,0:T(8,128)S(1)} %stats.2.a0), channel_id=1, source_target_pairs={{0,1},{1,0},{2,3},{3,2},{4,5},{5,4},{6,7},{7,6},{8,9},{9,8},{10,11... | collective-permute-start | bytes 49160 | tf_op jit(solution)/shard_map/ppermute | solution.py:33
  33.6 26.5 %collective-permute-start.4 = (bf16[1024,512]{1,0:T(8,128)(2,1)S(1)}, bf16[1024,512]{1,0:T(8,128)(2,1)S(1)}, u32[]{:S(2)}, u32[]{:S(2)}) collective-permute-start(bf16[1024,512]{1,0:T(8,128)(2,1)S(1)} %grads.1.refs_0_), channel_id=1, source_target_pairs={{0,12},{1,13},{2,14},{3,15},{4,0},{5,1},{6,2},{7,3},{8,4},{9,5},{1... | collective-permute-start | bytes 3145736 | tf_op jit(solution)/shard_map/ppermute | solution.py:33
  34.6 26.4 %collective-permute-start.3 = (bf16[1024,512]{1,0:T(8,128)(2,1)S(1)}, bf16[1024,512]{1,0:T(8,128)(2,1)S(1)}, u32[]{:S(2)}, u32[]{:S(2)}) collective-permute-start(bf16[1024,512]{1,0:T(8,128)(2,1)S(1)} %grads.1.refs_0_), channel_id=1, source_target_pairs={{0,4},{1,5},{2,6},{3,7},{4,8},{5,9},{6,10},{7,11},{8,12},{9,13},{1... | collective-permute-start | bytes 3145736 | tf_op jit(solution)/shard_map/ppermute | solution.py:33
  37.0 24.9 %collective-permute-start.6 = (bf16[512,1024]{1,0:T(8,128)(2,1)S(1)}, bf16[512,1024]{1,0:T(8,128)(2,1)}, u32[]{:S(2)}, u32[]{:S(2)}) collective-permute-start(bf16[512,1024]{1,0:T(8,128)(2,1)S(1)} %pad_maximum_fusion.2), channel_id=1, source_target_pairs={{0,2},{1,3},{2,0},{3,1},{4,6},{5,7},{6,4},{7,5},{8,10},{9,11},{10,... | collective-permute-start | bytes 3145736 | tf_op jit(solution)/shard_map/ppermute | solution.py:33
  38.4 26.6 %collective-permute-start.5 = (bf16[512,1024]{1,0:T(8,128)(2,1)S(1)}, bf16[512,1024]{1,0:T(8,128)(2,1)S(1)}, u32[]{:S(2)}, u32[]{:S(2)}) collective-permute-start(bf16[512,1024]{1,0:T(8,128)(2,1)S(1)} %pad_maximum_fusion.1.refs_3_.w0), channel_id=1, source_target_pairs={{0,1},{1,0},{2,3},{3,2},{4,5},{5,4},{6,7},{7,6},{8,9},{9,8},{10,11... | collective-permute-start | bytes 3145736 | tf_op jit(solution)/shard_map/ppermute | solution.py:33
  62.0 3.0 %collective-permute-start.7 = (bf16[512,1024]{1,0:T(8,128)(2,1)}, bf16[512,1024]{1,0:T(8,128)(2,1)}, u32[]{:S(2)}, u32[]{:S(2)}) collective-permute-start(bf16[512,1024]{1,0:T(8,128)(2,1)} %collective-permute-done.6.refs_5_.w0), channel_id=1, source_target_pairs={{0,1},{1,0},{2,3},{3,2},{4,5},{5,4},{6,7},{7,6},{8,9},{9,8},{10,11... | collective-permute-start | bytes 3145736 | tf_op jit(solution)/shard_map/ppermute | solution.py:33
  62.2 14.3 %collective-permute-start.8 = (bf16[512,512]{1,0:T(8,128)(2,1)}, bf16[512,512]{1,0:T(8,128)(2,1)S(1)}, u32[]{:S(2)}, u32[]{:S(2)}) collective-permute-start(bf16[512,512]{1,0:T(8,128)(2,1)} %slice.13), channel_id=1, source_target_pairs={{0,4},{1,5},{2,6},{3,7},{4,8},{5,9},{6,10},{7,11},{8,12},{9,13},{1... | collective-permute-start | bytes 1572872 | tf_op jit(solution)/shard_map/ppermute | solution.py:33
  64.3 15.2 %collective-permute-start.9 = (bf16[512,512]{1,0:T(8,128)(2,1)}, bf16[512,512]{1,0:T(8,128)(2,1)S(1)}, u32[]{:S(2)}, u32[]{:S(2)}) collective-permute-start(bf16[512,512]{1,0:T(8,128)(2,1)} %slice.14), channel_id=1, source_target_pairs={{0,12},{1,13},{2,14},{3,15},{4,0},{5,1},{6,2},{7,3},{8,4},{9,5},{1... | collective-permute-start | bytes 1572872 | tf_op jit(solution)/shard_map/ppermute | solution.py:33
  81.9 9.4 %collective-permute-start.13 = (bf16[256,512]{1,0:T(8,128)(2,1)S(1)}, bf16[256,512]{1,0:T(8,128)(2,1)S(1)}, u32[]{:S(2)}, u32[]{:S(2)}) collective-permute-start(bf16[256,512]{1,0:T(8,128)(2,1)S(1)} %get-tuple-element.40), channel_id=1, source_target_pairs={{0,16},{16,32},{32,48},{48,0},{64,80},{80,96},{96,112},{112,64},{1... | collective-permute-start | bytes 786440 | tf_op jit(solution)/shard_map/ppermute | solution.py:37
  83.6 15.8 %collective-permute-start.14 = (bf16[256,512]{1,0:T(8,128)(2,1)S(1)}, bf16[256,512]{1,0:T(8,128)(2,1)S(1)}, u32[]{:S(2)}, u32[]{:S(2)}) collective-permute-start(bf16[256,512]{1,0:T(8,128)(2,1)S(1)} %get-tuple-element.41), channel_id=1, source_target_pairs={{0,32},{16,48},{32,0},{48,16},{64,96},{80,112},{96,64},{112,80},{1... | collective-permute-start | bytes 786440 | tf_op jit(solution)/shard_map/ppermute | solution.py:37
  86.5 12.9 %collective-permute-start.15 = (bf16[256,512]{1,0:T(8,128)(2,1)S(1)}, bf16[256,512]{1,0:T(8,128)(2,1)S(1)}, u32[]{:S(2)}, u32[]{:S(2)}) collective-permute-start(bf16[256,512]{1,0:T(8,128)(2,1)S(1)} %get-tuple-element.42), channel_id=1, source_target_pairs={{0,48},{16,0},{32,16},{48,32},{64,112},{80,64},{96,80},{112,96},{1... | collective-permute-start | bytes 786440 | tf_op jit(solution)/shard_map/ppermute | solution.py:37
  89.3 13.4 %collective-permute-start.10 = (bf16[256,512]{1,0:T(8,128)(2,1)S(1)}, bf16[256,512]{1,0:T(8,128)(2,1)S(1)}, u32[]{:S(2)}, u32[]{:S(2)}) collective-permute-start(bf16[256,512]{1,0:T(8,128)(2,1)S(1)} %get-tuple-element.35), channel_id=1, source_target_pairs={{0,16},{16,32},{32,48},{48,0},{64,80},{80,96},{96,112},{112,64},{1... | collective-permute-start | bytes 786440 | tf_op jit(solution)/shard_map/ppermute | solution.py:37
  90.0 18.7 %collective-permute-start.11 = (bf16[256,512]{1,0:T(8,128)(2,1)S(1)}, bf16[256,512]{1,0:T(8,128)(2,1)S(1)}, u32[]{:S(2)}, u32[]{:S(2)}) collective-permute-start(bf16[256,512]{1,0:T(8,128)(2,1)S(1)} %get-tuple-element.36), channel_id=1, source_target_pairs={{0,32},{16,48},{32,0},{48,16},{64,96},{80,112},{96,64},{112,80},{1... | collective-permute-start | bytes 786440 | tf_op jit(solution)/shard_map/ppermute | solution.py:37
  91.4 17.4 %collective-permute-start.12 = (bf16[256,512]{1,0:T(8,128)(2,1)S(1)}, bf16[256,512]{1,0:T(8,128)(2,1)S(1)}, u32[]{:S(2)}, u32[]{:S(2)}) collective-permute-start(bf16[256,512]{1,0:T(8,128)(2,1)S(1)} %get-tuple-element.37), channel_id=1, source_target_pairs={{0,48},{16,0},{32,16},{48,32},{64,112},{80,64},{96,80},{112,96},{1... | collective-permute-start | bytes 786440 | tf_op jit(solution)/shard_map/ppermute | solution.py:37
  99.5 9.2 %collective-permute-start.16 = (bf16[256,512]{1,0:T(8,128)(2,1)S(1)}, bf16[256,512]{1,0:T(8,128)(2,1)S(1)}, u32[]{:S(2)}, u32[]{:S(2)}) collective-permute-start(bf16[256,512]{1,0:T(8,128)(2,1)S(1)} %sum_y.1), channel_id=1, source_target_pairs={{0,2},{1,3},{2,0},{3,1},{4,6},{5,7},{6,4},{7,5},{8,10},{9,11},{10,... | collective-permute-start | bytes 786440 | tf_op jit(solution)/shard_map/ppermute | solution.py:33
  109.6 10.5 %collective-permute-start.17 = (bf16[64,512]{1,0:T(8,128)(2,1)S(1)}, bf16[64,512]{1,0:T(8,128)(2,1)S(1)}, u32[]{:S(2)}, u32[]{:S(2)}) collective-permute-start(bf16[64,512]{1,0:T(8,128)(2,1)S(1)} %get-tuple-element.44), channel_id=1, source_target_pairs={{0,64},{16,80},{32,96},{48,112},{64,128},{80,144},{96,160},{112,17... | collective-permute-start | bytes 196616 | tf_op jit(solution)/shard_map/ppermute | solution.py:37
  112.9 8.7 %collective-permute-start.18 = (bf16[64,512]{1,0:T(8,128)(2,1)S(1)}, bf16[64,512]{1,0:T(8,128)(2,1)S(1)}, u32[]{:S(2)}, u32[]{:S(2)}) collective-permute-start(bf16[64,512]{1,0:T(8,128)(2,1)S(1)} %get-tuple-element.45), channel_id=1, source_target_pairs={{0,128},{16,144},{32,160},{48,176},{64,192},{80,208},{96,224},{112... | collective-permute-start | bytes 196616 | tf_op jit(solution)/shard_map/ppermute | solution.py:37
  117.4 6.3 %collective-permute-start.19 = (bf16[64,512]{1,0:T(8,128)(2,1)S(1)}, bf16[64,512]{1,0:T(8,128)(2,1)S(1)}, u32[]{:S(2)}, u32[]{:S(2)}) collective-permute-start(bf16[64,512]{1,0:T(8,128)(2,1)S(1)} %get-tuple-element.46), channel_id=1, source_target_pairs={{0,192},{16,208},{32,224},{48,240},{64,0},{80,16},{96,32},{112,48}... | collective-permute-start | bytes 196616 | tf_op jit(solution)/shard_map/ppermute | solution.py:37
  125.0 6.1 %collective-permute-start.23 = (bf16[64,512]{1,0:T(8,128)(2,1)S(1)}, bf16[64,512]{1,0:T(8,128)(2,1)S(1)}, u32[]{:S(2)}, u32[]{:S(2)}) collective-permute-start(bf16[64,512]{1,0:T(8,128)(2,1)S(1)} %constant_dynamic-update-slice_fusion), channel_id=1, source_target_pairs={{0,192},{16,208},{32,224},{48,240},{64,0},{80,16},{96,32},{112,48}... | collective-permute-start | bytes 196616 | tf_op jit(solution)/shard_map/ppermute | solution.py:37
  127.8 9.2 %collective-permute-start.22 = (bf16[64,512]{1,0:T(8,128)(2,1)S(1)}, bf16[64,512]{1,0:T(8,128)(2,1)S(1)}, u32[]{:S(2)}, u32[]{:S(2)}) collective-permute-start(bf16[64,512]{1,0:T(8,128)(2,1)S(1)} %constant_dynamic-update-slice_fusion), channel_id=1, source_target_pairs={{0,128},{16,144},{32,160},{48,176},{64,192},{80,208},{96,224},{112... | collective-permute-start | bytes 196616 | tf_op jit(solution)/shard_map/ppermute | solution.py:37
  129.6 7.6 %collective-permute-start.21 = (bf16[64,512]{1,0:T(8,128)(2,1)S(1)}, bf16[64,512]{1,0:T(8,128)(2,1)S(1)}, u32[]{:S(2)}, u32[]{:S(2)}) collective-permute-start(bf16[64,512]{1,0:T(8,128)(2,1)S(1)} %constant_dynamic-update-slice_fusion), channel_id=1, source_target_pairs={{0,64},{16,80},{32,96},{48,112},{64,128},{80,144},{96,160},{112,17... | collective-permute-start | bytes 196616 | tf_op jit(solution)/shard_map/ppermute | solution.py:37
  137.3 14.2 %collective-permute-start.26 = (bf16[4,64,512]{2,1,0:T(8,128)(2,1)S(1)}, bf16[4,64,512]{2,1,0:T(8,128)(2,1)S(1)}, u32[]{:S(2)}, u32[]{:S(2)}) collective-permute-start(bf16[4,64,512]{2,1,0:T(8,128)(2,1)S(1)} %pad_maximum_fusion.3.g0), channel_id=1, source_target_pairs={{0,48},{16,0},{32,16},{48,32},{64,112},{80,64},{96,80},{112,96},{1... | collective-permute-start | bytes 786440 | tf_op jit(solution)/shard_map/ppermute | solution.py:37
  141.3 10.8 %collective-permute-start.25 = (bf16[4,64,512]{2,1,0:T(8,128)(2,1)S(1)}, bf16[4,64,512]{2,1,0:T(8,128)(2,1)S(1)}, u32[]{:S(2)}, u32[]{:S(2)}) collective-permute-start(bf16[4,64,512]{2,1,0:T(8,128)(2,1)S(1)} %pad_maximum_fusion.3.g0), channel_id=1, source_target_pairs={{0,32},{16,48},{32,0},{48,16},{64,96},{80,112},{96,64},{112,80},{1... | collective-permute-start | bytes 786440 | tf_op jit(solution)/shard_map/ppermute | solution.py:37
  143.2 11.9 %collective-permute-start.24 = (bf16[4,64,512]{2,1,0:T(8,128)(2,1)S(1)}, bf16[4,64,512]{2,1,0:T(8,128)(2,1)S(1)}, u32[]{:S(2)}, u32[]{:S(2)}) collective-permute-start(bf16[4,64,512]{2,1,0:T(8,128)(2,1)S(1)} %pad_maximum_fusion.3.g0), channel_id=1, source_target_pairs={{0,16},{16,32},{32,48},{48,0},{64,80},{80,96},{96,112},{112,64},{1... | collective-permute-start | bytes 786440 | tf_op jit(solution)/shard_map/ppermute | solution.py:37
  (11 other events, 20.1 us)
